TPU v7x, 32 devices: a whole 2x2x4 slice. The times are simulated.
32 devices in a mesh: grp: 1, blk: 32 (over z, y, x, core).
Axes of the slice: x: 2, y: 2, z: 4, core: 2. Of those that a mesh axis runs over, the one named last changes fastest.
Arguments:
- sigma_anc: float32 [16384, 16384], P('grp', 'blk')
- panels: float32 [16384, 1024], P(('grp', 'blk')), may hold values from -0.0625 to 0.0625
- diag_inv: float32 [1024, 256], replicated, may hold values from -6 to 6
- scaled_parent_panel: float32 [512, 256], replicated, may hold values from -0.375 to 0.375
- struct_upper: int32 [2, 32], replicated, may hold values from 0 to 63, as said below
- struct_lower: int32 [2, 16], replicated, may hold values from 0 to 63, as said below
Outputs:
- cov_panel: float32 [16384, 1024], P(('blk', 'grp'))
- cov_diag: float32 [1024, 256], P('blk')
- cov_parent: float32 [512, 256], P('blk')
Inputs may be any that keep to these rules, and one draw needn't show every extreme that they name: `struct_upper`: each row lists 32 different ancestor blocks. `struct_lower`: each row lists 16 different blocks, all in its parent's row of struct_upper.
All inputs are finite; a program needn't handle non-finite values.
Results may differ from a plain program's by a relative error of at most 0.00011.
Values sent between devices are 32-bit elements; how exact they have to be, the bound alone decides.
No kernel may reach another device: no remote copies, remote signals or barrier semaphores. Data moves between devices by JAX's collectives and lax.ppermute only.
A program may use at most 192 MiB of HBM per device.

v0:
```python
import jax
import jax.numpy as jnp
from jax import lax
from jax.sharding import PartitionSpec as P

NODE_WIDTH = 256
UPPER_NODES_1 = 2
LOWER_NODES_2 = 2


HIGH_ACCURACY = lax.Precision.HIGHEST


def block_table(struct_upper, struct_lower, blocks):
    ids = jnp.arange(blocks, dtype=jnp.int32)
    upper = jnp.any(struct_upper[:, :, None] == ids[None, None, :], axis=1)
    lower = jnp.any(struct_lower[:, :, None] == ids[None, None, :], axis=1)
    return jnp.concatenate([upper, lower], axis=0).astype(jnp.float32)


def row_mask(table, first_row, count):
    blocks = table.shape[1]
    rows = first_row + jnp.arange(count, dtype=jnp.int32)
    membership_grid = (
        (rows // NODE_WIDTH)[:, None] == jnp.arange(blocks, dtype=jnp.int32)[None, :]
    ).astype(jnp.float32)
    return jnp.dot(
        membership_grid, table.T, precision=HIGH_ACCURACY, preferred_element_type=jnp.float32
    )


def strip_summands(reciprocal_lines, array_lines, membership_grid, stacked_arrays):
    count = reciprocal_lines.shape[0]
    upper_width_1 = UPPER_NODES_1 * NODE_WIDTH
    matrix_columns = jnp.repeat(array_lines, NODE_WIDTH, axis=1)
    g_up = -(matrix_columns[:, :upper_width_1] * reciprocal_lines[:, :upper_width_1])
    collected_elder_share = jnp.einsum(
        "rjw,cj->rcw",
        g_up.reshape(count, UPPER_NODES_1, NODE_WIDTH),
        membership_grid,
        precision=HIGH_ACCURACY,
    )
    resolved_bottom_share = matrix_columns[:, upper_width_1:].reshape(
        count, LOWER_NODES_2, NODE_WIDTH
    ) * (
        jnp.einsum("odf,dfy->ody", collected_elder_share, stacked_arrays, precision=HIGH_ACCURACY)
        + reciprocal_lines[:, upper_width_1:].reshape(count, LOWER_NODES_2, NODE_WIDTH)
    )
    strip_result = jnp.concatenate(
        [g_up, -resolved_bottom_share.reshape(count, LOWER_NODES_2 * NODE_WIDTH)], axis=1
    )
    return (strip_result, collected_elder_share, resolved_bottom_share)


def block_sums(urows, reciprocal_lines, collected_elder_share, resolved_bottom_share):
    count = urows.shape[0]
    upper_width_1 = UPPER_NODES_1 * NODE_WIDTH
    u_up = urows[:, :upper_width_1].reshape(count, UPPER_NODES_1, NODE_WIDTH)
    u_low = urows[:, upper_width_1:].reshape(count, LOWER_NODES_2, NODE_WIDTH)
    amat = jnp.einsum(
        "rjw,rjv->jwv",
        u_up,
        reciprocal_lines[:, :upper_width_1].reshape(count, UPPER_NODES_1, NODE_WIDTH),
        precision=HIGH_ACCURACY,
    )
    block_matrix = jnp.einsum("rcw,rcv->cwv", u_low, collected_elder_share, precision=HIGH_ACCURACY)
    extra_matrix = jnp.einsum("rcw,rcv->cwv", u_low, resolved_bottom_share, precision=HIGH_ACCURACY)
    return jnp.concatenate([amat, block_matrix, extra_matrix], axis=0)


def per_device(sigma_anc, panels, diag_inv, scaled_parent_panel, struct_upper, struct_lower):
    rows_grp, cols_dev = sigma_anc.shape
    rows_dev = panels.shape[0]
    grp_count = lax.axis_size("grp")
    blk_count = lax.axis_size("blk")
    grp_pos = lax.axis_index("grp")
    blk_pos = lax.axis_index("blk")
    blocks = cols_dev * blk_count // NODE_WIDTH
    table = block_table(struct_upper, struct_lower, blocks)
    parent_ids = jnp.arange(LOWER_NODES_2, dtype=jnp.int32) % UPPER_NODES_1
    membership_grid = (
        parent_ids[:, None] == jnp.arange(UPPER_NODES_1, dtype=jnp.int32)[None, :]
    ).astype(jnp.float32)
    stacked_arrays = scaled_parent_panel.reshape(LOWER_NODES_2, NODE_WIDTH, NODE_WIDTH)
    first_in = grp_pos * rows_grp + blk_pos * rows_dev
    upanel = panels * jnp.repeat(row_mask(table, first_in, rows_dev), NODE_WIDTH, axis=1)
    grouped = lax.all_gather(upanel, "blk", axis=0, tiled=True)
    partial_value = lax.dot_general(
        sigma_anc,
        grouped,
        (((0,), (0,)), ((), ())),
        precision=HIGH_ACCURACY,
        preferred_element_type=jnp.float32,
    )
    share = cols_dev // grp_count
    col_first = blk_pos * cols_dev
    root = col_first // rows_grp
    offset = jnp.clip(col_first - grp_pos * rows_grp, 0, rows_grp - cols_dev)
    own_first = col_first + grp_pos * share
    owned_mask = row_mask(table, own_first, share)
    nterms = UPPER_NODES_1 + 2 * LOWER_NODES_2
    inverse_columns = lax.psum(partial_value, "grp")
    inverse_owned = lax.dynamic_slice_in_dim(inverse_columns, grp_pos * share, share, 0)
    strip_result, collected_elder_share, resolved_bottom_share = strip_summands(
        inverse_owned, owned_mask, membership_grid, stacked_arrays
    )

    def on_root():
        u_cols = lax.dynamic_slice_in_dim(grouped, offset, cols_dev, 0)
        complete_mask = row_mask(table, col_first, cols_dev)
        discarded_result, collected_entire_factor, resolved_entire_factor = strip_summands(
            inverse_columns, complete_mask, membership_grid, stacked_arrays
        )
        return block_sums(u_cols, inverse_columns, collected_entire_factor, resolved_entire_factor)

    def off_root():
        return jnp.zeros((nterms, NODE_WIDTH, NODE_WIDTH), jnp.float32)

    terms = lax.cond(grp_pos == root, on_root, off_root)
    summed = lax.psum(terms, ("grp", "blk"))
    amat = summed[:UPPER_NODES_1]
    block_matrix = summed[UPPER_NODES_1 : UPPER_NODES_1 + LOWER_NODES_2]
    extra_matrix = summed[UPPER_NODES_1 + LOWER_NODES_2 :]
    diagonal_matrices = diag_inv.reshape(UPPER_NODES_1 + LOWER_NODES_2, NODE_WIDTH, NODE_WIDTH)
    s_up = diagonal_matrices[:UPPER_NODES_1] + amat
    parent_selection = jnp.einsum("cj,jwv->cwv", membership_grid, s_up, precision=HIGH_ACCURACY)
    solved_parent = jnp.einsum(
        "ghz,gzs->ghs", parent_selection, stacked_arrays, precision=HIGH_ACCURACY
    ) + jnp.transpose(block_matrix, (0, 2, 1))
    lower_selection = (
        diagonal_matrices[UPPER_NODES_1:]
        + jnp.einsum("lmt,lmx->ltx", stacked_arrays, solved_parent, precision=HIGH_ACCURACY)
        + extra_matrix
    )
    whole_diag = jnp.concatenate([s_up, lower_selection], axis=0).reshape(
        (UPPER_NODES_1 + LOWER_NODES_2) * NODE_WIDTH, NODE_WIDTH
    )
    whole_parent = -solved_parent.reshape(LOWER_NODES_2 * NODE_WIDTH, NODE_WIDTH)
    diag_rows = (UPPER_NODES_1 + LOWER_NODES_2) * NODE_WIDTH // blk_count
    parent_rows = LOWER_NODES_2 * NODE_WIDTH // blk_count
    cov_diag = lax.dynamic_slice_in_dim(whole_diag, blk_pos * diag_rows, diag_rows, 0)
    cov_parent = lax.dynamic_slice_in_dim(whole_parent, blk_pos * parent_rows, parent_rows, 0)
    return (strip_result, cov_diag, cov_parent)


def solution(mesh):
    return jax.shard_map(
        per_device,
        mesh=mesh,
        in_specs=(P("grp", "blk"), P(("grp", "blk"), None), P(), P(), P(), P()),
        out_specs=(P(("blk", "grp"), None), P("blk", None), P("blk", None)),
        check_vma=False,
    )
```

profile of v0, /device:TPU:0, one launch (start us, length us, event | category | flops | bytes accessed | tf_op | source)
XLA Modules:
  0.0 671.7 jit_solution(18074302837849964957)
XLA Ops:
  8.8 1.9 copy.57
  11.0 1.6 bitcast_multiply_fusion
  15.2 366.8 %all-gather.2.cloned.1.call-done = f32[16384,1024]{0,1:T(8,128)} async-done(((f32[512,1024]{0,1:T(8,128)}), f32[16384,1024]{0,1:T(8,128)}) %all-gather.2.cloned.1.call-update) | async-done | bytes 67108880 | tf_op jit(solution)/shard_map/all_gather | solution.py:87
  381.9 115.2 %convolution_bitcast_fusion.2 = f32[512,1024]{0,1:T(8,128)} fusion(f32[16384,1024]{0,1:T(8,128)} %all-gather.2.cloned.1.call-done, f32[16384,512]{1,0:T(8,128)} %param.8), kind=kOutput, calls=%fused_computation.25 | convolution fusion | flops 103079215104 | bytes 102760448 | tf_op jit(solution)/shard_map/dot_general | solution.py:88
  497.1 25.4 %conditional.1 = (f32[6,256,256]{2,1,0:T(8,128)S(1)}) conditional(s32[]{:T(128)} %convert_element_type.12, () %tuple.19, (s32[]{:T(128)}, f32[16384,1024]{0,1:T(8,128)}, f32[512,1024]{0,1:T(8,128)}, f32[4,64]{1,0:T(4,128)S(1)}, f32[2,2]{1,0:T(2,128)S(1)}, /*index=5*/f32[2,256,256]{2,1,0:T(8,128)S(1)}) %tuple.45), branch_computations={%region_2.3_spmd, %region_3.4_spmd} | conditional | flops 3230965760 | bytes 47207552 | solution.py:119
  497.4 1.6 broadcast_in_dim.1
  499.0 5.6 constant_dynamic-slice_fusion
  504.7 1.3 copy.52
  505.9 4.9 convolution_bitcast_fusion
  510.9 2.5 copy.55
  513.4 2.6 copy.56
  516.0 2.6 fusion.1
  520.9 1.1 fusion.37
  522.5 1.6 copy.61
  524.3 3.4 fusion.17
  528.3 2.2 convolution_bitcast_fusion.3
  530.5 1.2 fusion.14
  531.7 1.5 pad_maximum_fusion.1
  533.2 3.0 copy.69
  536.2 119.1 %all-reduce.2.cloned.1.call-done = f32[6,256,256]{1,2,0:T(8,128)} async-done(((f32[6,256,256]{1,2,0:T(8,128)}), f32[6,256,256]{1,2,0:T(8,128)}) %all-reduce.2.cloned.1.call-update) | async-done | bytes 1572880 | tf_op jit(solution)/shard_map/psum | solution.py:120
  656.7 1.2 fusion.27
  657.9 2.5 fusion.36
  660.4 2.1 fusion.16
  663.5 1.3 constant_dynamic-slice_fusion.1
  (40 shorter events, 10.4 us)
Async XLA Ops:
  7.2 374.7 %all-gather.2.cloned.1.call-start = ((), (), s32[]{:S(2)}) async-start(), calls=%async_computation | async-start | bytes 69206016 | tf_op jit(solution)/shard_map/all_gather | solution.py:87
  12.5 1.2 copy-start.6
  12.6 642.8 %all-reduce.2.cloned.1.call-start = ((), (), s32[]{:S(2)}) async-start(), calls=%async_computation.1 | async-start | bytes 3145728 | tf_op jit(solution)/shard_map/psum | solution.py:120
  15.2 481.9 %copy-start = (f32[512,256]{1,0:T(8,128)S(1)}, f32[512,256]{1,0:T(8,128)}, u32[]{:S(2)}) copy-start(f32[512,256]{1,0:T(8,128)} %param.11) | copy-start | bytes 1572868
  518.6 2.3 copy-start.1
  518.6 2.3 copy-start.2
  528.3 2.2 copy-start.3
  528.3 2.2 copy-start.4
  533.2 122.1 %copy-start.5 = (f32[2,256,256]{1,2,0:T(8,128)S(1)}, f32[2,256,256]{1,2,0:T(8,128)}, u32[]{:S(2)}) copy-start(f32[2,256,256]{1,2,0:T(8,128)} %copy.62) | copy-start | bytes 1572868
Sparse Core Ops, SparseCore 0:
  12.7 369.1 all-gather.1
  524.2 131.0 all-reduce.1
where the time goes:
time: 672 us
  waiting for transfers between devices  486 us (72%)
  matrix products  136 us (20%)
  local copies, waits for them, and re-layouts  20.2 us (3%)
  other arithmetic  15.1 us (2%)
  between operations  14.2 us (2%)
    all_gather x1, waiting for transfers between devices, per_device(): grouped = lax.all_gather(upanel, 'blk', axis=0, tiled=True)  367 us
    psum x1, waiting for transfers between devices, per_device(): summed = lax.psum(terms, ('grp', 'blk'))  119 us
    dot_general x1, matrix products, per_device(): lax.dot_general(sigma_anc, grouped, (((0,), (0,)), ((), ())), precision=H...  115 us
  transfers between devices with their start and end apart: 2, of which 2 were waited for; matrix products, arithmetic and copies ran while one was open for 2% of the time, Pallas kernels for 0%

commit v1 on v0

--- a/solution.py
+++ b/solution.py
@@ -1,14 +1,406 @@
 import jax
 import jax.numpy as jnp
 from jax import lax
+from jax.experimental import pallas as pl
+from jax.experimental.pallas import tpu as pltpu
 from jax.sharding import PartitionSpec as P
 
 NODE_WIDTH = 256
 UPPER_NODES_1 = 2
 LOWER_NODES_2 = 2
+F32 = jnp.float32
+BF16 = jnp.bfloat16
 
 
 HIGH_ACCURACY = lax.Precision.HIGHEST
+
+
+CHIPS_Z, CHIPS_Y, CHIPS_X, CORES = 4, 2, 2, 2
+PIECES = CHIPS_Z * CHIPS_Y * CHIPS_X * CORES
+SUB = NODE_WIDTH // PIECES
+SLOTS = 32
+PER_STEP = 4
+W = NODE_WIDTH
+VMEM_BYTES = 60 * 1024 * 1024
+
+
+def params(**kw):
+    return pltpu.CompilerParams(vmem_limit_bytes=VMEM_BYTES, **kw)
+
+
+def split(x):
+    hi = x.astype(BF16)
+    return hi, (x - hi.astype(F32)).astype(BF16)
+
+
+def dot3(a, b):
+    a_hi, a_lo = split(a)
+    b_hi, b_lo = split(b)
+    small = jnp.dot(a_lo, b_hi, preferred_element_type=F32) + jnp.dot(
+        a_hi, b_lo, preferred_element_type=F32
+    )
+    return jnp.dot(a_hi, b_hi, preferred_element_type=F32) + small
+
+
+def cost(flops, nbytes):
+    return pl.CostEstimate(flops=flops, bytes_accessed=nbytes, transcendentals=0)
+
+
+def transpose_body(x_ref, o_ref):
+    for c in range(o_ref.shape[1]):
+        for rb in range(2):
+            t = x_ref[rb * W : (rb + 1) * W, c * W : (c + 1) * W].T
+            o_ref[:, c, rb] = t.reshape(PIECES, SUB, W)
+
+
+def transposed_pieces(panels, first, count):
+    shape = (PIECES, count, 2, SUB, W)
+    return pl.pallas_call(
+        transpose_body,
+        out_shape=jax.ShapeDtypeStruct(shape, F32),
+        grid=(1,),
+        in_specs=[pl.BlockSpec((2 * W, count * W), lambda i: (0, first // count))],
+        out_specs=pl.BlockSpec(shape, lambda i: (0, 0, 0, 0, 0)),
+        compiler_params=params(),
+        cost_estimate=cost(0, 4 * panels.size * count // 2),
+        name="transposed_pieces",
+    )(panels)
+
+
+def pick_body(idx_ref, a_ref, o_ref):
+    for k in range(o_ref.shape[1]):
+        o_ref[0, k] = a_ref[idx_ref[k]]
+
+
+def picked(idx, a):
+    return pl.pallas_call(
+        pick_body,
+        out_shape=jax.ShapeDtypeStruct((1, idx.shape[0], SUB, W), F32),
+        in_specs=[
+            pl.BlockSpec(memory_space=pltpu.SMEM),
+            pl.BlockSpec(memory_space=pltpu.VMEM),
+        ],
+        out_specs=pl.BlockSpec(memory_space=pltpu.VMEM),
+        compiler_params=params(),
+        cost_estimate=cost(0, 4 * (a.size + idx.size * SUB * W)),
+        name="picked",
+    )(idx, a)
+
+
+def product_body(accs, idx_ref, *refs):
+    sig, lines, o_ref = refs[:PER_STEP], refs[PER_STEP:-1], refs[-1]
+    step = pl.program_id(0)
+    per_acc = pl.num_programs(0) // accs
+    left = []
+    for q in range(PER_STEP):
+        left.append(jnp.concatenate([r[:, q].reshape(-1, W) for r in lines], axis=0))
+    value = dot3(jnp.concatenate(left, axis=1), jnp.concatenate([r[...] for r in sig], axis=0))
+
+    @pl.when(lax.rem(step, per_acc) == 0)
+    def _():
+        o_ref[0] = value
+
+    @pl.when(lax.rem(step, per_acc) != 0)
+    def _():
+        o_ref[0] += value
+
+
+def product(idx, sigma, pieces, accs, chunk=0):
+    steps = SLOTS // PER_STEP
+    cols = sigma.shape[1]
+    rows = SUB * sum(p.shape[0] for p in pieces)
+
+    def sig_spec(q):
+        return pl.BlockSpec((W, cols), lambda i, idx, q=q: (idx[i * PER_STEP + q], 0))
+
+    piece_specs = [
+        pl.BlockSpec((p.shape[0], PER_STEP, SUB, W), lambda i, idx: (0, i + chunk * steps, 0, 0))
+        for p in pieces
+    ]
+    return pl.pallas_call(
+        lambda *refs: product_body(accs, *refs),
+        out_shape=jax.ShapeDtypeStruct((accs, rows, cols), F32),
+        grid_spec=pltpu.PrefetchScalarGridSpec(
+            num_scalar_prefetch=1,
+            grid=(steps,),
+            in_specs=[sig_spec(q) for q in range(PER_STEP)] + piece_specs,
+            out_specs=pl.BlockSpec((1, rows, cols), lambda i, idx: (lax.div(i * accs, steps), 0, 0)),
+        ),
+        compiler_params=params(),
+        cost_estimate=cost(6 * SLOTS * rows * W * cols, 4 * SLOTS * W * (cols + rows)),
+        name="product",
+    )(idx, *([sigma] * PER_STEP), *pieces)
+
+
+def row_flags(rows, lo, hi):
+    top = lax.broadcasted_iota(jnp.int32, (rows, 1), 0) < W
+    return jnp.where(top, lo.astype(F32), hi.astype(F32))
+
+
+def local_lines(ref, c):
+    return jnp.concatenate([ref[:, c, rb].reshape(W, W) for rb in range(2)], axis=1)
+
+
+def in_order(pos_ref, zt_refs, c, scratch):
+    g = 0
+    for ref in zt_refs:
+        for row in range(0, ref.shape[1], SUB):
+            at = pl.multiple_of(pos_ref[g] * SUB, SUB)
+            scratch[pl.ds(at, SUB), :] = ref[c, row : row + SUB, :]
+            g += 1
+    return scratch[...].T
+
+
+def upper_body(flag_ref, pos_ref, zt_ref, up_ref, low_ref, diag_ref, v_ref, vt_ref, *outs):
+    g_ref, gv_ref, a_ref, yp_ref, l_ref, scratch = outs
+    z = in_order(pos_ref, [zt_ref], 0, scratch)
+    g = -z * row_flags(z.shape[0], flag_ref[0], flag_ref[1])
+    g_ref[...] = g
+    on_first = flag_ref[4].astype(F32)
+    a = diag_ref[0] * on_first - dot3(local_lines(up_ref, 0), g)
+    a_ref[...] = a
+    below = g * row_flags(z.shape[0], flag_ref[2], flag_ref[3])
+    gv = dot3(below, v_ref[...])
+    gv_ref[...] = gv
+    u = local_lines(low_ref, 0)
+    yp = dot3(a, v_ref[...]) + dot3(u, below).T
+    yp_ref[...] = -yp
+    l_ref[...] = dot3(vt_ref[...], yp) + dot3(u, gv) + diag_ref[1] * on_first
+
+
+def upper(j, flags, pos, zt, pieces, diag, v, vt):
+    cols = zt.shape[2]
+    square = jax.ShapeDtypeStruct((W, W), F32)
+    tall = jax.ShapeDtypeStruct((cols, W), F32)
+    def whole(x):
+        return pl.BlockSpec(x.shape, lambda i: (0,) * x.ndim)
+
+    def own(s):
+        return pl.BlockSpec((PIECES, 1, 2, SUB, W), lambda i: (0, s, 0, 0, 0))
+
+    out_shape = (tall, tall, square, square, square)
+    return pl.pallas_call(
+        upper_body,
+        out_shape=out_shape,
+        grid=(1,),
+        in_specs=[pl.BlockSpec(memory_space=pltpu.SMEM)] * 2
+        + [whole(zt), own(j), own(UPPER_NODES_1 + j), whole(diag), whole(v), whole(vt)],
+        out_specs=tuple(whole(o) for o in out_shape),
+        scratch_shapes=[pltpu.VMEM((W, cols), F32)],
+        compiler_params=params(),
+        cost_estimate=cost(24 * W * W * (cols + W), 4 * W * (6 * cols + 8 * W)),
+        name="upper",
+    )(flags, pos, zt, pieces, pieces, diag, v, vt)
+
+
+def lower_body(parts, flag_ref, pos_ref, *refs):
+    zt_refs = refs[:parts]
+    low_ref, g0, g1, gv0, gv1, l0, l1, panel_ref, late_ref, scratch = refs[parts:]
+    for j, g_ref in enumerate((g0, g1)):
+        panel_ref[:, j * W : (j + 1) * W] = g_ref[...]
+    for c, (gv_ref, l_ref) in enumerate(((gv0, l0), (gv1, l1))):
+        z = in_order(pos_ref, zt_refs, c, scratch)
+        z = z * row_flags(z.shape[0], flag_ref[2 * c], flag_ref[2 * c + 1])
+        col = (UPPER_NODES_1 + c) * W
+        panel_ref[:, col : col + W] = -(gv_ref[...] + z)
+        late_ref[c * W : (c + 1) * W, :] = l_ref[...] + dot3(local_lines(low_ref, c), z)
+
+
+def lower(flags, pos, zts, low, ups):
+    cols = zts[0].shape[2]
+    operands = [ups[j][i] for i in (0, 1, 4) for j in range(UPPER_NODES_1)]
+    def whole(x):
+        return pl.BlockSpec(x.shape, lambda i: (0,) * x.ndim)
+
+    out_shape = (
+        jax.ShapeDtypeStruct((cols, 4 * W), F32),
+        jax.ShapeDtypeStruct((LOWER_NODES_2 * W, W), F32),
+    )
+    return pl.pallas_call(
+        lambda *refs: lower_body(len(zts), *refs),
+        out_shape=out_shape,
+        grid=(1,),
+        in_specs=[pl.BlockSpec(memory_space=pltpu.SMEM)] * 2
+        + [whole(z) for z in zts]
+        + [pl.BlockSpec((PIECES, LOWER_NODES_2, 2, SUB, W), lambda i: (0, 1, 0, 0, 0))]
+        + [whole(o) for o in operands],
+        out_specs=tuple(whole(o) for o in out_shape),
+        scratch_shapes=[pltpu.VMEM((W, cols), F32)],
+        compiler_params=params(),
+        cost_estimate=cost(12 * W * W * cols, 4 * W * (12 * cols + 6 * W)),
+        name="lower",
+    )(flags, pos, *zts, low, *operands)
+
+
+def device_at(z, y, x, c):
+    return ((z * CHIPS_Y + y) * CHIPS_X + x) * CORES + c
+
+
+def moves(f):
+    pairs = []
+    for z in range(CHIPS_Z):
+        for y in range(CHIPS_Y):
+            for x in range(CHIPS_X):
+                for c in range(CORES):
+                    pairs.append((device_at(z, y, x, c), device_at(*f(z, y, x, c))))
+    return pairs
+
+
+ALONG_Z = moves(lambda z, y, x, c: ((z + 1) % CHIPS_Z, y, x, c))
+AGAINST_Z = moves(lambda z, y, x, c: ((z - 1) % CHIPS_Z, y, x, c))
+ALONG_Y = moves(lambda z, y, x, c: (z, 1 - y, x, c))
+ALONG_X = moves(lambda z, y, x, c: (z, y, 1 - x, c))
+ALONG_C = moves(lambda z, y, x, c: (z, y, x, 1 - c))
+
+
+def move(x, pairs):
+    return lax.ppermute(x, "blk", pairs)
+
+
+def sync(values, after):
+    values, after = list(values), list(after)
+    anywhere = pl.BlockSpec(memory_space=pl.ANY)
+    return pl.pallas_call(
+        lambda *refs: None,
+        out_shape=[jax.ShapeDtypeStruct(x.shape, x.dtype) for x in values],
+        in_specs=[anywhere] * (len(values) + len(after)),
+        out_specs=[anywhere] * len(values),
+        input_output_aliases={i: i for i in range(len(values))},
+        compiler_params=params(),
+        cost_estimate=cost(0, 0),
+        name="sync",
+    )(*values, *after)
+
+
+def other_core(lines):
+    return [move(a, ALONG_C) for a in lines]
+
+
+def piece_order(me):
+    c = me % CORES
+    x = me // CORES % CHIPS_X
+    y = me // (CORES * CHIPS_X) % CHIPS_Y
+    z = me // (CORES * CHIPS_X * CHIPS_Y)
+    def chip(yy, xx, cc):
+        return [
+            device_at((z + CHIPS_Z - back) % CHIPS_Z, yy, xx, cc) for back in range(CHIPS_Z)
+        ]
+
+    near, corner = [], []
+    for cc in (c, 1 - c):
+        near.append(chip(y, x, cc) + chip(y, 1 - x, cc) + chip(1 - y, x, cc))
+        corner.append(chip(1 - y, 1 - x, cc))
+    return jnp.stack(near[0] + near[1] + corner[0] + corner[1]).astype(jnp.int32)
+
+
+def summed(me, share):
+    core = me % CORES
+    kept = lax.dynamic_index_in_dim(share, core, 1, keepdims=False)
+    sent = lax.dynamic_index_in_dim(share, 1 - core, 1, keepdims=False)
+    half = kept + move(sent, ALONG_C)
+    groups = [
+        [device_at(0, 0, 0, c) + CORES * i for i in range(share.shape[0])] for c in range(CORES)
+    ]
+    return jnp.sum(
+        lax.all_to_all(half, "blk", 0, 0, axis_index_groups=groups, tiled=True), axis=0
+    )
+
+
+def one_group(sigma_anc, panels, diag_inv, scaled_parent_panel, struct_upper, struct_lower):
+    me = lax.axis_index("blk")
+    pos = piece_order(me)
+    v = scaled_parent_panel.reshape(LOWER_NODES_2, W, W)
+    vt = jnp.transpose(v, (0, 2, 1))
+    diag = diag_inv.reshape(UPPER_NODES_1 + LOWER_NODES_2, W, W)
+    own_blocks = 2 * me + jnp.arange(2, dtype=jnp.int32)
+    on_first = (me == 0).astype(jnp.int32)[None]
+
+    def owns(row):
+        return jnp.any(row[None, :] == own_blocks[:, None], axis=1).astype(jnp.int32)
+
+    def finish_upper(j, gathered):
+        zt = product(struct_upper[j], sigma_anc, gathered, 1, j)
+        return upper(j, upper_flags[j], pos, zt, pieces, upper_diag[j], v[j], vt[j])
+
+    def both_cores(lines):
+        return lines + other_core(lines)
+
+    low_blocks = struct_lower.reshape(SLOTS)
+    pieces = transposed_pieces(panels, 0, 4)
+    spread = lax.all_to_all(pieces, "blk", 0, 0, tiled=True).reshape(-1, SUB, W)
+
+    def offsets(blocks, which):
+        return 8 * (blocks // 2) + 2 * which + blocks % 2
+
+    which = jnp.arange(LOWER_NODES_2, dtype=jnp.int32)[:, None]
+    upper_flags = [
+        jnp.concatenate([owns(struct_upper[j]), owns(struct_lower[j]), on_first])
+        for j in range(UPPER_NODES_1)
+    ]
+    upper_diag = [jnp.stack([diag[j], diag[UPPER_NODES_1 + j]]) for j in range(UPPER_NODES_1)]
+    lower_flags = jnp.concatenate([owns(struct_lower[0]), owns(struct_lower[1])])
+    own = picked(offsets(struct_upper, which).reshape(-1), spread)
+    own_low = picked(offsets(struct_lower, UPPER_NODES_1 + which).reshape(-1), spread)
+    small = upper_flags + upper_diag + [v[0], v[1], vt[0], vt[1], lower_flags, pos, low_blocks]
+    own, own_low, *small = sync([own, own_low, *small], [])
+    upper_flags, upper_diag, v, vt = (small[i : i + 2] for i in range(0, 8, 2))
+    lower_flags, pos, low_blocks = small[8:]
+
+    lines, xs, ys = [own], [], []
+    far_lines, far_xs, far_ys = [], [], []
+    for step in range(CHIPS_Z - 1):
+        moved = [move(lines[-1], d) for d in (ALONG_Z, ALONG_X, ALONG_Y)]
+        swapped = [move(lines[-1], ALONG_C)]
+        if step > 0:
+            swapped.append(move(xs[-1] if step == 1 else ys[0], ALONG_C))
+        line, x, y = sync(moved, swapped)
+        lines, xs, ys = lines + [line], xs + [x], ys + [y]
+        far_lines.append(swapped[0])
+        if step > 0:
+            (far_xs if step == 1 else far_ys).append(swapped[1])
+    moved = [
+        move(lines[3], ALONG_X),
+        move(lines[3], ALONG_Y),
+        move(ys[0], ALONG_X),
+        move(xs[1], ALONG_Y),
+        move(own_low, ALONG_Z),
+    ]
+    swapped = other_core([lines[3], xs[1], ys[1], xs[2], ys[2]])
+    x3, y3, d0, d1, behind = sync(moved, swapped)
+    far_lines.append(swapped[0])
+    far_xs += swapped[1::2]
+    far_ys += swapped[2::2]
+    xs, ys = xs + [x3], ys + [y3]
+    moved = [
+        move(ys[2], ALONG_X),
+        move(xs[3], ALONG_Y),
+        move(behind, ALONG_Z),
+        move(own_low, AGAINST_Z),
+        jnp.concatenate([own_low, behind]),
+    ]
+    swapped = other_core([xs[3], ys[3], d0, d1])
+    d2, d3, across, before, first_pair = sync(moved, swapped)
+    far_xs.append(swapped[0])
+    far_ys.append(swapped[1])
+    gathered = lines + xs + ys + far_lines + far_xs + far_ys
+    gathered += [d0, d1, d2, d3, swapped[2], swapped[3], *other_core([d2, d3])]
+
+    s = [first_pair, jnp.concatenate([across, before])]
+    sides = [move(a, ALONG_X) for a in s] + [move(a, ALONG_Y) for a in s]
+    up0 = finish_upper(0, gathered)
+    sides = list(sync(sides, [up0[2]]))
+    corner = [move(sides[2], ALONG_X), move(sides[1], ALONG_Y)]
+    near = both_cores(s + sides)
+    up1 = finish_upper(1, gathered)
+    corner = list(sync(corner, [up1[2], *near]))
+    zt = product(low_blocks, sigma_anc, near + both_cores(corner), LOWER_NODES_2)
+    panel, late = lower(lower_flags, pos, [zt], pieces, (up0, up1))
+    chips = PIECES // CORES
+    diag_share = jnp.concatenate([up0[2], up1[2], late]).reshape(chips, CORES, -1, W)
+    parent_share = jnp.concatenate([up0[3], up1[3]]).reshape(chips, CORES, -1, W)
+    total = summed(me, jnp.concatenate([diag_share, parent_share], axis=2))
+    diag_rows = diag_share.shape[2]
+    return panel, total[:diag_rows], total[diag_rows:]
 
 
 def block_table(struct_upper, struct_lower, blocks):
@@ -144,8 +536,9 @@
 
 
 def solution(mesh):
+    single = mesh.shape["grp"] == 1 and mesh.shape["blk"] == PIECES
     return jax.shard_map(
-        per_device,
+        one_group if single else per_device,
         mesh=mesh,
         in_specs=(P("grp", "blk"), P(("grp", "blk"), None), P(), P(), P(), P()),
         out_specs=(P(("blk", "grp"), None), P("blk", None), P("blk", None)),

time: 672 us -> 268 us (0.40)
  waiting for transfers between devices: 486 us -> 107 us
  matrix products: 136 us -> 0 us
  Pallas kernels: 0 us -> 65.9 us
  starting transfers between devices: 0.08 us -> 36.9 us
  blocking collectives: 0 us -> 26 us
  between operations: 14.2 us -> 1.41 us
  other arithmetic: 15.1 us -> 7.06 us
    all_gather x1 -> x0, waiting for transfers between devices: 367 us -> none  [per_device(): grouped = lax.all_gather(upanel, 'blk', axis=0, tiled=True)]
    dot_general x13 -> x0, matrix products: 136 us -> none  [the longest x1 115 us: per_device(): lax.dot_general(sigma_anc, grouped, (((0,), (0,)), ((), ())), precision=H...]
    psum x1 -> x0, waiting for transfers between devices: 119 us -> none  [per_device(): summed = lax.psum(terms, ('grp', 'blk'))]
    ppermute x0 -> x49, waiting for transfers between devices: none -> 66.7 us  [move(): return lax.ppermute(x, 'blk', pairs)]
    pallas_call x0 -> x17, Pallas kernels: none -> 65.9 us  [the longest x3 43.6 us: product(): pl.pallas_call(lambda *refs: product_body(accs, *refs), out_shape=jax.Sha...]
    all_to_all x0 -> x1, waiting for transfers between devices: none -> 40.2 us  [one_group(): spread = lax.all_to_all(pieces, 'blk', 0, 0, tiled=True).reshape(-1, SUB, W)]
    ppermute x0 -> x49, starting transfers between devices: none -> 29.6 us  [move(): return lax.ppermute(x, 'blk', pairs)]
    all_to_all x0 -> x1, blocking collectives: none -> 26 us  [summed(): lax.all_to_all(half, 'blk', 0, 0, axis_index_groups=groups, tiled=True)]
  transfers between devices with their start and end apart: 2 -> 50, of which waited for: 2 -> 18; matrix products, arithmetic and copies ran while one was open for 2% -> 5% of each run, Pallas kernels for 0% -> 14%
where the time goes in v1:
time: 268 us; the launch traced here: 267 us
  waiting for transfers between devices  107 us (40%)
  Pallas kernels  65.9 us (25%)
  starting transfers between devices  36.9 us (14%)
  blocking collectives  26 us (10%)
  local copies, waits for them, and re-layouts  23.3 us (9%)
  other arithmetic  7.06 us (3%)
    ppermute x49, waiting for transfers between devices, move(): return lax.ppermute(x, 'blk', pairs)  66.7 us
    pallas_call x3, Pallas kernels, product(): pl.pallas_call(lambda *refs: product_body(accs, *refs), out_shape=jax.Sha...  43.6 us
    all_to_all x1, waiting for transfers between devices, one_group(): spread = lax.all_to_all(pieces, 'blk', 0, 0, tiled=True).reshape(-1, SUB, W)  40.2 us
    ppermute x49, starting transfers between devices, move(): return lax.ppermute(x, 'blk', pairs)  29.6 us
    all_to_all x1, blocking collectives, summed(): lax.all_to_all(half, 'blk', 0, 0, axis_index_groups=groups, tiled=True)  26 us
    unnamed x113, local copies, waits for them, and re-layouts  15.5 us
    pallas_call x2, Pallas kernels, upper(): pl.pallas_call(upper_body, out_shape=out_shape, grid=(1,), in_specs=[pl.B...  9.18 us
    all_to_all x1, starting transfers between devices, one_group(): spread = lax.all_to_all(pieces, 'blk', 0, 0, tiled=True).reshape(-1, SUB, W)  7.3 us
  transfers between devices with their start and end apart: 50, of which 18 were waited for; matrix products, arithmetic and copies ran while one was open for 5% of the time, Pallas kernels for 14%

profile of v1, /device:TPU:0, one launch (start us, length us, event | category | flops | bytes accessed | tf_op | source)
XLA Modules:
  0.0 267.4 jit_solution(10560657768310035915)
XLA Ops:
  0.6 3.5 %transposed_pieces.1.up_ref.low_ref.refs_3_ = f32[32,4,2,8,256]{4,3,2,1,0:T(8,128)} custom-call(f32[512,1024]{1,0:T(8,128)} %x_ref.1), custom_call_target="tpu_custom_call" | custom-call | bytes 4194304 | tf_op jit(solution)/shard_map/transposed_pieces/pallas_call | solution.py:58
  4.1 7.3 %all-to-all-start = ((f32[32,4,2,8,256]{4,3,2,1,0:T(8,128)}), f32[32,4,2,8,256]{4,3,2,1,0:T(8,128)S(1)}, u32[]{:S(2)}, u32[]{:S(2)}) async-start(f32[32,4,2,8,256]{4,3,2,1,0:T(8,128)} %transposed_pieces.1.up_ref.low_ref.refs_3_), calls=%async_computation | async-start | bytes 4194304 | tf_op jit(solution)/shard_map/all_to_all | solution.py:330
  20.1 40.2 %all-to-all-done = f32[32,4,2,8,256]{4,3,2,1,0:T(8,128)S(1)} async-done(((f32[32,4,2,8,256]{4,3,2,1,0:T(8,128)}), f32[32,4,2,8,256]{4,3,2,1,0:T(8,128)S(1)}, u32[]{:S(2)}, u32[]{:S(2)}) %all-to-all-start) | async-done | bytes 2097184 | tf_op jit(solution)/shard_map/all_to_all | solution.py:330
  61.7 2.5 picked.2.refs_0_
  64.1 2.3 picked.3.refs_1_
  69.3 12.7 %collective-permute-done.refs_0_ = f32[1,64,8,256]{3,2,1,0:T(8,128)S(1)} collective-permute-done((f32[1,64,8,256]{3,2,1,0:T(8,128)}, f32[1,64,8,256]{3,2,1,0:T(8,128)S(1)}, u32[]{:S(2)}, u32[]{:S(2)}) %collective-permute-start) | collective-permute-done | bytes 524320 | tf_op jit(solution)/shard_map/ppermute | solution.py:257
  87.2 11.3 %collective-permute-done.4.refs_0_ = f32[1,64,8,256]{3,2,1,0:T(8,128)S(1)} collective-permute-done((f32[1,64,8,256]{3,2,1,0:T(8,128)}, f32[1,64,8,256]{3,2,1,0:T(8,128)S(1)}, u32[]{:S(2)}, u32[]{:S(2)}) %collective-permute-start.4) | collective-permute-done | bytes 524320 | tf_op jit(solution)/shard_map/ppermute | solution.py:257
  104.5 10.6 %collective-permute-done.10.refs_1_ = f32[1,64,8,256]{3,2,1,0:T(8,128)S(1)} collective-permute-done((f32[1,64,8,256]{3,2,1,0:T(8,128)}, f32[1,64,8,256]{3,2,1,0:T(8,128)S(1)}, u32[]{:S(2)}, u32[]{:S(2)}) %collective-permute-start.10) | collective-permute-done | bytes 524320 | tf_op jit(solution)/shard_map/ppermute | solution.py:257
  118.7 1.5 collective-permute-done.9.refs_0_
  121.0 4.5 %collective-permute-done.19.refs_4_ = f32[1,32,8,256]{3,2,1,0:T(8,128)} collective-permute-done((f32[1,32,8,256]{3,2,1,0:T(8,128)S(1)}, f32[1,32,8,256]{3,2,1,0:T(8,128)}, u32[]{:S(2)}, u32[]{:S(2)}) %collective-permute-start.19) | collective-permute-done | bytes 262176 | tf_op jit(solution)/shard_map/ppermute | solution.py:257
  126.0 3.1 %collective-permute-done.17.refs_2_ = f32[1,64,8,256]{3,2,1,0:T(8,128)S(1)} collective-permute-done((f32[1,64,8,256]{3,2,1,0:T(8,128)}, f32[1,64,8,256]{3,2,1,0:T(8,128)S(1)}, u32[]{:S(2)}, u32[]{:S(2)}) %collective-permute-start.17) | collective-permute-done | bytes 524320 | tf_op jit(solution)/shard_map/ppermute | solution.py:257
  129.1 2.0 collective-permute-start.16
  131.7 8.2 %collective-permute-done.15.refs_0_ = f32[1,64,8,256]{3,2,1,0:T(8,128)S(1)} collective-permute-done((f32[1,64,8,256]{3,2,1,0:T(8,128)}, f32[1,64,8,256]{3,2,1,0:T(8,128)S(1)}, u32[]{:S(2)}, u32[]{:S(2)}) %collective-permute-start.15) | collective-permute-done | bytes 524320 | tf_op jit(solution)/shard_map/ppermute | solution.py:257
  143.7 2.0 collective-permute-start.26
  147.2 6.9 %collective-permute-done.27.refs_3_ = f32[1,32,8,256]{3,2,1,0:T(8,128)} collective-permute-done((f32[1,32,8,256]{3,2,1,0:T(8,128)S(1)}, f32[1,32,8,256]{3,2,1,0:T(8,128)}, u32[]{:S(2)}, u32[]{:S(2)}) %collective-permute-start.27) | collective-permute-done | bytes 262176 | tf_op jit(solution)/shard_map/ppermute | solution.py:257
  154.6 1.8 pad_maximum_fusion.3.refs_4_
  166.7 14.4 %product.3.zt_ref = f32[1,256,512]{2,1,0:T(8,128)} custom-call(s32[32]{0:T(128)} %copy-done.53, f32[16384,512]{1,0:T(8,128)} %refs_4_.5, f32[16384,512]{1,0:T(8,128)} %refs_4_.5, f32[16384,512]{1,0:T(8,128)} %refs_4_.5, f32[16384,512]{1,0:T(8,128)} %refs_4_.5, f32[1,64,8,256]{3,2,1,0:T(8,128)} %get-tuple-element.56.refs_5_, ...), custom_call_target="tpu_custom_call" | custom-call | flops 6442450944 | bytes 25165824 | tf_op jit(solution)/shard_map/product/pallas_call | solution.py:120
  181.2 4.6 %upper.2 = (f32[512,256]{1,0:T(8,128)}, f32[512,256]{1,0:T(8,128)}, f32[256,256]{1,0:T(8,128)}, f32[256,256]{1,0:T(8,128)}, f32[256,256]{1,0:T(8,128)}) custom-call(s32[5]{0:T(128)} %get-tuple-element.75.flag_ref, s32[32]{0:T(128)} %get-tuple-element.54.pos_ref.refs_1_, f32[1,256,512]{2,1,0:T(8,128)} %product.3.zt_ref, ...), custom_call_target="tpu_custom_call" | custom-call | flops 1207959552 | bytes 5242880 | tf_op jit(solution)/shard_map/upper/pallas_call | solution.py:182
  191.5 14.5 %product.4.zt_ref = f32[1,256,512]{2,1,0:T(8,128)} custom-call(s32[32]{0:T(128)} %copy-done.52, f32[16384,512]{1,0:T(8,128)} %refs_4_.5, f32[16384,512]{1,0:T(8,128)} %refs_4_.5, f32[16384,512]{1,0:T(8,128)} %refs_4_.5, f32[16384,512]{1,0:T(8,128)} %refs_4_.5, f32[1,64,8,256]{3,2,1,0:T(8,128)} %get-tuple-element.56.refs_5_, ...), custom_call_target="tpu_custom_call" | custom-call | flops 6442450944 | bytes 25165824 | tf_op jit(solution)/shard_map/product/pallas_call | solution.py:120
  206.0 4.5 %upper.3 = (f32[512,256]{1,0:T(8,128)}, f32[512,256]{1,0:T(8,128)}, f32[256,256]{1,0:T(8,128)}, f32[256,256]{1,0:T(8,128)}, f32[256,256]{1,0:T(8,128)}) custom-call(s32[5]{0:T(128)} %get-tuple-element.86.flag_ref, s32[32]{0:T(128)} %get-tuple-element.54.pos_ref.refs_1_, f32[1,256,512]{2,1,0:T(8,128)} %product.4.zt_ref, ...), custom_call_target="tpu_custom_call" | custom-call | flops 1207959552 | bytes 5242880 | tf_op jit(solution)/shard_map/upper/pallas_call | solution.py:182
  215.7 14.7 %product.5.refs_2_ = f32[2,256,512]{2,1,0:T(8,128)} custom-call(s32[32]{0:T(128)} %get-tuple-element.55.refs_0_, f32[16384,512]{1,0:T(8,128)} %refs_4_.5, f32[16384,512]{1,0:T(8,128)} %refs_4_.5, f32[16384,512]{1,0:T(8,128)} %refs_4_.5, f32[16384,512]{1,0:T(8,128)} %refs_4_.5, f32[2,32,8,256]{3,2,1,0:T(8,128)} %get-tuple-element.72.refs_3_.refs_5_, ...), custom_call_target="tpu_custom_call" | custom-call | flops 6442450944 | bytes 25165824 | tf_op jit(solution)/shard_map/product/pallas_call | solution.py:120
  230.4 4.8 %lower.1 = (f32[512,1024]{1,0:T(8,128)}, f32[512,256]{1,0:T(8,128)}) custom-call(s32[4]{0:T(128)} %get-tuple-element.53.refs_0_, s32[32]{0:T(128)} %get-tuple-element.54.pos_ref.refs_1_, f32[2,256,512]{2,1,0:T(8,128)} %product.5.refs_2_, f32[32,4,2,8,256]{4,3,2,1,0:T(8,128)} %transposed_pieces.1.up_ref.low_ref.refs_3_, ...), custom_call_target="tpu_custom_call" | custom-call | flops 402653184 | bytes 7864320 | tf_op jit(solution)/shard_map/lower/pallas_call | solution.py:219
  236.8 2.1 collective-permute-done.48
  240.1 26.0 %all_to_all.10 = f32[16,48,256]{2,1,0:T(8,128)S(1)} all-to-all(f32[16,48,256]{2,1,0:T(8,128)S(1)} %fusion.4), channel_id=1, replica_groups={{0,2,4,6,8,10,12,14,16,18,20,22,24,26,28,30},{1,3,5,7,9,11,13,15,17,19,..., dimensions={0} | all-to-all | bytes 1572864 | tf_op jit(solution)/shard_map/all_to_all | solution.py:305
  (240 shorter events, 60.2 us)
Async XLA Ops:
  4.1 56.2 %all-to-all-start = ((f32[32,4,2,8,256]{4,3,2,1,0:T(8,128)}), f32[32,4,2,8,256]{4,3,2,1,0:T(8,128)S(1)}, u32[]{:S(2)}, u32[]{:S(2)}) async-start(f32[32,4,2,8,256]{4,3,2,1,0:T(8,128)} %transposed_pieces.1.up_ref.low_ref.refs_3_), calls=%async_computation | async-start | bytes 4194304 | tf_op jit(solution)/shard_map/all_to_all | solution.py:330
  66.5 15.5 %collective-permute-start = (f32[1,64,8,256]{3,2,1,0:T(8,128)}, f32[1,64,8,256]{3,2,1,0:T(8,128)S(1)}, u32[]{:S(2)}, u32[]{:S(2)}) collective-permute-start(f32[1,64,8,256]{3,2,1,0:T(8,128)} %get-tuple-element.56.refs_5_), channel_id=1, source_target_pairs={{0,8},{1,9},{2,10},{3,11},{4,12},{5,13},{6,14},{7,15},{8,16},{9,17... | collective-permute-start | bytes 1572872 | tf_op jit(solution)/shard_map/ppermute | solution.py:257
  66.5 15.5 %collective-permute-start.1 = (f32[1,64,8,256]{3,2,1,0:T(8,128)}, f32[1,64,8,256]{3,2,1,0:T(8,128)S(1)}, u32[]{:S(2)}, u32[]{:S(2)}) collective-permute-start(f32[1,64,8,256]{3,2,1,0:T(8,128)} %get-tuple-element.56.refs_5_), channel_id=1, source_target_pairs={{0,2},{1,3},{2,0},{3,1},{4,6},{5,7},{6,4},{7,5},{8,10},{9,11},{10,... | collective-permute-start | bytes 1572872 | tf_op jit(solution)/shard_map/ppermute | solution.py:257
  67.9 14.1 %collective-permute-start.2 = (f32[1,64,8,256]{3,2,1,0:T(8,128)}, f32[1,64,8,256]{3,2,1,0:T(8,128)S(1)}, u32[]{:S(2)}, u32[]{:S(2)}) collective-permute-start(f32[1,64,8,256]{3,2,1,0:T(8,128)} %get-tuple-element.56.refs_5_), channel_id=1, source_target_pairs={{0,4},{1,5},{2,6},{3,7},{4,0},{5,1},{6,2},{7,3},{8,12},{9,13},{10,... | collective-permute-start | bytes 1572872 | tf_op jit(solution)/shard_map/ppermute | solution.py:257
  83.9 14.6 %collective-permute-start.4 = (f32[1,64,8,256]{3,2,1,0:T(8,128)}, f32[1,64,8,256]{3,2,1,0:T(8,128)S(1)}, u32[]{:S(2)}, u32[]{:S(2)}) collective-permute-start(f32[1,64,8,256]{3,2,1,0:T(8,128)} %get-tuple-element.57.refs_6_), channel_id=1, source_target_pairs={{0,8},{1,9},{2,10},{3,11},{4,12},{5,13},{6,14},{7,15},{8,16},{9,17... | collective-permute-start | bytes 1572872 | tf_op jit(solution)/shard_map/ppermute | solution.py:257
  83.9 14.6 %collective-permute-start.5 = (f32[1,64,8,256]{3,2,1,0:T(8,128)}, f32[1,64,8,256]{3,2,1,0:T(8,128)S(1)}, u32[]{:S(2)}, u32[]{:S(2)}) collective-permute-start(f32[1,64,8,256]{3,2,1,0:T(8,128)} %get-tuple-element.57.refs_6_), channel_id=1, source_target_pairs={{0,2},{1,3},{2,0},{3,1},{4,6},{5,7},{6,4},{7,5},{8,10},{9,11},{10,... | collective-permute-start | bytes 1572872 | tf_op jit(solution)/shard_map/ppermute | solution.py:257
  100.6 14.4 %collective-permute-start.10 = (f32[1,64,8,256]{3,2,1,0:T(8,128)}, f32[1,64,8,256]{3,2,1,0:T(8,128)S(1)}, u32[]{:S(2)}, u32[]{:S(2)}) collective-permute-start(f32[1,64,8,256]{3,2,1,0:T(8,128)} %get-tuple-element.59.refs_7_), channel_id=1, source_target_pairs={{0,2},{1,3},{2,0},{3,1},{4,6},{5,7},{6,4},{7,5},{8,10},{9,11},{10,... | collective-permute-start | bytes 1572872 | tf_op jit(solution)/shard_map/ppermute | solution.py:257
  102.0 14.4 %collective-permute-start.11 = (f32[1,64,8,256]{3,2,1,0:T(8,128)}, f32[1,64,8,256]{3,2,1,0:T(8,128)S(1)}, u32[]{:S(2)}, u32[]{:S(2)}) collective-permute-start(f32[1,64,8,256]{3,2,1,0:T(8,128)} %get-tuple-element.59.refs_7_), channel_id=1, source_target_pairs={{0,4},{1,5},{2,6},{3,7},{4,0},{5,1},{6,2},{7,3},{8,12},{9,13},{10,... | collective-permute-start | bytes 1572872 | tf_op jit(solution)/shard_map/ppermute | solution.py:257
  103.5 15.2 %collective-permute-start.12 = (f32[1,64,8,256]{3,2,1,0:T(8,128)}, f32[1,64,8,256]{3,2,1,0:T(8,128)S(1)}, u32[]{:S(2)}, u32[]{:S(2)}) collective-permute-start(f32[1,64,8,256]{3,2,1,0:T(8,128)} %get-tuple-element.59.refs_7_), channel_id=1, source_target_pairs={{0,1},{1,0},{2,3},{3,2},{4,5},{5,4},{6,7},{7,6},{8,9},{9,8},{10,11... | collective-permute-start | bytes 1572872 | tf_op jit(solution)/shard_map/ppermute | solution.py:257
  103.5 16.7 %collective-permute-start.9 = (f32[1,64,8,256]{3,2,1,0:T(8,128)}, f32[1,64,8,256]{3,2,1,0:T(8,128)S(1)}, u32[]{:S(2)}, u32[]{:S(2)}) collective-permute-start(f32[1,64,8,256]{3,2,1,0:T(8,128)} %get-tuple-element.59.refs_7_), channel_id=1, source_target_pairs={{0,8},{1,9},{2,10},{3,11},{4,12},{5,13},{6,14},{7,15},{8,16},{9,17... | collective-permute-start | bytes 1572872 | tf_op jit(solution)/shard_map/ppermute | solution.py:257
  103.5 22.1 %collective-permute-start.19 = (f32[1,32,8,256]{3,2,1,0:T(8,128)S(1)}, f32[1,32,8,256]{3,2,1,0:T(8,128)}, u32[]{:S(2)}, u32[]{:S(2)}) collective-permute-start(f32[1,32,8,256]{3,2,1,0:T(8,128)S(1)} %copy-done.34), channel_id=1, source_target_pairs={{0,8},{1,9},{2,10},{3,11},{4,12},{5,13},{6,14},{7,15},{8,16},{9,17... | collective-permute-start | bytes 786440 | tf_op jit(solution)/shard_map/ppermute | solution.py:257
  115.0 14.1 %collective-permute-start.17 = (f32[1,64,8,256]{3,2,1,0:T(8,128)}, f32[1,64,8,256]{3,2,1,0:T(8,128)S(1)}, u32[]{:S(2)}, u32[]{:S(2)}) collective-permute-start(f32[1,64,8,256]{3,2,1,0:T(8,128)} %get-tuple-element.60.refs_13_), channel_id=1, source_target_pairs={{0,2},{1,3},{2,0},{3,1},{4,6},{5,7},{6,4},{7,5},{8,10},{9,11},{10,... | collective-permute-start | bytes 1572872 | tf_op jit(solution)/shard_map/ppermute | solution.py:257
  125.5 14.3 %collective-permute-start.15 = (f32[1,64,8,256]{3,2,1,0:T(8,128)}, f32[1,64,8,256]{3,2,1,0:T(8,128)S(1)}, u32[]{:S(2)}, u32[]{:S(2)}) collective-permute-start(f32[1,64,8,256]{3,2,1,0:T(8,128)} %get-tuple-element.62.refs_8_), channel_id=1, source_target_pairs={{0,2},{1,3},{2,0},{3,1},{4,6},{5,7},{6,4},{7,5},{8,10},{9,11},{10,... | collective-permute-start | bytes 1572872 | tf_op jit(solution)/shard_map/ppermute | solution.py:257
  139.9 14.2 %collective-permute-start.14 = (f32[1,64,8,256]{3,2,1,0:T(8,128)}, f32[1,64,8,256]{3,2,1,0:T(8,128)}, u32[]{:S(2)}, u32[]{:S(2)}) collective-permute-start(f32[1,64,8,256]{3,2,1,0:T(8,128)} %get-tuple-element.61.refs_15_), channel_id=1, source_target_pairs={{0,2},{1,3},{2,0},{3,1},{4,6},{5,7},{6,4},{7,5},{8,10},{9,11},{10,... | collective-permute-start | bytes 1572872 | tf_op jit(solution)/shard_map/ppermute | solution.py:257
  161.8 24.0 %collective-permute-start.33 = (f32[2,32,8,256]{3,2,1,0:T(8,128)S(1)}, f32[2,32,8,256]{3,2,1,0:T(8,128)S(1)}, u32[]{:S(2)}, u32[]{:S(2)}) collective-permute-start(f32[2,32,8,256]{3,2,1,0:T(8,128)S(1)} %constant_dynamic-update-slice_fusion.refs_4_.refs_6_), channel_id=1, source_target_pairs={{0,2},{1,3},{2,0},{3,1},{4,6},{5,7},{6,4},{7,5},{8,10},{9,11},{10,... | collective-permute-start | bytes 1572872 | tf_op jit(solution)/shard_map/ppermute | solution.py:257
  163.1 22.8 %collective-permute-start.35 = (f32[2,32,8,256]{3,2,1,0:T(8,128)S(1)}, f32[2,32,8,256]{3,2,1,0:T(8,128)S(1)}, u32[]{:S(2)}, u32[]{:S(2)}) collective-permute-start(f32[2,32,8,256]{3,2,1,0:T(8,128)S(1)} %constant_dynamic-update-slice_fusion.refs_4_.refs_6_), channel_id=1, source_target_pairs={{0,4},{1,5},{2,6},{3,7},{4,0},{5,1},{6,2},{7,3},{8,12},{9,13},{10,... | collective-permute-start | bytes 1572872 | tf_op jit(solution)/shard_map/ppermute | solution.py:257
  164.0 22.9 %collective-permute-start.32 = (f32[2,32,8,256]{3,2,1,0:T(8,128)}, f32[2,32,8,256]{3,2,1,0:T(8,128)S(1)}, u32[]{:S(2)}, u32[]{:S(2)}) collective-permute-start(f32[2,32,8,256]{3,2,1,0:T(8,128)} %get-tuple-element.72.refs_3_.refs_5_), channel_id=1, source_target_pairs={{0,2},{1,3},{2,0},{3,1},{4,6},{5,7},{6,4},{7,5},{8,10},{9,11},{10,... | collective-permute-start | bytes 1572872 | tf_op jit(solution)/shard_map/ppermute | solution.py:257
  165.2 22.8 %collective-permute-start.34 = (f32[2,32,8,256]{3,2,1,0:T(8,128)}, f32[2,32,8,256]{3,2,1,0:T(8,128)S(1)}, u32[]{:S(2)}, u32[]{:S(2)}) collective-permute-start(f32[2,32,8,256]{3,2,1,0:T(8,128)} %get-tuple-element.72.refs_3_.refs_5_), channel_id=1, source_target_pairs={{0,4},{1,5},{2,6},{3,7},{4,0},{5,1},{6,2},{7,3},{8,12},{9,13},{10,... | collective-permute-start | bytes 1572872 | tf_op jit(solution)/shard_map/ppermute | solution.py:257
  165.9 24.1 %collective-permute-start.39 = (f32[2,32,8,256]{3,2,1,0:T(8,128)S(1)}, f32[2,32,8,256]{3,2,1,0:T(8,128)}, u32[]{:S(2)}, u32[]{:S(2)}) collective-permute-start(f32[2,32,8,256]{3,2,1,0:T(8,128)S(1)} %constant_dynamic-update-slice_fusion.refs_4_.refs_6_), channel_id=1, source_target_pairs={{0,1},{1,0},{2,3},{3,2},{4,5},{5,4},{6,7},{7,6},{8,9},{9,8},{10,11... | collective-permute-start | bytes 1572872 | tf_op jit(solution)/shard_map/ppermute | solution.py:257
  188.7 21.8 %collective-permute-start.42 = (f32[2,32,8,256]{3,2,1,0:T(8,128)}, f32[2,32,8,256]{3,2,1,0:T(8,128)S(1)}, u32[]{:S(2)}, u32[]{:S(2)}) collective-permute-start(f32[2,32,8,256]{3,2,1,0:T(8,128)} %get-tuple-element.84.refs_7_.refs_9_), channel_id=1, source_target_pairs={{0,1},{1,0},{2,3},{3,2},{4,5},{5,4},{6,7},{7,6},{8,9},{9,8},{10,11... | collective-permute-start | bytes 1572872 | tf_op jit(solution)/shard_map/ppermute | solution.py:257
  189.2 21.4 %collective-permute-start.44 = (f32[2,32,8,256]{3,2,1,0:T(8,128)}, f32[2,32,8,256]{3,2,1,0:T(8,128)S(1)}, u32[]{:S(2)}, u32[]{:S(2)}) collective-permute-start(f32[2,32,8,256]{3,2,1,0:T(8,128)} %get-tuple-element.84.refs_7_.refs_9_), channel_id=1, source_target_pairs={{0,2},{1,3},{2,0},{3,1},{4,6},{5,7},{6,4},{7,5},{8,10},{9,11},{10,... | collective-permute-start | bytes 1572872 | tf_op jit(solution)/shard_map/ppermute | solution.py:257
  190.0 20.6 %collective-permute-start.41 = (f32[2,32,8,256]{3,2,1,0:T(8,128)}, f32[2,32,8,256]{3,2,1,0:T(8,128)S(1)}, u32[]{:S(2)}, u32[]{:S(2)}) collective-permute-start(f32[2,32,8,256]{3,2,1,0:T(8,128)} %get-tuple-element.83.refs_6_.refs_8_), channel_id=1, source_target_pairs={{0,1},{1,0},{2,3},{3,2},{4,5},{5,4},{6,7},{7,6},{8,9},{9,8},{10,11... | collective-permute-start | bytes 1572872 | tf_op jit(solution)/shard_map/ppermute | solution.py:257
  190.0 20.7 %collective-permute-start.45 = (f32[2,32,8,256]{3,2,1,0:T(8,128)}, f32[2,32,8,256]{3,2,1,0:T(8,128)S(1)}, u32[]{:S(2)}, u32[]{:S(2)}) collective-permute-start(f32[2,32,8,256]{3,2,1,0:T(8,128)} %get-tuple-element.83.refs_6_.refs_8_), channel_id=1, source_target_pairs={{0,4},{1,5},{2,6},{3,7},{4,0},{5,1},{6,2},{7,3},{8,12},{9,13},{10,... | collective-permute-start | bytes 1572872 | tf_op jit(solution)/shard_map/ppermute | solution.py:257
  191.3 19.2 %collective-permute-start.43 = (f32[2,32,8,256]{3,2,1,0:T(8,128)}, f32[2,32,8,256]{3,2,1,0:T(8,128)S(1)}, u32[]{:S(2)}, u32[]{:S(2)}) collective-permute-start(f32[2,32,8,256]{3,2,1,0:T(8,128)} %get-tuple-element.85.refs_8_.refs_10_), channel_id=1, source_target_pairs={{0,1},{1,0},{2,3},{3,2},{4,5},{5,4},{6,7},{7,6},{8,9},{9,8},{10,11... | collective-permute-start | bytes 1572872 | tf_op jit(solution)/shard_map/ppermute | solution.py:257
  (82 other events, 468.7 us)

commit v2 on v1

--- a/solution.py
+++ b/solution.py
@@ -19,13 +19,12 @@
 PIECES = CHIPS_Z * CHIPS_Y * CHIPS_X * CORES
 SUB = NODE_WIDTH // PIECES
 SLOTS = 32
-PER_STEP = 4
+PER_STEP = 8
 W = NODE_WIDTH
-VMEM_BYTES = 60 * 1024 * 1024
-
-
-def params(**kw):
-    return pltpu.CompilerParams(vmem_limit_bytes=VMEM_BYTES, **kw)
+
+
+def params(mib):
+    return pltpu.CompilerParams(vmem_limit_bytes=mib * 1024 * 1024)
 
 
 def split(x):
@@ -61,7 +60,7 @@
         grid=(1,),
         in_specs=[pl.BlockSpec((2 * W, count * W), lambda i: (0, first // count))],
         out_specs=pl.BlockSpec(shape, lambda i: (0, 0, 0, 0, 0)),
-        compiler_params=params(),
+        compiler_params=params(16),
         cost_estimate=cost(0, 4 * panels.size * count // 2),
         name="transposed_pieces",
     )(panels)
@@ -81,7 +80,7 @@
             pl.BlockSpec(memory_space=pltpu.VMEM),
         ],
         out_specs=pl.BlockSpec(memory_space=pltpu.VMEM),
-        compiler_params=params(),
+        compiler_params=params(16),
         cost_estimate=cost(0, 4 * (a.size + idx.size * SUB * W)),
         name="picked",
     )(idx, a)
@@ -105,7 +104,7 @@
         o_ref[0] += value
 
 
-def product(idx, sigma, pieces, accs, chunk=0):
+def product(idx, sigma, pieces, accs, chunk=0, mib=40):
     steps = SLOTS // PER_STEP
     cols = sigma.shape[1]
     rows = SUB * sum(p.shape[0] for p in pieces)
@@ -126,7 +125,7 @@
             in_specs=[sig_spec(q) for q in range(PER_STEP)] + piece_specs,
             out_specs=pl.BlockSpec((1, rows, cols), lambda i, idx: (lax.div(i * accs, steps), 0, 0)),
         ),
-        compiler_params=params(),
+        compiler_params=params(mib),
         cost_estimate=cost(6 * SLOTS * rows * W * cols, 4 * SLOTS * W * (cols + rows)),
         name="product",
     )(idx, *([sigma] * PER_STEP), *pieces)
@@ -187,7 +186,7 @@
         + [whole(zt), own(j), own(UPPER_NODES_1 + j), whole(diag), whole(v), whole(vt)],
         out_specs=tuple(whole(o) for o in out_shape),
         scratch_shapes=[pltpu.VMEM((W, cols), F32)],
-        compiler_params=params(),
+        compiler_params=params(24),
         cost_estimate=cost(24 * W * W * (cols + W), 4 * W * (6 * cols + 8 * W)),
         name="upper",
     )(flags, pos, zt, pieces, pieces, diag, v, vt)
@@ -226,7 +225,7 @@
         + [whole(o) for o in operands],
         out_specs=tuple(whole(o) for o in out_shape),
         scratch_shapes=[pltpu.VMEM((W, cols), F32)],
-        compiler_params=params(),
+        compiler_params=params(32),
         cost_estimate=cost(12 * W * W * cols, 4 * W * (12 * cols + 6 * W)),
         name="lower",
     )(flags, pos, *zts, low, *operands)
@@ -266,7 +265,7 @@
         in_specs=[anywhere] * (len(values) + len(after)),
         out_specs=[anywhere] * len(values),
         input_output_aliases={i: i for i in range(len(values))},
-        compiler_params=params(),
+        compiler_params=params(1),
         cost_estimate=cost(0, 0),
         name="sync",
     )(*values, *after)
@@ -293,17 +292,21 @@
     return jnp.stack(near[0] + near[1] + corner[0] + corner[1]).astype(jnp.int32)
 
 
+def exchanged(x, groups):
+    return lax.all_to_all(x, "blk", 0, 0, axis_index_groups=groups, tiled=True)
+
+
 def summed(me, share):
     core = me % CORES
-    kept = lax.dynamic_index_in_dim(share, core, 1, keepdims=False)
-    sent = lax.dynamic_index_in_dim(share, 1 - core, 1, keepdims=False)
-    half = kept + move(sent, ALONG_C)
-    groups = [
-        [device_at(0, 0, 0, c) + CORES * i for i in range(share.shape[0])] for c in range(CORES)
-    ]
-    return jnp.sum(
-        lax.all_to_all(half, "blk", 0, 0, axis_index_groups=groups, tiled=True), axis=0
-    )
+    kept = lax.dynamic_index_in_dim(share, core, 2, keepdims=False)
+    sent = lax.dynamic_index_in_dim(share, 1 - core, 2, keepdims=False)
+    plane = [device_at(0, y, x, 0) for y in range(CHIPS_Y) for x in range(CHIPS_X)]
+    column = [device_at(z, 0, 0, 0) for z in range(CHIPS_Z)]
+    total = kept + move(sent, ALONG_C)
+    total = exchanged(total, [[p + q + c for p in plane] for q in column for c in range(CORES)])
+    total = jnp.sum(total, axis=0)
+    total = exchanged(total, [[p + q + c for q in column] for p in plane for c in range(CORES)])
+    return jnp.sum(total, axis=0)
 
 
 def one_group(sigma_anc, panels, diag_inv, scaled_parent_panel, struct_upper, struct_lower):
@@ -342,9 +345,8 @@
     own = picked(offsets(struct_upper, which).reshape(-1), spread)
     own_low = picked(offsets(struct_lower, UPPER_NODES_1 + which).reshape(-1), spread)
     small = upper_flags + upper_diag + [v[0], v[1], vt[0], vt[1], lower_flags, pos, low_blocks]
-    own, own_low, *small = sync([own, own_low, *small], [])
-    upper_flags, upper_diag, v, vt = (small[i : i + 2] for i in range(0, 8, 2))
-    lower_flags, pos, low_blocks = small[8:]
+    (own,) = sync([own], small)
+    v, vt = small[4:6], small[6:8]
 
     lines, xs, ys = [own], [], []
     far_lines, far_xs, far_ys = [], [], []
@@ -353,7 +355,10 @@
         swapped = [move(lines[-1], ALONG_C)]
         if step > 0:
             swapped.append(move(xs[-1] if step == 1 else ys[0], ALONG_C))
-        line, x, y = sync(moved, swapped)
+        if step == 0:
+            line, x, y, own_low = sync(moved + [own_low], swapped)
+        else:
+            line, x, y = sync(moved, swapped)
         lines, xs, ys = lines + [line], xs + [x], ys + [y]
         far_lines.append(swapped[0])
         if step > 0:
@@ -393,13 +398,13 @@
     near = both_cores(s + sides)
     up1 = finish_upper(1, gathered)
     corner = list(sync(corner, [up1[2], *near]))
-    zt = product(low_blocks, sigma_anc, near + both_cores(corner), LOWER_NODES_2)
+    zt = product(low_blocks, sigma_anc, near + both_cores(corner), LOWER_NODES_2, mib=60)
     panel, late = lower(lower_flags, pos, [zt], pieces, (up0, up1))
-    chips = PIECES // CORES
-    diag_share = jnp.concatenate([up0[2], up1[2], late]).reshape(chips, CORES, -1, W)
-    parent_share = jnp.concatenate([up0[3], up1[3]]).reshape(chips, CORES, -1, W)
-    total = summed(me, jnp.concatenate([diag_share, parent_share], axis=2))
-    diag_rows = diag_share.shape[2]
+    by_device = (CHIPS_Z, CHIPS_Y * CHIPS_X, CORES, -1, W)
+    diag_share = jnp.concatenate([up0[2], up1[2], late]).reshape(by_device)
+    parent_share = jnp.concatenate([up0[3], up1[3]]).reshape(by_device)
+    total = summed(me, jnp.swapaxes(jnp.concatenate([diag_share, parent_share], axis=3), 0, 1))
+    diag_rows = diag_share.shape[3]
     return panel, total[:diag_rows], total[diag_rows:]
 
 

time: 268 us -> 245 us (0.914)
  Pallas kernels: 65.9 us -> 49.1 us
  local copies, waits for them, and re-layouts: 23.3 us -> 12.8 us
  waiting for transfers between devices: 107 us -> 117 us
  other arithmetic: 7.06 us -> 2.99 us
    unnamed x113 -> x100, local copies, waits for them, and re-layouts: 15.5 us -> 7.29 us
    pallas_call x3, Pallas kernels: 43.6 us -> 35.7 us  [product(): pl.pallas_call(lambda *refs: product_body(accs, *refs), out_shape=jax.Sha...]
    ppermute x49, waiting for transfers between devices: 66.7 us -> 73.8 us  [move(): return lax.ppermute(x, 'blk', pairs)]
    pallas_call x2, Pallas kernels: 4.81 us -> 1.16 us  [picked(): pl.pallas_call(pick_body, out_shape=jax.ShapeDtypeStruct((1, idx.shape[0]...]
    all_to_all x1, waiting for transfers between devices: 40.2 us -> 43 us  [one_group(): spread = lax.all_to_all(pieces, 'blk', 0, 0, tiled=True).reshape(-1, SUB, W)]
    all_to_all x1 -> x2, blocking collectives: 26 us -> 24 us  [exchanged(): return lax.all_to_all(x, 'blk', 0, 0, axis_index_groups=groups, tiled=True)]
  transfers between devices with their start and end apart: 50 -> 50, of which waited for: 18 -> 21; matrix products, arithmetic and copies ran while one was open for 5% -> 3% of each run, Pallas kernels for 14% -> 12%
where the time goes in v2:
time: 245 us
  waiting for transfers between devices  117 us (48%)
  Pallas kernels  49.1 us (20%)
  starting transfers between devices  37.7 us (15%)
  blocking collectives  24 us (10%)
  local copies, waits for them, and re-layouts  12.8 us (5%)
  other arithmetic  2.99 us (1%)
    ppermute x49, waiting for transfers between devices, move(): return lax.ppermute(x, 'blk', pairs)  73.8 us
    all_to_all x1, waiting for transfers between devices, one_group(): spread = lax.all_to_all(pieces, 'blk', 0, 0, tiled=True).reshape(-1, SUB, W)  43 us
    pallas_call x3, Pallas kernels, product(): pl.pallas_call(lambda *refs: product_body(accs, *refs), out_shape=jax.Sha...  35.7 us
    ppermute x49, starting transfers between devices, move(): return lax.ppermute(x, 'blk', pairs)  30.4 us
    all_to_all x2, blocking collectives, exchanged(): return lax.all_to_all(x, 'blk', 0, 0, axis_index_groups=groups, tiled=True)  24 us
    all_to_all x1, starting transfers between devices, one_group(): spread = lax.all_to_all(pieces, 'blk', 0, 0, tiled=True).reshape(-1, SUB, W)  7.3 us
    unnamed x100, local copies, waits for them, and re-layouts  7.29 us
    pallas_call x2, Pallas kernels, upper(): pl.pallas_call(upper_body, out_shape=out_shape, grid=(1,), in_specs=[pl.B...  6.78 us
  transfers between devices with their start and end apart: 50, of which 21 were waited for; matrix products, arithmetic and copies ran while one was open for 3% of the time, Pallas kernels for 12%

profile of v2, /device:TPU:0, one launch (start us, length us, event | category | flops | bytes accessed | tf_op | source)
XLA Modules:
  0.0 244.9 jit_solution(2010938606879977227)
XLA Ops:
  2.2 1.9 transposed_pieces.1.up_ref.low_ref.refs_3_
  4.1 7.3 %all-to-all-start = ((f32[32,4,2,8,256]{4,3,2,1,0:T(8,128)}), f32[32,4,2,8,256]{4,3,2,1,0:T(8,128)S(1)}, u32[]{:S(2)}, u32[]{:S(2)}) async-start(f32[32,4,2,8,256]{4,3,2,1,0:T(8,128)} %transposed_pieces.1.up_ref.low_ref.refs_3_), calls=%async_computation | async-start | bytes 4194304 | tf_op jit(solution)/shard_map/all_to_all | solution.py:333
  17.4 43.0 %all-to-all-done = f32[32,4,2,8,256]{4,3,2,1,0:T(8,128)S(1)} async-done(((f32[32,4,2,8,256]{4,3,2,1,0:T(8,128)}), f32[32,4,2,8,256]{4,3,2,1,0:T(8,128)S(1)}, u32[]{:S(2)}, u32[]{:S(2)}) %all-to-all-start) | async-done | bytes 2097184 | tf_op jit(solution)/shard_map/all_to_all | solution.py:333
  66.0 11.8 %collective-permute-done.refs_0_ = f32[1,64,8,256]{3,2,1,0:T(8,128)} collective-permute-done((f32[1,64,8,256]{3,2,1,0:T(8,128)S(1)}, f32[1,64,8,256]{3,2,1,0:T(8,128)}, u32[]{:S(2)}, u32[]{:S(2)}) %collective-permute-start) | collective-permute-done | bytes 524320 | tf_op jit(solution)/shard_map/ppermute | solution.py:256
  81.3 11.2 %collective-permute-done.4.refs_0_ = f32[1,64,8,256]{3,2,1,0:T(8,128)S(1)} collective-permute-done((f32[1,64,8,256]{3,2,1,0:T(8,128)}, f32[1,64,8,256]{3,2,1,0:T(8,128)S(1)}, u32[]{:S(2)}, u32[]{:S(2)}) %collective-permute-start.4) | collective-permute-done | bytes 524320 | tf_op jit(solution)/shard_map/ppermute | solution.py:256
  96.7 11.3 %collective-permute-done.10.refs_1_ = f32[1,64,8,256]{3,2,1,0:T(8,128)S(1)} collective-permute-done((f32[1,64,8,256]{3,2,1,0:T(8,128)S(1)}, f32[1,64,8,256]{3,2,1,0:T(8,128)S(1)}, u32[]{:S(2)}, u32[]{:S(2)}) %collective-permute-start.10) | collective-permute-done | bytes 524320 | tf_op jit(solution)/shard_map/ppermute | solution.py:256
  109.5 2.4 collective-permute-done.9.refs_0_
  111.9 5.2 %collective-permute-done.19.refs_4_ = f32[1,32,8,256]{3,2,1,0:T(8,128)S(1)} collective-permute-done((f32[1,32,8,256]{3,2,1,0:T(8,128)S(1)}, f32[1,32,8,256]{3,2,1,0:T(8,128)S(1)}, u32[]{:S(2)}, u32[]{:S(2)}) %collective-permute-start.19) | collective-permute-done | bytes 262176 | tf_op jit(solution)/shard_map/ppermute | solution.py:256
  119.9 2.6 %collective-permute-done.18.refs_3_ = f32[1,64,8,256]{3,2,1,0:T(8,128)S(1)} collective-permute-done((f32[1,64,8,256]{3,2,1,0:T(8,128)S(1)}, f32[1,64,8,256]{3,2,1,0:T(8,128)S(1)}, u32[]{:S(2)}, u32[]{:S(2)}) %collective-permute-start.18) | collective-permute-done | bytes 524320 | tf_op jit(solution)/shard_map/ppermute | solution.py:256
  123.1 6.4 %collective-permute-done.15.refs_0_ = f32[1,64,8,256]{3,2,1,0:T(8,128)S(1)} collective-permute-done((f32[1,64,8,256]{3,2,1,0:T(8,128)S(1)}, f32[1,64,8,256]{3,2,1,0:T(8,128)S(1)}, u32[]{:S(2)}, u32[]{:S(2)}) %collective-permute-start.15) | collective-permute-done | bytes 524320 | tf_op jit(solution)/shard_map/ppermute | solution.py:256
  132.5 2.3 collective-permute-start.27
  134.9 1.8 collective-permute-start.25
  136.7 8.6 %collective-permute-done.27.refs_3_ = f32[1,32,8,256]{3,2,1,0:T(8,128)S(1)} collective-permute-done((f32[1,32,8,256]{3,2,1,0:T(8,128)S(1)}, f32[1,32,8,256]{3,2,1,0:T(8,128)S(1)}, u32[]{:S(2)}, u32[]{:S(2)}) %collective-permute-start.27) | collective-permute-done | bytes 262176 | tf_op jit(solution)/shard_map/ppermute | solution.py:256
  152.0 1.9 collective-permute-start.32
  155.0 11.3 %product.3.zt_ref = f32[1,256,512]{2,1,0:T(8,128)S(1)} custom-call(s32[32]{0:T(128)S(1)} %get-tuple-element.93.refs_0_, f32[16384,512]{1,0:T(8,128)} %refs_8_.5, f32[16384,512]{1,0:T(8,128)} %refs_8_.5, f32[16384,512]{1,0:T(8,128)} %refs_8_.5, f32[16384,512]{1,0:T(8,128)} %refs_8_.5, f32[16384,512]{1,0:T(8,128)} %refs_8_.5, f32[16384,512]{1,0:T(8,128)} %refs_8_.5, ...), custom_call_target="tpu_custom_call" | custom-call | flops 6442450944 | bytes 25165824 | tf_op jit(solution)/shard_map/product/pallas_call | solution.py:119
  166.4 3.4 %upper.2 = (f32[512,256]{1,0:T(8,128)S(1)}, f32[512,256]{1,0:T(8,128)S(1)}, f32[256,256]{1,0:T(8,128)S(1)}, f32[256,256]{1,0:T(8,128)S(1)}, f32[256,256]{1,0:T(8,128)S(1)}) custom-call(s32[5]{0:T(128)S(1)} %get-tuple-element.97.refs_1_.flag_ref, s32[32]{0:T(128)S(1)} %stack.137.refs_10_.pos_ref.refs_1_, f32[1,256,512]{2,1,0:T(8,128)S(1)} %product.3.zt_ref, ...), custom_call_target="tpu_custom_call" | custom-call | flops 1207959552 | bytes 5242880 | tf_op jit(solution)/shard_map/upper/pallas_call | solution.py:181
  169.9 5.4 %collective-permute-done.32.refs_0_ = f32[2,32,8,256]{3,2,1,0:T(8,128)S(1)} collective-permute-done((f32[2,32,8,256]{3,2,1,0:T(8,128)S(1)}, f32[2,32,8,256]{3,2,1,0:T(8,128)S(1)}, u32[]{:S(2)}, u32[]{:S(2)}) %collective-permute-start.32) | collective-permute-done | bytes 524320 | tf_op jit(solution)/shard_map/ppermute | solution.py:256
  179.8 11.1 %product.4.zt_ref = f32[1,256,512]{2,1,0:T(8,128)S(1)} custom-call(s32[32]{0:T(128)S(1)} %get-tuple-element.94.refs_0_, f32[16384,512]{1,0:T(8,128)} %refs_8_.5, f32[16384,512]{1,0:T(8,128)} %refs_8_.5, f32[16384,512]{1,0:T(8,128)} %refs_8_.5, f32[16384,512]{1,0:T(8,128)} %refs_8_.5, f32[16384,512]{1,0:T(8,128)} %refs_8_.5, f32[16384,512]{1,0:T(8,128)} %refs_8_.5, ...), custom_call_target="tpu_custom_call" | custom-call | flops 6442450944 | bytes 25165824 | tf_op jit(solution)/shard_map/product/pallas_call | solution.py:119
  191.0 3.4 %upper.3 = (f32[512,256]{1,0:T(8,128)S(1)}, f32[512,256]{1,0:T(8,128)S(1)}, f32[256,256]{1,0:T(8,128)S(1)}, f32[256,256]{1,0:T(8,128)S(1)}, f32[256,256]{1,0:T(8,128)S(1)}) custom-call(s32[5]{0:T(128)S(1)} %get-tuple-element.98.refs_2_.flag_ref, s32[32]{0:T(128)S(1)} %stack.137.refs_10_.pos_ref.refs_1_, f32[1,256,512]{2,1,0:T(8,128)S(1)} %product.4.zt_ref, ...), custom_call_target="tpu_custom_call" | custom-call | flops 1207959552 | bytes 5242880 | tf_op jit(solution)/shard_map/upper/pallas_call | solution.py:181
  198.8 13.3 %product.5.refs_2_ = f32[2,256,512]{2,1,0:T(8,128)} custom-call(s32[32]{0:T(128)} %copy-done.41, f32[16384,512]{1,0:T(8,128)} %refs_8_.5, f32[16384,512]{1,0:T(8,128)} %refs_8_.5, f32[16384,512]{1,0:T(8,128)} %refs_8_.5, f32[16384,512]{1,0:T(8,128)} %refs_8_.5, f32[16384,512]{1,0:T(8,128)} %refs_8_.5, f32[16384,512]{1,0:T(8,128)} %refs_8_.5, ...), custom_call_target="tpu_custom_call" | custom-call | flops 6442450944 | bytes 25165824 | tf_op jit(solution)/shard_map/product/pallas_call | solution.py:119
  213.3 3.5 %lower.1 = (f32[512,1024]{1,0:T(8,128)}, f32[512,256]{1,0:T(8,128)S(1)}) custom-call(s32[4]{0:T(128)S(1)} %pad_add_fusion.refs_9_.refs_0_, s32[32]{0:T(128)S(1)} %stack.137.refs_10_.pos_ref.refs_1_, f32[2,256,512]{2,1,0:T(8,128)S(1)} %copy-done.13, f32[32,4,2,8,256]{4,3,2,1,0:T(8,128)} %transposed_pieces.1.up_ref.low_ref.refs_3_, f32[512,256]{1,0:T(8,128)S(1)} %copy-done.31, ...), custom_call_target="tpu_custom_call" | custom-call | flops 402653184 | bytes 7864320 | tf_op jit(solution)/shard_map/lower/pallas_call | solution.py:218
  217.6 1.9 collective-permute-done.48
  219.6 14.5 %all_to_all.15 = f32[4,4,48,256]{3,2,1,0:T(8,128)S(1)} all-to-all(f32[4,4,48,256]{3,2,1,0:T(8,128)S(1)} %fusion.2), channel_id=1, replica_groups={{0,2,4,6},{1,3,5,7},{8,10,12,14},{9,11,13,15},{16,18,20,22},{17,19,21,2..., dimensions={0} | all-to-all | bytes 1572864 | tf_op jit(solution)/shard_map/all_to_all | solution.py:296
  234.2 9.4 %all_to_all.16 = f32[4,48,256]{2,1,0:T(8,128)S(1)} all-to-all(f32[4,48,256]{2,1,0:T(8,128)S(1)} %reduce_sum.18), channel_id=1, replica_groups={{0,8,16,24},{1,9,17,25},{2,10,18,26},{3,11,19,27},{4,12,20,28},{5,13,21..., dimensions={0} | all-to-all | bytes 393216 | tf_op jit(solution)/shard_map/all_to_all | solution.py:296
  (229 shorter events, 48.2 us)
Async XLA Ops:
  4.1 56.2 %all-to-all-start = ((f32[32,4,2,8,256]{4,3,2,1,0:T(8,128)}), f32[32,4,2,8,256]{4,3,2,1,0:T(8,128)S(1)}, u32[]{:S(2)}, u32[]{:S(2)}) async-start(f32[32,4,2,8,256]{4,3,2,1,0:T(8,128)} %transposed_pieces.1.up_ref.low_ref.refs_3_), calls=%async_computation | async-start | bytes 4194304 | tf_op jit(solution)/shard_map/all_to_all | solution.py:333
  62.5 15.4 %collective-permute-start = (f32[1,64,8,256]{3,2,1,0:T(8,128)S(1)}, f32[1,64,8,256]{3,2,1,0:T(8,128)}, u32[]{:S(2)}, u32[]{:S(2)}) collective-permute-start(f32[1,64,8,256]{3,2,1,0:T(8,128)S(1)} %sync.8.refs_9_), channel_id=1, source_target_pairs={{0,8},{1,9},{2,10},{3,11},{4,12},{5,13},{6,14},{7,15},{8,16},{9,17... | collective-permute-start | bytes 1572872 | tf_op jit(solution)/shard_map/ppermute | solution.py:256
  62.5 15.4 %collective-permute-start.1 = (f32[1,64,8,256]{3,2,1,0:T(8,128)S(1)}, f32[1,64,8,256]{3,2,1,0:T(8,128)}, u32[]{:S(2)}, u32[]{:S(2)}) collective-permute-start(f32[1,64,8,256]{3,2,1,0:T(8,128)S(1)} %sync.8.refs_9_), channel_id=1, source_target_pairs={{0,2},{1,3},{2,0},{3,1},{4,6},{5,7},{6,4},{7,5},{8,10},{9,11},{10,... | collective-permute-start | bytes 1572872 | tf_op jit(solution)/shard_map/ppermute | solution.py:256
  63.9 14.0 %collective-permute-start.2 = (f32[1,64,8,256]{3,2,1,0:T(8,128)S(1)}, f32[1,64,8,256]{3,2,1,0:T(8,128)}, u32[]{:S(2)}, u32[]{:S(2)}) collective-permute-start(f32[1,64,8,256]{3,2,1,0:T(8,128)S(1)} %sync.8.refs_9_), channel_id=1, source_target_pairs={{0,4},{1,5},{2,6},{3,7},{4,0},{5,1},{6,2},{7,3},{8,12},{9,13},{10,... | collective-permute-start | bytes 1572872 | tf_op jit(solution)/shard_map/ppermute | solution.py:256
  77.9 14.6 %collective-permute-start.4 = (f32[1,64,8,256]{3,2,1,0:T(8,128)}, f32[1,64,8,256]{3,2,1,0:T(8,128)S(1)}, u32[]{:S(2)}, u32[]{:S(2)}) collective-permute-start(f32[1,64,8,256]{3,2,1,0:T(8,128)} %get-tuple-element.41.refs_10_), channel_id=1, source_target_pairs={{0,8},{1,9},{2,10},{3,11},{4,12},{5,13},{6,14},{7,15},{8,16},{9,17... | collective-permute-start | bytes 1572872 | tf_op jit(solution)/shard_map/ppermute | solution.py:256
  78.0 14.6 %collective-permute-start.5 = (f32[1,64,8,256]{3,2,1,0:T(8,128)}, f32[1,64,8,256]{3,2,1,0:T(8,128)S(1)}, u32[]{:S(2)}, u32[]{:S(2)}) collective-permute-start(f32[1,64,8,256]{3,2,1,0:T(8,128)} %get-tuple-element.41.refs_10_), channel_id=1, source_target_pairs={{0,2},{1,3},{2,0},{3,1},{4,6},{5,7},{6,4},{7,5},{8,10},{9,11},{10,... | collective-permute-start | bytes 1572872 | tf_op jit(solution)/shard_map/ppermute | solution.py:256
  93.1 14.9 %collective-permute-start.10 = (f32[1,64,8,256]{3,2,1,0:T(8,128)S(1)}, f32[1,64,8,256]{3,2,1,0:T(8,128)S(1)}, u32[]{:S(2)}, u32[]{:S(2)}) collective-permute-start(f32[1,64,8,256]{3,2,1,0:T(8,128)S(1)} %get-tuple-element.43.refs_11_), channel_id=1, source_target_pairs={{0,2},{1,3},{2,0},{3,1},{4,6},{5,7},{6,4},{7,5},{8,10},{9,11},{10,... | collective-permute-start | bytes 1572872 | tf_op jit(solution)/shard_map/ppermute | solution.py:256
  94.0 14.4 %collective-permute-start.11 = (f32[1,64,8,256]{3,2,1,0:T(8,128)S(1)}, f32[1,64,8,256]{3,2,1,0:T(8,128)S(1)}, u32[]{:S(2)}, u32[]{:S(2)}) collective-permute-start(f32[1,64,8,256]{3,2,1,0:T(8,128)S(1)} %get-tuple-element.43.refs_11_), channel_id=1, source_target_pairs={{0,4},{1,5},{2,6},{3,7},{4,0},{5,1},{6,2},{7,3},{8,12},{9,13},{10,... | collective-permute-start | bytes 1572872 | tf_op jit(solution)/shard_map/ppermute | solution.py:256
  95.4 14.1 %collective-permute-start.12 = (f32[1,64,8,256]{3,2,1,0:T(8,128)S(1)}, f32[1,64,8,256]{3,2,1,0:T(8,128)S(1)}, u32[]{:S(2)}, u32[]{:S(2)}) collective-permute-start(f32[1,64,8,256]{3,2,1,0:T(8,128)S(1)} %get-tuple-element.43.refs_11_), channel_id=1, source_target_pairs={{0,1},{1,0},{2,3},{3,2},{4,5},{5,4},{6,7},{7,6},{8,9},{9,8},{10,11... | collective-permute-start | bytes 1572872 | tf_op jit(solution)/shard_map/ppermute | solution.py:256
  95.4 16.5 %collective-permute-start.9 = (f32[1,64,8,256]{3,2,1,0:T(8,128)S(1)}, f32[1,64,8,256]{3,2,1,0:T(8,128)S(1)}, u32[]{:S(2)}, u32[]{:S(2)}) collective-permute-start(f32[1,64,8,256]{3,2,1,0:T(8,128)S(1)} %get-tuple-element.43.refs_11_), channel_id=1, source_target_pairs={{0,8},{1,9},{2,10},{3,11},{4,12},{5,13},{6,14},{7,15},{8,16},{9,17... | collective-permute-start | bytes 1572872 | tf_op jit(solution)/shard_map/ppermute | solution.py:256
  96.0 22.3 %collective-permute-start.17 = (f32[1,64,8,256]{3,2,1,0:T(8,128)}, f32[1,64,8,256]{3,2,1,0:T(8,128)S(1)}, u32[]{:S(2)}, u32[]{:S(2)}) collective-permute-start(f32[1,64,8,256]{3,2,1,0:T(8,128)} %get-tuple-element.44.refs_17_), channel_id=1, source_target_pairs={{0,2},{1,3},{2,0},{3,1},{4,6},{5,7},{6,4},{7,5},{8,10},{9,11},{10,... | collective-permute-start | bytes 1572872 | tf_op jit(solution)/shard_map/ppermute | solution.py:256
  108.4 14.1 %collective-permute-start.18 = (f32[1,64,8,256]{3,2,1,0:T(8,128)S(1)}, f32[1,64,8,256]{3,2,1,0:T(8,128)S(1)}, u32[]{:S(2)}, u32[]{:S(2)}) collective-permute-start(f32[1,64,8,256]{3,2,1,0:T(8,128)S(1)} %get-tuple-element.47.refs_14_), channel_id=1, source_target_pairs={{0,4},{1,5},{2,6},{3,7},{4,0},{5,1},{6,2},{7,3},{8,12},{9,13},{10,... | collective-permute-start | bytes 1572872 | tf_op jit(solution)/shard_map/ppermute | solution.py:256
  118.3 14.3 %collective-permute-start.16 = (f32[1,64,8,256]{3,2,1,0:T(8,128)S(1)}, f32[1,64,8,256]{3,2,1,0:T(8,128)S(1)}, u32[]{:S(2)}, u32[]{:S(2)}) collective-permute-start(f32[1,64,8,256]{3,2,1,0:T(8,128)S(1)} %get-tuple-element.46.refs_12_), channel_id=1, source_target_pairs={{0,4},{1,5},{2,6},{3,7},{4,0},{5,1},{6,2},{7,3},{8,12},{9,13},{10,... | collective-permute-start | bytes 1572872 | tf_op jit(solution)/shard_map/ppermute | solution.py:256
  129.4 15.9 %collective-permute-start.14 = (f32[1,64,8,256]{3,2,1,0:T(8,128)S(1)}, f32[1,64,8,256]{3,2,1,0:T(8,128)S(1)}, u32[]{:S(2)}, u32[]{:S(2)}) collective-permute-start(f32[1,64,8,256]{3,2,1,0:T(8,128)S(1)} %get-tuple-element.45.refs_19_), channel_id=1, source_target_pairs={{0,2},{1,3},{2,0},{3,1},{4,6},{5,7},{6,4},{7,5},{8,10},{9,11},{10,... | collective-permute-start | bytes 1572872 | tf_op jit(solution)/shard_map/ppermute | solution.py:256
  150.1 19.7 %collective-permute-start.33 = (f32[2,32,8,256]{3,2,1,0:T(8,128)S(1)}, f32[2,32,8,256]{3,2,1,0:T(8,128)S(1)}, u32[]{:S(2)}, u32[]{:S(2)}) collective-permute-start(f32[2,32,8,256]{3,2,1,0:T(8,128)S(1)} %constant_dynamic-update-slice_fusion.refs_4_.refs_10_), channel_id=1, source_target_pairs={{0,2},{1,3},{2,0},{3,1},{4,6},{5,7},{6,4},{7,5},{8,10},{9,11},{10,... | collective-permute-start | bytes 1572872 | tf_op jit(solution)/shard_map/ppermute | solution.py:256
  150.2 19.7 %collective-permute-start.35 = (f32[2,32,8,256]{3,2,1,0:T(8,128)S(1)}, f32[2,32,8,256]{3,2,1,0:T(8,128)S(1)}, u32[]{:S(2)}, u32[]{:S(2)}) collective-permute-start(f32[2,32,8,256]{3,2,1,0:T(8,128)S(1)} %constant_dynamic-update-slice_fusion.refs_4_.refs_10_), channel_id=1, source_target_pairs={{0,4},{1,5},{2,6},{3,7},{4,0},{5,1},{6,2},{7,3},{8,12},{9,13},{10,... | collective-permute-start | bytes 1572872 | tf_op jit(solution)/shard_map/ppermute | solution.py:256
  152.0 23.4 %collective-permute-start.32 = (f32[2,32,8,256]{3,2,1,0:T(8,128)S(1)}, f32[2,32,8,256]{3,2,1,0:T(8,128)S(1)}, u32[]{:S(2)}, u32[]{:S(2)}) collective-permute-start(f32[2,32,8,256]{3,2,1,0:T(8,128)S(1)} %get-tuple-element.56.refs_3_.refs_9_), channel_id=1, source_target_pairs={{0,2},{1,3},{2,0},{3,1},{4,6},{5,7},{6,4},{7,5},{8,10},{9,11},{10,... | collective-permute-start | bytes 1572872 | tf_op jit(solution)/shard_map/ppermute | solution.py:256
  153.9 21.5 %collective-permute-start.34 = (f32[2,32,8,256]{3,2,1,0:T(8,128)S(1)}, f32[2,32,8,256]{3,2,1,0:T(8,128)S(1)}, u32[]{:S(2)}, u32[]{:S(2)}) collective-permute-start(f32[2,32,8,256]{3,2,1,0:T(8,128)S(1)} %get-tuple-element.56.refs_3_.refs_9_), channel_id=1, source_target_pairs={{0,4},{1,5},{2,6},{3,7},{4,0},{5,1},{6,2},{7,3},{8,12},{9,13},{10,... | collective-permute-start | bytes 1572872 | tf_op jit(solution)/shard_map/ppermute | solution.py:256
  154.2 23.5 %collective-permute-start.39 = (f32[2,32,8,256]{3,2,1,0:T(8,128)S(1)}, f32[2,32,8,256]{3,2,1,0:T(8,128)S(1)}, u32[]{:S(2)}, u32[]{:S(2)}) collective-permute-start(f32[2,32,8,256]{3,2,1,0:T(8,128)S(1)} %constant_dynamic-update-slice_fusion.refs_4_.refs_10_), channel_id=1, source_target_pairs={{0,1},{1,0},{2,3},{3,2},{4,5},{5,4},{6,7},{7,6},{8,9},{9,8},{10,11... | collective-permute-start | bytes 1572872 | tf_op jit(solution)/shard_map/ppermute | solution.py:256
  175.5 18.9 %collective-permute-start.42 = (f32[2,32,8,256]{3,2,1,0:T(8,128)S(1)}, f32[2,32,8,256]{3,2,1,0:T(8,128)S(1)}, u32[]{:S(2)}, u32[]{:S(2)}) collective-permute-start(f32[2,32,8,256]{3,2,1,0:T(8,128)S(1)} %get-tuple-element.64.refs_7_.refs_13_), channel_id=1, source_target_pairs={{0,1},{1,0},{2,3},{3,2},{4,5},{5,4},{6,7},{7,6},{8,9},{9,8},{10,11... | collective-permute-start | bytes 1572872 | tf_op jit(solution)/shard_map/ppermute | solution.py:256
  176.0 18.5 %collective-permute-start.44 = (f32[2,32,8,256]{3,2,1,0:T(8,128)S(1)}, f32[2,32,8,256]{3,2,1,0:T(8,128)}, u32[]{:S(2)}, u32[]{:S(2)}) collective-permute-start(f32[2,32,8,256]{3,2,1,0:T(8,128)S(1)} %get-tuple-element.64.refs_7_.refs_13_), channel_id=1, source_target_pairs={{0,2},{1,3},{2,0},{3,1},{4,6},{5,7},{6,4},{7,5},{8,10},{9,11},{10,... | collective-permute-start | bytes 1572872 | tf_op jit(solution)/shard_map/ppermute | solution.py:256
  177.7 16.7 %collective-permute-start.41 = (f32[2,32,8,256]{3,2,1,0:T(8,128)S(1)}, f32[2,32,8,256]{3,2,1,0:T(8,128)S(1)}, u32[]{:S(2)}, u32[]{:S(2)}) collective-permute-start(f32[2,32,8,256]{3,2,1,0:T(8,128)S(1)} %get-tuple-element.63.refs_6_.refs_12_), channel_id=1, source_target_pairs={{0,1},{1,0},{2,3},{3,2},{4,5},{5,4},{6,7},{7,6},{8,9},{9,8},{10,11... | collective-permute-start | bytes 1572872 | tf_op jit(solution)/shard_map/ppermute | solution.py:256
  177.7 16.8 %collective-permute-start.45 = (f32[2,32,8,256]{3,2,1,0:T(8,128)S(1)}, f32[2,32,8,256]{3,2,1,0:T(8,128)}, u32[]{:S(2)}, u32[]{:S(2)}) collective-permute-start(f32[2,32,8,256]{3,2,1,0:T(8,128)S(1)} %get-tuple-element.63.refs_6_.refs_12_), channel_id=1, source_target_pairs={{0,4},{1,5},{2,6},{3,7},{4,0},{5,1},{6,2},{7,3},{8,12},{9,13},{10,... | collective-permute-start | bytes 1572872 | tf_op jit(solution)/shard_map/ppermute | solution.py:256
  179.6 14.9 %collective-permute-start.43 = (f32[2,32,8,256]{3,2,1,0:T(8,128)S(1)}, f32[2,32,8,256]{3,2,1,0:T(8,128)S(1)}, u32[]{:S(2)}, u32[]{:S(2)}) collective-permute-start(f32[2,32,8,256]{3,2,1,0:T(8,128)S(1)} %get-tuple-element.65.refs_8_.refs_14_), channel_id=1, source_target_pairs={{0,1},{1,0},{2,3},{3,2},{4,5},{5,4},{6,7},{7,6},{8,9},{9,8},{10,11... | collective-permute-start | bytes 1572872 | tf_op jit(solution)/shard_map/ppermute | solution.py:256
  (75 other events, 756.1 us)

commit v3 on v2

--- a/solution.py
+++ b/solution.py
@@ -19,7 +19,7 @@
 PIECES = CHIPS_Z * CHIPS_Y * CHIPS_X * CORES
 SUB = NODE_WIDTH // PIECES
 SLOTS = 32
-PER_STEP = 8
+PER_STEP = 4
 W = NODE_WIDTH
 
 
@@ -104,7 +104,7 @@
         o_ref[0] += value
 
 
-def product(idx, sigma, pieces, accs, chunk=0, mib=40):
+def product(idx, sigma, pieces, accs, chunk=0, mib=18):
     steps = SLOTS // PER_STEP
     cols = sigma.shape[1]
     rows = SUB * sum(p.shape[0] for p in pieces)
@@ -247,6 +247,8 @@
 
 ALONG_Z = moves(lambda z, y, x, c: ((z + 1) % CHIPS_Z, y, x, c))
 AGAINST_Z = moves(lambda z, y, x, c: ((z - 1) % CHIPS_Z, y, x, c))
+DIAGONAL = moves(lambda z, y, x, c: (z, 1 - y, 1 - x, c))
+Z_BY = [moves(lambda z, y, x, c, s=s: ((z + s) % CHIPS_Z, y, x, c)) for s in range(CHIPS_Z)]
 ALONG_Y = moves(lambda z, y, x, c: (z, 1 - y, x, c))
 ALONG_X = moves(lambda z, y, x, c: (z, y, 1 - x, c))
 ALONG_C = moves(lambda z, y, x, c: (z, y, x, 1 - c))
@@ -292,21 +294,23 @@
     return jnp.stack(near[0] + near[1] + corner[0] + corner[1]).astype(jnp.int32)
 
 
-def exchanged(x, groups):
-    return lax.all_to_all(x, "blk", 0, 0, axis_index_groups=groups, tiled=True)
-
-
 def summed(me, share):
-    core = me % CORES
-    kept = lax.dynamic_index_in_dim(share, core, 2, keepdims=False)
-    sent = lax.dynamic_index_in_dim(share, 1 - core, 2, keepdims=False)
-    plane = [device_at(0, y, x, 0) for y in range(CHIPS_Y) for x in range(CHIPS_X)]
-    column = [device_at(z, 0, 0, 0) for z in range(CHIPS_Z)]
-    total = kept + move(sent, ALONG_C)
-    total = exchanged(total, [[p + q + c for p in plane] for q in column for c in range(CORES)])
-    total = jnp.sum(total, axis=0)
-    total = exchanged(total, [[p + q + c for q in column] for p in plane for c in range(CORES)])
-    return jnp.sum(total, axis=0)
+    core, place, z = me % CORES, me // CORES % (CHIPS_Y * CHIPS_X), me // device_at(1, 0, 0, 0)
+
+    def rows(x, at, dim=0):
+        return lax.dynamic_index_in_dim(x, at, dim, keepdims=False)
+
+    share = rows(share, core, 2) + move(rows(share, 1 - core, 2), ALONG_C)
+    share = (
+        rows(share, place)
+        + move(rows(share, place ^ 1), ALONG_X)
+        + move(rows(share, place ^ CHIPS_X), ALONG_Y)
+        + move(rows(share, place ^ (1 + CHIPS_X)), DIAGONAL)
+    )
+    total = rows(share, z)
+    for step in range(1, CHIPS_Z):
+        total += move(rows(share, (z + step) % CHIPS_Z), Z_BY[step])
+    return total
 
 
 def one_group(sigma_anc, panels, diag_inv, scaled_parent_panel, struct_upper, struct_lower):

time: 245 us -> 243 us (level)
  blocking collectives: 24 us -> 0 us
  waiting for transfers between devices: 117 us -> 129 us
  starting transfers between devices: 37.7 us -> 45.8 us
  Pallas kernels: 49.1 us -> 53.1 us
    all_to_all x2 -> x0, blocking collectives: 24 us -> none  [exchanged(): return lax.all_to_all(x, 'blk', 0, 0, axis_index_groups=groups, tiled=True)]
    ppermute x49 -> x55, waiting for transfers between devices: 73.8 us -> 85.7 us  [move(): return lax.ppermute(x, 'blk', pairs)]
    ppermute x49 -> x55, starting transfers between devices: 30.4 us -> 38.5 us  [move(): return lax.ppermute(x, 'blk', pairs)]
    pallas_call x3, Pallas kernels: 35.7 us -> 39.7 us  [product(): pl.pallas_call(lambda *refs: product_body(accs, *refs), out_shape=jax.Sha...]
    unnamed x100 -> x79, local copies, waits for them, and re-layouts: 7.29 us -> 5.43 us
  transfers between devices with their start and end apart: 50 -> 56, of which waited for: 21 -> 26; matrix products, arithmetic and copies ran while one was open for 3% -> 2% of each run, Pallas kernels for 12% -> 13%
where the time goes in v3:
time: 243 us; the launch traced here: 242 us
  waiting for transfers between devices  129 us (53%)
  Pallas kernels  53.1 us (22%)
  starting transfers between devices  45.8 us (19%)
  local copies, waits for them, and re-layouts  11 us (5%)
    ppermute x55, waiting for transfers between devices, move(): return lax.ppermute(x, 'blk', pairs)  85.7 us
    all_to_all x1, waiting for transfers between devices, one_group(): spread = lax.all_to_all(pieces, 'blk', 0, 0, tiled=True).reshape(-1, SUB, W)  43 us
    pallas_call x3, Pallas kernels, product(): pl.pallas_call(lambda *refs: product_body(accs, *refs), out_shape=jax.Sha...  39.7 us
    ppermute x55, starting transfers between devices, move(): return lax.ppermute(x, 'blk', pairs)  38.5 us
    all_to_all x1, starting transfers between devices, one_group(): spread = lax.all_to_all(pieces, 'blk', 0, 0, tiled=True).reshape(-1, SUB, W)  7.3 us
    pallas_call x2, Pallas kernels, upper(): pl.pallas_call(upper_body, out_shape=out_shape, grid=(1,), in_specs=[pl.B...  6.78 us
    unnamed x79, local copies, waits for them, and re-layouts  5.43 us
  transfers between devices with their start and end apart: 56, of which 26 were waited for; matrix products, arithmetic and copies ran while one was open for 2% of the time, Pallas kernels for 13%

profile of v3, /device:TPU:0, one launch (start us, length us, event | category | flops | bytes accessed | tf_op | source)
XLA Modules:
  0.0 242.0 jit_solution(1926753952960219315)
XLA Ops:
  4.1 7.3 %all-to-all-start = ((f32[32,4,2,8,256]{4,3,2,1,0:T(8,128)}), f32[32,4,2,8,256]{4,3,2,1,0:T(8,128)S(1)}, u32[]{:S(2)}, u32[]{:S(2)}) async-start(f32[32,4,2,8,256]{4,3,2,1,0:T(8,128)} %transposed_pieces.1.up_ref.low_ref.refs_3_), calls=%async_computation | async-start | bytes 4194304 | tf_op jit(solution)/shard_map/all_to_all | solution.py:337
  17.4 43.0 %all-to-all-done = f32[32,4,2,8,256]{4,3,2,1,0:T(8,128)S(1)} async-done(((f32[32,4,2,8,256]{4,3,2,1,0:T(8,128)}), f32[32,4,2,8,256]{4,3,2,1,0:T(8,128)S(1)}, u32[]{:S(2)}, u32[]{:S(2)}) %all-to-all-start) | async-done | bytes 2097184 | tf_op jit(solution)/shard_map/all_to_all | solution.py:337
  66.0 11.8 %collective-permute-done.refs_0_ = f32[1,64,8,256]{3,2,1,0:T(8,128)} collective-permute-done((f32[1,64,8,256]{3,2,1,0:T(8,128)S(1)}, f32[1,64,8,256]{3,2,1,0:T(8,128)}, u32[]{:S(2)}, u32[]{:S(2)}) %collective-permute-start) | collective-permute-done | bytes 524320 | tf_op jit(solution)/shard_map/ppermute | solution.py:258
  81.3 11.2 %collective-permute-done.4.refs_0_ = f32[1,64,8,256]{3,2,1,0:T(8,128)S(1)} collective-permute-done((f32[1,64,8,256]{3,2,1,0:T(8,128)}, f32[1,64,8,256]{3,2,1,0:T(8,128)S(1)}, u32[]{:S(2)}, u32[]{:S(2)}) %collective-permute-start.4) | collective-permute-done | bytes 524320 | tf_op jit(solution)/shard_map/ppermute | solution.py:258
  96.7 11.3 %collective-permute-done.10.refs_1_ = f32[1,64,8,256]{3,2,1,0:T(8,128)S(1)} collective-permute-done((f32[1,64,8,256]{3,2,1,0:T(8,128)S(1)}, f32[1,64,8,256]{3,2,1,0:T(8,128)S(1)}, u32[]{:S(2)}, u32[]{:S(2)}) %collective-permute-start.10) | collective-permute-done | bytes 524320 | tf_op jit(solution)/shard_map/ppermute | solution.py:258
  109.5 2.4 %collective-permute-done.9.refs_0_ = f32[1,64,8,256]{3,2,1,0:T(8,128)S(1)} collective-permute-done((f32[1,64,8,256]{3,2,1,0:T(8,128)S(1)}, f32[1,64,8,256]{3,2,1,0:T(8,128)S(1)}, u32[]{:S(2)}, u32[]{:S(2)}) %collective-permute-start.9) | collective-permute-done | bytes 524320 | tf_op jit(solution)/shard_map/ppermute | solution.py:258
  112.0 5.2 %collective-permute-done.19.refs_4_ = f32[1,32,8,256]{3,2,1,0:T(8,128)S(1)} collective-permute-done((f32[1,32,8,256]{3,2,1,0:T(8,128)S(1)}, f32[1,32,8,256]{3,2,1,0:T(8,128)S(1)}, u32[]{:S(2)}, u32[]{:S(2)}) %collective-permute-start.19) | collective-permute-done | bytes 262176 | tf_op jit(solution)/shard_map/ppermute | solution.py:258
  119.9 2.6 %collective-permute-done.18.refs_3_ = f32[1,64,8,256]{3,2,1,0:T(8,128)S(1)} collective-permute-done((f32[1,64,8,256]{3,2,1,0:T(8,128)S(1)}, f32[1,64,8,256]{3,2,1,0:T(8,128)S(1)}, u32[]{:S(2)}, u32[]{:S(2)}) %collective-permute-start.18) | collective-permute-done | bytes 524320 | tf_op jit(solution)/shard_map/ppermute | solution.py:258
  123.1 6.4 %collective-permute-done.15.refs_0_ = f32[1,64,8,256]{3,2,1,0:T(8,128)S(1)} collective-permute-done((f32[1,64,8,256]{3,2,1,0:T(8,128)S(1)}, f32[1,64,8,256]{3,2,1,0:T(8,128)S(1)}, u32[]{:S(2)}, u32[]{:S(2)}) %collective-permute-start.15) | collective-permute-done | bytes 524320 | tf_op jit(solution)/shard_map/ppermute | solution.py:258
  132.5 2.3 collective-permute-start.27
  136.9 8.4 %collective-permute-done.27.refs_3_ = f32[1,32,8,256]{3,2,1,0:T(8,128)S(1)} collective-permute-done((f32[1,32,8,256]{3,2,1,0:T(8,128)S(1)}, f32[1,32,8,256]{3,2,1,0:T(8,128)S(1)}, u32[]{:S(2)}, u32[]{:S(2)}) %collective-permute-start.27) | collective-permute-done | bytes 262176 | tf_op jit(solution)/shard_map/ppermute | solution.py:258
  151.2 1.9 collective-permute-start.32
  153.4 12.5 %product.3.zt_ref = f32[1,256,512]{2,1,0:T(8,128)S(1)} custom-call(s32[32]{0:T(128)S(1)} %get-tuple-element.97.refs_0_, f32[16384,512]{1,0:T(8,128)} %refs_4_.5, f32[16384,512]{1,0:T(8,128)} %refs_4_.5, f32[16384,512]{1,0:T(8,128)} %refs_4_.5, f32[16384,512]{1,0:T(8,128)} %refs_4_.5, f32[1,64,8,256]{3,2,1,0:T(8,128)S(1)} %sync.8.refs_5_, ...), custom_call_target="tpu_custom_call" | custom-call | flops 6442450944 | bytes 25165824 | tf_op jit(solution)/shard_map/product/pallas_call | solution.py:119
  165.9 3.4 %upper.2 = (f32[512,256]{1,0:T(8,128)S(1)}, f32[512,256]{1,0:T(8,128)S(1)}, f32[256,256]{1,0:T(8,128)S(1)}, f32[256,256]{1,0:T(8,128)S(1)}, f32[256,256]{1,0:T(8,128)S(1)}) custom-call(s32[5]{0:T(128)S(1)} %get-tuple-element.101.refs_1_.flag_ref, s32[32]{0:T(128)S(1)} %stack.137.refs_10_.pos_ref.refs_1_, f32[1,256,512]{2,1,0:T(8,128)S(1)} %product.3.zt_ref, ...), custom_call_target="tpu_custom_call" | custom-call | flops 1207959552 | bytes 5242880 | tf_op jit(solution)/shard_map/upper/pallas_call | solution.py:181
  170.0 4.6 %collective-permute-done.32.refs_0_ = f32[2,32,8,256]{3,2,1,0:T(8,128)S(1)} collective-permute-done((f32[2,32,8,256]{3,2,1,0:T(8,128)S(1)}, f32[2,32,8,256]{3,2,1,0:T(8,128)S(1)}, u32[]{:S(2)}, u32[]{:S(2)}) %collective-permute-start.32) | collective-permute-done | bytes 524320 | tf_op jit(solution)/shard_map/ppermute | solution.py:258
  179.0 12.5 %product.4.zt_ref = f32[1,256,512]{2,1,0:T(8,128)S(1)} custom-call(s32[32]{0:T(128)S(1)} %get-tuple-element.98.refs_0_, f32[16384,512]{1,0:T(8,128)} %refs_4_.5, f32[16384,512]{1,0:T(8,128)} %refs_4_.5, f32[16384,512]{1,0:T(8,128)} %refs_4_.5, f32[16384,512]{1,0:T(8,128)} %refs_4_.5, f32[1,64,8,256]{3,2,1,0:T(8,128)S(1)} %sync.8.refs_5_, ...), custom_call_target="tpu_custom_call" | custom-call | flops 6442450944 | bytes 25165824 | tf_op jit(solution)/shard_map/product/pallas_call | solution.py:119
  191.6 3.4 %upper.3 = (f32[512,256]{1,0:T(8,128)S(1)}, f32[512,256]{1,0:T(8,128)S(1)}, f32[256,256]{1,0:T(8,128)S(1)}, f32[256,256]{1,0:T(8,128)S(1)}, f32[256,256]{1,0:T(8,128)S(1)}) custom-call(s32[5]{0:T(128)S(1)} %get-tuple-element.102.refs_2_.flag_ref, s32[32]{0:T(128)S(1)} %stack.137.refs_10_.pos_ref.refs_1_, f32[1,256,512]{2,1,0:T(8,128)S(1)} %product.4.zt_ref, ...), custom_call_target="tpu_custom_call" | custom-call | flops 1207959552 | bytes 5242880 | tf_op jit(solution)/shard_map/upper/pallas_call | solution.py:181
  199.1 14.7 %product.5.refs_2_ = f32[2,256,512]{2,1,0:T(8,128)} custom-call(s32[32]{0:T(128)} %copy-done.34, f32[16384,512]{1,0:T(8,128)} %refs_4_.5, f32[16384,512]{1,0:T(8,128)} %refs_4_.5, f32[16384,512]{1,0:T(8,128)} %refs_4_.5, f32[16384,512]{1,0:T(8,128)} %refs_4_.5, f32[2,32,8,256]{3,2,1,0:T(8,128)} %copy-done, f32[2,32,8,256]{3,2,1,0:T(8,128)} %copy-done.10, ...), custom_call_target="tpu_custom_call" | custom-call | flops 6442450944 | bytes 25165824 | tf_op jit(solution)/shard_map/product/pallas_call | solution.py:119
  215.0 3.5 %lower.1 = (f32[512,1024]{1,0:T(8,128)}, f32[512,256]{1,0:T(8,128)S(1)}) custom-call(s32[4]{0:T(128)S(1)} %pad_add_fusion.refs_9_.refs_0_, s32[32]{0:T(128)S(1)} %stack.137.refs_10_.pos_ref.refs_1_, f32[2,256,512]{2,1,0:T(8,128)S(1)} %copy-done.9, f32[32,4,2,8,256]{4,3,2,1,0:T(8,128)} %transposed_pieces.1.up_ref.low_ref.refs_3_, f32[512,256]{1,0:T(8,128)S(1)} %copy-done.27, ...), custom_call_target="tpu_custom_call" | custom-call | flops 402653184 | bytes 7864320 | tf_op jit(solution)/shard_map/lower/pallas_call | solution.py:218
  222.6 2.2 collective-permute-start.51
  224.8 4.2 %collective-permute-done.49 = f32[4,48,256]{2,1,0:T(8,128)S(1)} collective-permute-done((f32[4,48,256]{2,1,0:T(8,128)S(1)}, f32[4,48,256]{2,1,0:T(8,128)S(1)}, u32[]{:S(2)}, u32[]{:S(2)}) %collective-permute-start.49) | collective-permute-done | bytes 196640 | tf_op jit(solution)/shard_map/ppermute | solution.py:258
  229.1 3.7 %collective-permute-done.50 = f32[4,48,256]{2,1,0:T(8,128)S(1)} collective-permute-done((f32[4,48,256]{2,1,0:T(8,128)S(1)}, f32[4,48,256]{2,1,0:T(8,128)S(1)}, u32[]{:S(2)}, u32[]{:S(2)}) %collective-permute-start.50) | collective-permute-done | bytes 196640 | tf_op jit(solution)/shard_map/ppermute | solution.py:258
  234.1 2.2 collective-permute-start.53
  236.8 2.2 collective-permute-done.52
  (220 shorter events, 57.5 us)
Async XLA Ops:
  4.1 56.2 %all-to-all-start = ((f32[32,4,2,8,256]{4,3,2,1,0:T(8,128)}), f32[32,4,2,8,256]{4,3,2,1,0:T(8,128)S(1)}, u32[]{:S(2)}, u32[]{:S(2)}) async-start(f32[32,4,2,8,256]{4,3,2,1,0:T(8,128)} %transposed_pieces.1.up_ref.low_ref.refs_3_), calls=%async_computation | async-start | bytes 4194304 | tf_op jit(solution)/shard_map/all_to_all | solution.py:337
  62.5 15.4 %collective-permute-start = (f32[1,64,8,256]{3,2,1,0:T(8,128)S(1)}, f32[1,64,8,256]{3,2,1,0:T(8,128)}, u32[]{:S(2)}, u32[]{:S(2)}) collective-permute-start(f32[1,64,8,256]{3,2,1,0:T(8,128)S(1)} %sync.8.refs_5_), channel_id=1, source_target_pairs={{0,8},{1,9},{2,10},{3,11},{4,12},{5,13},{6,14},{7,15},{8,16},{9,17... | collective-permute-start | bytes 1572872 | tf_op jit(solution)/shard_map/ppermute | solution.py:258
  62.5 15.4 %collective-permute-start.1 = (f32[1,64,8,256]{3,2,1,0:T(8,128)S(1)}, f32[1,64,8,256]{3,2,1,0:T(8,128)}, u32[]{:S(2)}, u32[]{:S(2)}) collective-permute-start(f32[1,64,8,256]{3,2,1,0:T(8,128)S(1)} %sync.8.refs_5_), channel_id=1, source_target_pairs={{0,2},{1,3},{2,0},{3,1},{4,6},{5,7},{6,4},{7,5},{8,10},{9,11},{10,... | collective-permute-start | bytes 1572872 | tf_op jit(solution)/shard_map/ppermute | solution.py:258
  63.9 14.0 %collective-permute-start.2 = (f32[1,64,8,256]{3,2,1,0:T(8,128)S(1)}, f32[1,64,8,256]{3,2,1,0:T(8,128)}, u32[]{:S(2)}, u32[]{:S(2)}) collective-permute-start(f32[1,64,8,256]{3,2,1,0:T(8,128)S(1)} %sync.8.refs_5_), channel_id=1, source_target_pairs={{0,4},{1,5},{2,6},{3,7},{4,0},{5,1},{6,2},{7,3},{8,12},{9,13},{10,... | collective-permute-start | bytes 1572872 | tf_op jit(solution)/shard_map/ppermute | solution.py:258
  77.9 14.6 %collective-permute-start.4 = (f32[1,64,8,256]{3,2,1,0:T(8,128)}, f32[1,64,8,256]{3,2,1,0:T(8,128)S(1)}, u32[]{:S(2)}, u32[]{:S(2)}) collective-permute-start(f32[1,64,8,256]{3,2,1,0:T(8,128)} %get-tuple-element.41.refs_6_), channel_id=1, source_target_pairs={{0,8},{1,9},{2,10},{3,11},{4,12},{5,13},{6,14},{7,15},{8,16},{9,17... | collective-permute-start | bytes 1572872 | tf_op jit(solution)/shard_map/ppermute | solution.py:258
  78.0 14.6 %collective-permute-start.5 = (f32[1,64,8,256]{3,2,1,0:T(8,128)}, f32[1,64,8,256]{3,2,1,0:T(8,128)S(1)}, u32[]{:S(2)}, u32[]{:S(2)}) collective-permute-start(f32[1,64,8,256]{3,2,1,0:T(8,128)} %get-tuple-element.41.refs_6_), channel_id=1, source_target_pairs={{0,2},{1,3},{2,0},{3,1},{4,6},{5,7},{6,4},{7,5},{8,10},{9,11},{10,... | collective-permute-start | bytes 1572872 | tf_op jit(solution)/shard_map/ppermute | solution.py:258
  93.1 14.9 %collective-permute-start.10 = (f32[1,64,8,256]{3,2,1,0:T(8,128)S(1)}, f32[1,64,8,256]{3,2,1,0:T(8,128)S(1)}, u32[]{:S(2)}, u32[]{:S(2)}) collective-permute-start(f32[1,64,8,256]{3,2,1,0:T(8,128)S(1)} %get-tuple-element.43.refs_7_), channel_id=1, source_target_pairs={{0,2},{1,3},{2,0},{3,1},{4,6},{5,7},{6,4},{7,5},{8,10},{9,11},{10,... | collective-permute-start | bytes 1572872 | tf_op jit(solution)/shard_map/ppermute | solution.py:258
  94.0 14.4 %collective-permute-start.11 = (f32[1,64,8,256]{3,2,1,0:T(8,128)S(1)}, f32[1,64,8,256]{3,2,1,0:T(8,128)S(1)}, u32[]{:S(2)}, u32[]{:S(2)}) collective-permute-start(f32[1,64,8,256]{3,2,1,0:T(8,128)S(1)} %get-tuple-element.43.refs_7_), channel_id=1, source_target_pairs={{0,4},{1,5},{2,6},{3,7},{4,0},{5,1},{6,2},{7,3},{8,12},{9,13},{10,... | collective-permute-start | bytes 1572872 | tf_op jit(solution)/shard_map/ppermute | solution.py:258
  95.4 14.1 %collective-permute-start.12 = (f32[1,64,8,256]{3,2,1,0:T(8,128)S(1)}, f32[1,64,8,256]{3,2,1,0:T(8,128)S(1)}, u32[]{:S(2)}, u32[]{:S(2)}) collective-permute-start(f32[1,64,8,256]{3,2,1,0:T(8,128)S(1)} %get-tuple-element.43.refs_7_), channel_id=1, source_target_pairs={{0,1},{1,0},{2,3},{3,2},{4,5},{5,4},{6,7},{7,6},{8,9},{9,8},{10,11... | collective-permute-start | bytes 1572872 | tf_op jit(solution)/shard_map/ppermute | solution.py:258
  95.4 16.5 %collective-permute-start.9 = (f32[1,64,8,256]{3,2,1,0:T(8,128)S(1)}, f32[1,64,8,256]{3,2,1,0:T(8,128)S(1)}, u32[]{:S(2)}, u32[]{:S(2)}) collective-permute-start(f32[1,64,8,256]{3,2,1,0:T(8,128)S(1)} %get-tuple-element.43.refs_7_), channel_id=1, source_target_pairs={{0,8},{1,9},{2,10},{3,11},{4,12},{5,13},{6,14},{7,15},{8,16},{9,17... | collective-permute-start | bytes 1572872 | tf_op jit(solution)/shard_map/ppermute | solution.py:258
  96.0 22.3 %collective-permute-start.17 = (f32[1,64,8,256]{3,2,1,0:T(8,128)}, f32[1,64,8,256]{3,2,1,0:T(8,128)S(1)}, u32[]{:S(2)}, u32[]{:S(2)}) collective-permute-start(f32[1,64,8,256]{3,2,1,0:T(8,128)} %get-tuple-element.44.refs_13_), channel_id=1, source_target_pairs={{0,2},{1,3},{2,0},{3,1},{4,6},{5,7},{6,4},{7,5},{8,10},{9,11},{10,... | collective-permute-start | bytes 1572872 | tf_op jit(solution)/shard_map/ppermute | solution.py:258
  108.4 14.1 %collective-permute-start.18 = (f32[1,64,8,256]{3,2,1,0:T(8,128)S(1)}, f32[1,64,8,256]{3,2,1,0:T(8,128)S(1)}, u32[]{:S(2)}, u32[]{:S(2)}) collective-permute-start(f32[1,64,8,256]{3,2,1,0:T(8,128)S(1)} %get-tuple-element.47.refs_10_), channel_id=1, source_target_pairs={{0,4},{1,5},{2,6},{3,7},{4,0},{5,1},{6,2},{7,3},{8,12},{9,13},{10,... | collective-permute-start | bytes 1572872 | tf_op jit(solution)/shard_map/ppermute | solution.py:258
  118.3 14.3 %collective-permute-start.16 = (f32[1,64,8,256]{3,2,1,0:T(8,128)S(1)}, f32[1,64,8,256]{3,2,1,0:T(8,128)S(1)}, u32[]{:S(2)}, u32[]{:S(2)}) collective-permute-start(f32[1,64,8,256]{3,2,1,0:T(8,128)S(1)} %get-tuple-element.46.refs_8_), channel_id=1, source_target_pairs={{0,4},{1,5},{2,6},{3,7},{4,0},{5,1},{6,2},{7,3},{8,12},{9,13},{10,... | collective-permute-start | bytes 1572872 | tf_op jit(solution)/shard_map/ppermute | solution.py:258
  129.4 15.9 %collective-permute-start.14 = (f32[1,64,8,256]{3,2,1,0:T(8,128)S(1)}, f32[1,64,8,256]{3,2,1,0:T(8,128)S(1)}, u32[]{:S(2)}, u32[]{:S(2)}) collective-permute-start(f32[1,64,8,256]{3,2,1,0:T(8,128)S(1)} %get-tuple-element.45.refs_15_), channel_id=1, source_target_pairs={{0,2},{1,3},{2,0},{3,1},{4,6},{5,7},{6,4},{7,5},{8,10},{9,11},{10,... | collective-permute-start | bytes 1572872 | tf_op jit(solution)/shard_map/ppermute | solution.py:258
  149.3 20.1 %collective-permute-start.33 = (f32[2,32,8,256]{3,2,1,0:T(8,128)S(1)}, f32[2,32,8,256]{3,2,1,0:T(8,128)S(1)}, u32[]{:S(2)}, u32[]{:S(2)}) collective-permute-start(f32[2,32,8,256]{3,2,1,0:T(8,128)S(1)} %constant_dynamic-update-slice_fusion.refs_4_.refs_6_), channel_id=1, source_target_pairs={{0,2},{1,3},{2,0},{3,1},{4,6},{5,7},{6,4},{7,5},{8,10},{9,11},{10,... | collective-permute-start | bytes 1572872 | tf_op jit(solution)/shard_map/ppermute | solution.py:258
  149.4 20.5 %collective-permute-start.35 = (f32[2,32,8,256]{3,2,1,0:T(8,128)S(1)}, f32[2,32,8,256]{3,2,1,0:T(8,128)S(1)}, u32[]{:S(2)}, u32[]{:S(2)}) collective-permute-start(f32[2,32,8,256]{3,2,1,0:T(8,128)S(1)} %constant_dynamic-update-slice_fusion.refs_4_.refs_6_), channel_id=1, source_target_pairs={{0,4},{1,5},{2,6},{3,7},{4,0},{5,1},{6,2},{7,3},{8,12},{9,13},{10,... | collective-permute-start | bytes 1572872 | tf_op jit(solution)/shard_map/ppermute | solution.py:258
  151.2 23.4 %collective-permute-start.32 = (f32[2,32,8,256]{3,2,1,0:T(8,128)S(1)}, f32[2,32,8,256]{3,2,1,0:T(8,128)S(1)}, u32[]{:S(2)}, u32[]{:S(2)}) collective-permute-start(f32[2,32,8,256]{3,2,1,0:T(8,128)S(1)} %get-tuple-element.56.refs_3_.refs_5_), channel_id=1, source_target_pairs={{0,2},{1,3},{2,0},{3,1},{4,6},{5,7},{6,4},{7,5},{8,10},{9,11},{10,... | collective-permute-start | bytes 1572872 | tf_op jit(solution)/shard_map/ppermute | solution.py:258
  153.1 21.5 %collective-permute-start.34 = (f32[2,32,8,256]{3,2,1,0:T(8,128)S(1)}, f32[2,32,8,256]{3,2,1,0:T(8,128)S(1)}, u32[]{:S(2)}, u32[]{:S(2)}) collective-permute-start(f32[2,32,8,256]{3,2,1,0:T(8,128)S(1)} %get-tuple-element.56.refs_3_.refs_5_), channel_id=1, source_target_pairs={{0,4},{1,5},{2,6},{3,7},{4,0},{5,1},{6,2},{7,3},{8,12},{9,13},{10,... | collective-permute-start | bytes 1572872 | tf_op jit(solution)/shard_map/ppermute | solution.py:258
  153.4 23.5 %collective-permute-start.39 = (f32[2,32,8,256]{3,2,1,0:T(8,128)S(1)}, f32[2,32,8,256]{3,2,1,0:T(8,128)S(1)}, u32[]{:S(2)}, u32[]{:S(2)}) collective-permute-start(f32[2,32,8,256]{3,2,1,0:T(8,128)S(1)} %constant_dynamic-update-slice_fusion.refs_4_.refs_6_), channel_id=1, source_target_pairs={{0,1},{1,0},{2,3},{3,2},{4,5},{5,4},{6,7},{7,6},{8,9},{9,8},{10,11... | collective-permute-start | bytes 1572872 | tf_op jit(solution)/shard_map/ppermute | solution.py:258
  174.7 20.3 %collective-permute-start.42 = (f32[2,32,8,256]{3,2,1,0:T(8,128)S(1)}, f32[2,32,8,256]{3,2,1,0:T(8,128)S(1)}, u32[]{:S(2)}, u32[]{:S(2)}) collective-permute-start(f32[2,32,8,256]{3,2,1,0:T(8,128)S(1)} %get-tuple-element.64.refs_7_.refs_9_), channel_id=1, source_target_pairs={{0,1},{1,0},{2,3},{3,2},{4,5},{5,4},{6,7},{7,6},{8,9},{9,8},{10,11... | collective-permute-start | bytes 1572872 | tf_op jit(solution)/shard_map/ppermute | solution.py:258
  175.2 19.8 %collective-permute-start.44 = (f32[2,32,8,256]{3,2,1,0:T(8,128)S(1)}, f32[2,32,8,256]{3,2,1,0:T(8,128)}, u32[]{:S(2)}, u32[]{:S(2)}) collective-permute-start(f32[2,32,8,256]{3,2,1,0:T(8,128)S(1)} %get-tuple-element.64.refs_7_.refs_9_), channel_id=1, source_target_pairs={{0,2},{1,3},{2,0},{3,1},{4,6},{5,7},{6,4},{7,5},{8,10},{9,11},{10,... | collective-permute-start | bytes 1572872 | tf_op jit(solution)/shard_map/ppermute | solution.py:258
  176.9 18.1 %collective-permute-start.41 = (f32[2,32,8,256]{3,2,1,0:T(8,128)S(1)}, f32[2,32,8,256]{3,2,1,0:T(8,128)S(1)}, u32[]{:S(2)}, u32[]{:S(2)}) collective-permute-start(f32[2,32,8,256]{3,2,1,0:T(8,128)S(1)} %get-tuple-element.63.refs_6_.refs_8_), channel_id=1, source_target_pairs={{0,1},{1,0},{2,3},{3,2},{4,5},{5,4},{6,7},{7,6},{8,9},{9,8},{10,11... | collective-permute-start | bytes 1572872 | tf_op jit(solution)/shard_map/ppermute | solution.py:258
  176.9 18.1 %collective-permute-start.45 = (f32[2,32,8,256]{3,2,1,0:T(8,128)S(1)}, f32[2,32,8,256]{3,2,1,0:T(8,128)}, u32[]{:S(2)}, u32[]{:S(2)}) collective-permute-start(f32[2,32,8,256]{3,2,1,0:T(8,128)S(1)} %get-tuple-element.63.refs_6_.refs_8_), channel_id=1, source_target_pairs={{0,4},{1,5},{2,6},{3,7},{4,0},{5,1},{6,2},{7,3},{8,12},{9,13},{10,... | collective-permute-start | bytes 1572872 | tf_op jit(solution)/shard_map/ppermute | solution.py:258
  178.7 16.3 %collective-permute-start.43 = (f32[2,32,8,256]{3,2,1,0:T(8,128)S(1)}, f32[2,32,8,256]{3,2,1,0:T(8,128)S(1)}, u32[]{:S(2)}, u32[]{:S(2)}) collective-permute-start(f32[2,32,8,256]{3,2,1,0:T(8,128)S(1)} %get-tuple-element.65.refs_8_.refs_10_), channel_id=1, source_target_pairs={{0,1},{1,0},{2,3},{3,2},{4,5},{5,4},{6,7},{7,6},{8,9},{9,8},{10,11... | collective-permute-start | bytes 1572872 | tf_op jit(solution)/shard_map/ppermute | solution.py:258
  (71 other events, 792.9 us)

commit v4 on v3

--- a/solution.py
+++ b/solution.py
@@ -325,8 +325,7 @@
     def owns(row):
         return jnp.any(row[None, :] == own_blocks[:, None], axis=1).astype(jnp.int32)
 
-    def finish_upper(j, gathered):
-        zt = product(struct_upper[j], sigma_anc, gathered, 1, j)
+    def finish_upper(j, zt):
         return upper(j, upper_flags[j], pos, zt, pieces, upper_diag[j], v[j], vt[j])
 
     def both_cores(lines):
@@ -395,13 +394,17 @@
     gathered += [d0, d1, d2, d3, swapped[2], swapped[3], *other_core([d2, d3])]
 
     s = [first_pair, jnp.concatenate([across, before])]
-    sides = [move(a, ALONG_X) for a in s] + [move(a, ALONG_Y) for a in s]
-    up0 = finish_upper(0, gathered)
-    sides = list(sync(sides, [up0[2]]))
-    corner = [move(sides[2], ALONG_X), move(sides[1], ALONG_Y)]
-    near = both_cores(s + sides)
-    up1 = finish_upper(1, gathered)
-    corner = list(sync(corner, [up1[2], *near]))
+    tx = [move(a, ALONG_X) for a in s]
+    ty = [move(a, ALONG_Y) for a in s]
+    zt0 = product(struct_upper[0], sigma_anc, gathered, 1, 0)
+    zt1 = product(struct_upper[1], sigma_anc, gathered, 1, 1)
+    far_s = other_core(s)
+    *sides, zt0, zt1 = sync([*tx, *ty, zt0, zt1], far_s)
+    tx, ty = sides[:2], sides[2:]
+    corner = [move(ty[0], ALONG_X), move(tx[1], ALONG_Y)]
+    up0, up1 = finish_upper(0, zt0), finish_upper(1, zt1)
+    near = s + sides + far_s + other_core(sides)
+    corner = list(sync(corner, [up0[2], up1[2], *near]))
     zt = product(low_blocks, sigma_anc, near + both_cores(corner), LOWER_NODES_2, mib=60)
     panel, late = lower(lower_flags, pos, [zt], pieces, (up0, up1))
     by_device = (CHIPS_Z, CHIPS_Y * CHIPS_X, CORES, -1, W)

time: 243 us -> 242 us (level)
  waiting for transfers between devices: 129 us -> 126 us
    ppermute x55, waiting for transfers between devices: 85.7 us -> 83 us  [move(): return lax.ppermute(x, 'blk', pairs)]
    unnamed x79 -> x95, local copies, waits for them, and re-layouts: 5.43 us -> 6.98 us
  transfers between devices with their start and end apart: 56 -> 56, of which waited for: 26 -> 27; matrix products, arithmetic and copies ran while one was open for 2% -> 3% of each run, Pallas kernels for 13% -> 14%
where the time goes in v4:
time: 242 us; the launch traced here: 241 us
  waiting for transfers between devices  126 us (52%)
  Pallas kernels  53.3 us (22%)
  starting transfers between devices  44.7 us (18%)
  local copies, waits for them, and re-layouts  12.6 us (5%)
  other arithmetic  2.92 us (1%)
    ppermute x55, waiting for transfers between devices, move(): return lax.ppermute(x, 'blk', pairs)  83 us
    all_to_all x1, waiting for transfers between devices, one_group(): spread = lax.all_to_all(pieces, 'blk', 0, 0, tiled=True).reshape(-1, SUB, W)  42.9 us
    pallas_call x3, Pallas kernels, product(): pl.pallas_call(lambda *refs: product_body(accs, *refs), out_shape=jax.Sha...  39.7 us
    ppermute x55, starting transfers between devices, move(): return lax.ppermute(x, 'blk', pairs)  37.4 us
    all_to_all x1, starting transfers between devices, one_group(): spread = lax.all_to_all(pieces, 'blk', 0, 0, tiled=True).reshape(-1, SUB, W)  7.3 us
    pallas_call x2, Pallas kernels, upper(): pl.pallas_call(upper_body, out_shape=out_shape, grid=(1,), in_specs=[pl.B...  7.02 us
    unnamed x95, local copies, waits for them, and re-layouts  6.98 us
  transfers between devices with their start and end apart: 56, of which 27 were waited for; matrix products, arithmetic and copies ran while one was open for 3% of the time, Pallas kernels for 14%

profile of v4, /device:TPU:0, one launch (start us, length us, event | category | flops | bytes accessed | tf_op | source)
XLA Modules:
  0.0 241.1 jit_solution(2874461425540236676)
XLA Ops:
  2.2 1.9 transposed_pieces.1.up_ref.low_ref.refs_3_
  4.1 7.3 %all-to-all-start = ((f32[32,4,2,8,256]{4,3,2,1,0:T(8,128)}), f32[32,4,2,8,256]{4,3,2,1,0:T(8,128)S(1)}, u32[]{:S(2)}, u32[]{:S(2)}) async-start(f32[32,4,2,8,256]{4,3,2,1,0:T(8,128)} %transposed_pieces.1.up_ref.low_ref.refs_3_), calls=%async_computation | async-start | bytes 4194304 | tf_op jit(solution)/shard_map/all_to_all | solution.py:336
  17.4 42.9 %all-to-all-done = f32[32,4,2,8,256]{4,3,2,1,0:T(8,128)S(1)} async-done(((f32[32,4,2,8,256]{4,3,2,1,0:T(8,128)}), f32[32,4,2,8,256]{4,3,2,1,0:T(8,128)S(1)}, u32[]{:S(2)}, u32[]{:S(2)}) %all-to-all-start) | async-done | bytes 2097184 | tf_op jit(solution)/shard_map/all_to_all | solution.py:336
  66.0 11.8 %collective-permute-done.refs_0_ = f32[1,64,8,256]{3,2,1,0:T(8,128)} collective-permute-done((f32[1,64,8,256]{3,2,1,0:T(8,128)S(1)}, f32[1,64,8,256]{3,2,1,0:T(8,128)}, u32[]{:S(2)}, u32[]{:S(2)}) %collective-permute-start) | collective-permute-done | bytes 524320 | tf_op jit(solution)/shard_map/ppermute | solution.py:258
  81.3 11.2 %collective-permute-done.4.refs_0_ = f32[1,64,8,256]{3,2,1,0:T(8,128)S(1)} collective-permute-done((f32[1,64,8,256]{3,2,1,0:T(8,128)}, f32[1,64,8,256]{3,2,1,0:T(8,128)S(1)}, u32[]{:S(2)}, u32[]{:S(2)}) %collective-permute-start.4) | collective-permute-done | bytes 524320 | tf_op jit(solution)/shard_map/ppermute | solution.py:258
  96.7 11.3 %collective-permute-done.10.refs_1_ = f32[1,64,8,256]{3,2,1,0:T(8,128)S(1)} collective-permute-done((f32[1,64,8,256]{3,2,1,0:T(8,128)S(1)}, f32[1,64,8,256]{3,2,1,0:T(8,128)S(1)}, u32[]{:S(2)}, u32[]{:S(2)}) %collective-permute-start.10) | collective-permute-done | bytes 524320 | tf_op jit(solution)/shard_map/ppermute | solution.py:258
  109.5 2.4 %collective-permute-done.9.refs_0_ = f32[1,64,8,256]{3,2,1,0:T(8,128)S(1)} collective-permute-done((f32[1,64,8,256]{3,2,1,0:T(8,128)S(1)}, f32[1,64,8,256]{3,2,1,0:T(8,128)S(1)}, u32[]{:S(2)}, u32[]{:S(2)}) %collective-permute-start.9) | collective-permute-done | bytes 524320 | tf_op jit(solution)/shard_map/ppermute | solution.py:258
  111.9 5.2 %collective-permute-done.19.refs_4_ = f32[1,32,8,256]{3,2,1,0:T(8,128)S(1)} collective-permute-done((f32[1,32,8,256]{3,2,1,0:T(8,128)S(1)}, f32[1,32,8,256]{3,2,1,0:T(8,128)S(1)}, u32[]{:S(2)}, u32[]{:S(2)}) %collective-permute-start.19) | collective-permute-done | bytes 262176 | tf_op jit(solution)/shard_map/ppermute | solution.py:258
  119.9 2.6 %collective-permute-done.18.refs_3_ = f32[1,64,8,256]{3,2,1,0:T(8,128)S(1)} collective-permute-done((f32[1,64,8,256]{3,2,1,0:T(8,128)S(1)}, f32[1,64,8,256]{3,2,1,0:T(8,128)S(1)}, u32[]{:S(2)}, u32[]{:S(2)}) %collective-permute-start.18) | collective-permute-done | bytes 524320 | tf_op jit(solution)/shard_map/ppermute | solution.py:258
  123.1 6.4 %collective-permute-done.15.refs_0_ = f32[1,64,8,256]{3,2,1,0:T(8,128)S(1)} collective-permute-done((f32[1,64,8,256]{3,2,1,0:T(8,128)S(1)}, f32[1,64,8,256]{3,2,1,0:T(8,128)S(1)}, u32[]{:S(2)}, u32[]{:S(2)}) %collective-permute-start.15) | collective-permute-done | bytes 524320 | tf_op jit(solution)/shard_map/ppermute | solution.py:258
  132.5 2.3 collective-permute-start.27
  136.9 8.4 %collective-permute-done.27.refs_3_ = f32[1,32,8,256]{3,2,1,0:T(8,128)S(1)} collective-permute-done((f32[1,32,8,256]{3,2,1,0:T(8,128)S(1)}, f32[1,32,8,256]{3,2,1,0:T(8,128)S(1)}, u32[]{:S(2)}, u32[]{:S(2)}) %collective-permute-start.27) | collective-permute-done | bytes 262176 | tf_op jit(solution)/shard_map/ppermute | solution.py:258
  151.2 1.9 collective-permute-start.32
  153.4 12.5 %product.4.refs_5_ = f32[1,256,512]{2,1,0:T(8,128)S(1)} custom-call(s32[32]{0:T(128)S(1)} %get-tuple-element.102.refs_0_, f32[16384,512]{1,0:T(8,128)} %refs_4_.5, f32[16384,512]{1,0:T(8,128)} %refs_4_.5, f32[16384,512]{1,0:T(8,128)} %refs_4_.5, f32[16384,512]{1,0:T(8,128)} %refs_4_.5, f32[1,64,8,256]{3,2,1,0:T(8,128)S(1)} %sync.8.refs_5_, ...), custom_call_target="tpu_custom_call" | custom-call | flops 6442450944 | bytes 25165824 | tf_op jit(solution)/shard_map/product/pallas_call | solution.py:119
  166.0 12.5 %product.3.refs_4_ = f32[1,256,512]{2,1,0:T(8,128)S(1)} custom-call(s32[32]{0:T(128)S(1)} %get-tuple-element.101.refs_0_, f32[16384,512]{1,0:T(8,128)} %refs_4_.5, f32[16384,512]{1,0:T(8,128)} %refs_4_.5, f32[16384,512]{1,0:T(8,128)} %refs_4_.5, f32[16384,512]{1,0:T(8,128)} %refs_4_.5, f32[1,64,8,256]{3,2,1,0:T(8,128)S(1)} %sync.8.refs_5_, ...), custom_call_target="tpu_custom_call" | custom-call | flops 6442450944 | bytes 25165824 | tf_op jit(solution)/shard_map/product/pallas_call | solution.py:119
  182.5 3.5 %upper.3 = (f32[512,256]{1,0:T(8,128)S(1)}, f32[512,256]{1,0:T(8,128)S(1)}, f32[256,256]{1,0:T(8,128)S(1)}, f32[256,256]{1,0:T(8,128)S(1)}, f32[256,256]{1,0:T(8,128)S(1)}) custom-call(s32[5]{0:T(128)S(1)} %get-tuple-element.106.refs_2_.flag_ref, s32[32]{0:T(128)S(1)} %stack.137.refs_10_.pos_ref.refs_1_, f32[1,256,512]{2,1,0:T(8,128)S(1)} %get-tuple-element.69.zt_ref, ...), custom_call_target="tpu_custom_call" | custom-call | flops 1207959552 | bytes 5242880 | tf_op jit(solution)/shard_map/upper/pallas_call | solution.py:181
  188.2 3.6 %upper.2 = (f32[512,256]{1,0:T(8,128)S(1)}, f32[512,256]{1,0:T(8,128)S(1)}, f32[256,256]{1,0:T(8,128)S(1)}, f32[256,256]{1,0:T(8,128)S(1)}, f32[256,256]{1,0:T(8,128)S(1)}) custom-call(s32[5]{0:T(128)S(1)} %get-tuple-element.105.refs_1_.flag_ref, s32[32]{0:T(128)S(1)} %stack.137.refs_10_.pos_ref.refs_1_, f32[1,256,512]{2,1,0:T(8,128)S(1)} %get-tuple-element.67.zt_ref, ...), custom_call_target="tpu_custom_call" | custom-call | flops 1207959552 | bytes 5242880 | tf_op jit(solution)/shard_map/upper/pallas_call | solution.py:181
  198.3 14.7 %product.5.refs_2_ = f32[2,256,512]{2,1,0:T(8,128)} custom-call(s32[32]{0:T(128)} %copy-done.41, f32[16384,512]{1,0:T(8,128)} %refs_4_.5, f32[16384,512]{1,0:T(8,128)} %refs_4_.5, f32[16384,512]{1,0:T(8,128)} %refs_4_.5, f32[16384,512]{1,0:T(8,128)} %refs_4_.5, f32[2,32,8,256]{3,2,1,0:T(8,128)} %copy-done, f32[2,32,8,256]{3,2,1,0:T(8,128)} %copy-done.12, ...), custom_call_target="tpu_custom_call" | custom-call | flops 6442450944 | bytes 25165824 | tf_op jit(solution)/shard_map/product/pallas_call | solution.py:119
  214.2 3.5 %lower.1 = (f32[512,1024]{1,0:T(8,128)}, f32[512,256]{1,0:T(8,128)S(1)}) custom-call(s32[4]{0:T(128)S(1)} %pad_add_fusion.refs_9_.refs_0_, s32[32]{0:T(128)S(1)} %stack.137.refs_10_.pos_ref.refs_1_, f32[2,256,512]{2,1,0:T(8,128)S(1)} %copy-done.11, f32[32,4,2,8,256]{4,3,2,1,0:T(8,128)} %transposed_pieces.1.up_ref.low_ref.refs_3_, f32[512,256]{1,0:T(8,128)S(1)} %copy-done.31, ...), custom_call_target="tpu_custom_call" | custom-call | flops 402653184 | bytes 7864320 | tf_op jit(solution)/shard_map/lower/pallas_call | solution.py:218
  218.1 2.1 collective-permute-done.48
  224.0 4.3 %collective-permute-done.49 = f32[4,48,256]{2,1,0:T(8,128)S(1)} collective-permute-done((f32[4,48,256]{2,1,0:T(8,128)S(1)}, f32[4,48,256]{2,1,0:T(8,128)S(1)}, u32[]{:S(2)}, u32[]{:S(2)}) %collective-permute-start.49) | collective-permute-done | bytes 196640 | tf_op jit(solution)/shard_map/ppermute | solution.py:258
  228.3 3.3 %collective-permute-done.50 = f32[4,48,256]{2,1,0:T(8,128)S(1)} collective-permute-done((f32[4,48,256]{2,1,0:T(8,128)S(1)}, f32[4,48,256]{2,1,0:T(8,128)S(1)}, u32[]{:S(2)}, u32[]{:S(2)}) %collective-permute-start.50) | collective-permute-done | bytes 196640 | tf_op jit(solution)/shard_map/ppermute | solution.py:258
  233.4 2.2 collective-permute-start.53
  236.8 2.2 collective-permute-done.52
  (236 shorter events, 59.4 us)
Async XLA Ops:
  4.1 56.2 %all-to-all-start = ((f32[32,4,2,8,256]{4,3,2,1,0:T(8,128)}), f32[32,4,2,8,256]{4,3,2,1,0:T(8,128)S(1)}, u32[]{:S(2)}, u32[]{:S(2)}) async-start(f32[32,4,2,8,256]{4,3,2,1,0:T(8,128)} %transposed_pieces.1.up_ref.low_ref.refs_3_), calls=%async_computation | async-start | bytes 4194304 | tf_op jit(solution)/shard_map/all_to_all | solution.py:336
  62.5 15.4 %collective-permute-start = (f32[1,64,8,256]{3,2,1,0:T(8,128)S(1)}, f32[1,64,8,256]{3,2,1,0:T(8,128)}, u32[]{:S(2)}, u32[]{:S(2)}) collective-permute-start(f32[1,64,8,256]{3,2,1,0:T(8,128)S(1)} %sync.8.refs_5_), channel_id=1, source_target_pairs={{0,8},{1,9},{2,10},{3,11},{4,12},{5,13},{6,14},{7,15},{8,16},{9,17... | collective-permute-start | bytes 1572872 | tf_op jit(solution)/shard_map/ppermute | solution.py:258
  62.5 15.4 %collective-permute-start.1 = (f32[1,64,8,256]{3,2,1,0:T(8,128)S(1)}, f32[1,64,8,256]{3,2,1,0:T(8,128)}, u32[]{:S(2)}, u32[]{:S(2)}) collective-permute-start(f32[1,64,8,256]{3,2,1,0:T(8,128)S(1)} %sync.8.refs_5_), channel_id=1, source_target_pairs={{0,2},{1,3},{2,0},{3,1},{4,6},{5,7},{6,4},{7,5},{8,10},{9,11},{10,... | collective-permute-start | bytes 1572872 | tf_op jit(solution)/shard_map/ppermute | solution.py:258
  63.9 14.0 %collective-permute-start.2 = (f32[1,64,8,256]{3,2,1,0:T(8,128)S(1)}, f32[1,64,8,256]{3,2,1,0:T(8,128)}, u32[]{:S(2)}, u32[]{:S(2)}) collective-permute-start(f32[1,64,8,256]{3,2,1,0:T(8,128)S(1)} %sync.8.refs_5_), channel_id=1, source_target_pairs={{0,4},{1,5},{2,6},{3,7},{4,0},{5,1},{6,2},{7,3},{8,12},{9,13},{10,... | collective-permute-start | bytes 1572872 | tf_op jit(solution)/shard_map/ppermute | solution.py:258
  77.9 14.6 %collective-permute-start.4 = (f32[1,64,8,256]{3,2,1,0:T(8,128)}, f32[1,64,8,256]{3,2,1,0:T(8,128)S(1)}, u32[]{:S(2)}, u32[]{:S(2)}) collective-permute-start(f32[1,64,8,256]{3,2,1,0:T(8,128)} %get-tuple-element.43.refs_6_), channel_id=1, source_target_pairs={{0,8},{1,9},{2,10},{3,11},{4,12},{5,13},{6,14},{7,15},{8,16},{9,17... | collective-permute-start | bytes 1572872 | tf_op jit(solution)/shard_map/ppermute | solution.py:258
  78.0 14.6 %collective-permute-start.5 = (f32[1,64,8,256]{3,2,1,0:T(8,128)}, f32[1,64,8,256]{3,2,1,0:T(8,128)S(1)}, u32[]{:S(2)}, u32[]{:S(2)}) collective-permute-start(f32[1,64,8,256]{3,2,1,0:T(8,128)} %get-tuple-element.43.refs_6_), channel_id=1, source_target_pairs={{0,2},{1,3},{2,0},{3,1},{4,6},{5,7},{6,4},{7,5},{8,10},{9,11},{10,... | collective-permute-start | bytes 1572872 | tf_op jit(solution)/shard_map/ppermute | solution.py:258
  79.7 13.4 %collective-permute-start.6 = (f32[1,64,8,256]{3,2,1,0:T(8,128)}, f32[1,64,8,256]{3,2,1,0:T(8,128)S(1)}, u32[]{:S(2)}, u32[]{:S(2)}) collective-permute-start(f32[1,64,8,256]{3,2,1,0:T(8,128)} %get-tuple-element.43.refs_6_), channel_id=1, source_target_pairs={{0,4},{1,5},{2,6},{3,7},{4,0},{5,1},{6,2},{7,3},{8,12},{9,13},{10,... | collective-permute-start | bytes 1572872 | tf_op jit(solution)/shard_map/ppermute | solution.py:258
  93.1 14.9 %collective-permute-start.10 = (f32[1,64,8,256]{3,2,1,0:T(8,128)S(1)}, f32[1,64,8,256]{3,2,1,0:T(8,128)S(1)}, u32[]{:S(2)}, u32[]{:S(2)}) collective-permute-start(f32[1,64,8,256]{3,2,1,0:T(8,128)S(1)} %get-tuple-element.45.refs_7_), channel_id=1, source_target_pairs={{0,2},{1,3},{2,0},{3,1},{4,6},{5,7},{6,4},{7,5},{8,10},{9,11},{10,... | collective-permute-start | bytes 1572872 | tf_op jit(solution)/shard_map/ppermute | solution.py:258
  94.0 14.4 %collective-permute-start.11 = (f32[1,64,8,256]{3,2,1,0:T(8,128)S(1)}, f32[1,64,8,256]{3,2,1,0:T(8,128)S(1)}, u32[]{:S(2)}, u32[]{:S(2)}) collective-permute-start(f32[1,64,8,256]{3,2,1,0:T(8,128)S(1)} %get-tuple-element.45.refs_7_), channel_id=1, source_target_pairs={{0,4},{1,5},{2,6},{3,7},{4,0},{5,1},{6,2},{7,3},{8,12},{9,13},{10,... | collective-permute-start | bytes 1572872 | tf_op jit(solution)/shard_map/ppermute | solution.py:258
  95.4 14.1 %collective-permute-start.12 = (f32[1,64,8,256]{3,2,1,0:T(8,128)S(1)}, f32[1,64,8,256]{3,2,1,0:T(8,128)S(1)}, u32[]{:S(2)}, u32[]{:S(2)}) collective-permute-start(f32[1,64,8,256]{3,2,1,0:T(8,128)S(1)} %get-tuple-element.45.refs_7_), channel_id=1, source_target_pairs={{0,1},{1,0},{2,3},{3,2},{4,5},{5,4},{6,7},{7,6},{8,9},{9,8},{10,11... | collective-permute-start | bytes 1572872 | tf_op jit(solution)/shard_map/ppermute | solution.py:258
  95.4 16.5 %collective-permute-start.9 = (f32[1,64,8,256]{3,2,1,0:T(8,128)S(1)}, f32[1,64,8,256]{3,2,1,0:T(8,128)S(1)}, u32[]{:S(2)}, u32[]{:S(2)}) collective-permute-start(f32[1,64,8,256]{3,2,1,0:T(8,128)S(1)} %get-tuple-element.45.refs_7_), channel_id=1, source_target_pairs={{0,8},{1,9},{2,10},{3,11},{4,12},{5,13},{6,14},{7,15},{8,16},{9,17... | collective-permute-start | bytes 1572872 | tf_op jit(solution)/shard_map/ppermute | solution.py:258
  96.0 22.3 %collective-permute-start.17 = (f32[1,64,8,256]{3,2,1,0:T(8,128)}, f32[1,64,8,256]{3,2,1,0:T(8,128)S(1)}, u32[]{:S(2)}, u32[]{:S(2)}) collective-permute-start(f32[1,64,8,256]{3,2,1,0:T(8,128)} %get-tuple-element.46.refs_13_), channel_id=1, source_target_pairs={{0,2},{1,3},{2,0},{3,1},{4,6},{5,7},{6,4},{7,5},{8,10},{9,11},{10,... | collective-permute-start | bytes 1572872 | tf_op jit(solution)/shard_map/ppermute | solution.py:258
  108.4 14.1 %collective-permute-start.18 = (f32[1,64,8,256]{3,2,1,0:T(8,128)S(1)}, f32[1,64,8,256]{3,2,1,0:T(8,128)S(1)}, u32[]{:S(2)}, u32[]{:S(2)}) collective-permute-start(f32[1,64,8,256]{3,2,1,0:T(8,128)S(1)} %get-tuple-element.49.refs_10_), channel_id=1, source_target_pairs={{0,4},{1,5},{2,6},{3,7},{4,0},{5,1},{6,2},{7,3},{8,12},{9,13},{10,... | collective-permute-start | bytes 1572872 | tf_op jit(solution)/shard_map/ppermute | solution.py:258
  109.5 13.0 %collective-permute-start.21 = (f32[1,64,8,256]{3,2,1,0:T(8,128)S(1)}, f32[1,64,8,256]{3,2,1,0:T(8,128)S(1)}, u32[]{:S(2)}, u32[]{:S(2)}) collective-permute-start(f32[1,64,8,256]{3,2,1,0:T(8,128)S(1)} %get-tuple-element.49.refs_10_), channel_id=1, source_target_pairs={{0,1},{1,0},{2,3},{3,2},{4,5},{5,4},{6,7},{7,6},{8,9},{9,8},{10,11... | collective-permute-start | bytes 1572872 | tf_op jit(solution)/shard_map/ppermute | solution.py:258
  118.3 14.3 %collective-permute-start.16 = (f32[1,64,8,256]{3,2,1,0:T(8,128)S(1)}, f32[1,64,8,256]{3,2,1,0:T(8,128)S(1)}, u32[]{:S(2)}, u32[]{:S(2)}) collective-permute-start(f32[1,64,8,256]{3,2,1,0:T(8,128)S(1)} %get-tuple-element.48.refs_8_), channel_id=1, source_target_pairs={{0,4},{1,5},{2,6},{3,7},{4,0},{5,1},{6,2},{7,3},{8,12},{9,13},{10,... | collective-permute-start | bytes 1572872 | tf_op jit(solution)/shard_map/ppermute | solution.py:258
  129.4 15.9 %collective-permute-start.14 = (f32[1,64,8,256]{3,2,1,0:T(8,128)S(1)}, f32[1,64,8,256]{3,2,1,0:T(8,128)S(1)}, u32[]{:S(2)}, u32[]{:S(2)}) collective-permute-start(f32[1,64,8,256]{3,2,1,0:T(8,128)S(1)} %get-tuple-element.47.refs_15_), channel_id=1, source_target_pairs={{0,2},{1,3},{2,0},{3,1},{4,6},{5,7},{6,4},{7,5},{8,10},{9,11},{10,... | collective-permute-start | bytes 1572872 | tf_op jit(solution)/shard_map/ppermute | solution.py:258
  132.5 12.8 %collective-permute-start.27 = (f32[1,32,8,256]{3,2,1,0:T(8,128)S(1)}, f32[1,32,8,256]{3,2,1,0:T(8,128)S(1)}, u32[]{:S(2)}, u32[]{:S(2)}) collective-permute-start(f32[1,32,8,256]{3,2,1,0:T(8,128)S(1)} %get-tuple-element.50), channel_id=1, source_target_pairs={{0,24},{1,25},{2,26},{3,27},{4,28},{5,29},{6,30},{7,31},{8,0},{9,1... | collective-permute-start | bytes 786440 | tf_op jit(solution)/shard_map/ppermute | solution.py:258
  149.3 16.6 %collective-permute-start.33 = (f32[2,32,8,256]{3,2,1,0:T(8,128)S(1)}, f32[2,32,8,256]{3,2,1,0:T(8,128)S(1)}, u32[]{:S(2)}, u32[]{:S(2)}) collective-permute-start(f32[2,32,8,256]{3,2,1,0:T(8,128)S(1)} %constant_dynamic-update-slice_fusion.refs_5_.refs_6_), channel_id=1, source_target_pairs={{0,2},{1,3},{2,0},{3,1},{4,6},{5,7},{6,4},{7,5},{8,10},{9,11},{10,... | collective-permute-start | bytes 1572872 | tf_op jit(solution)/shard_map/ppermute | solution.py:258
  149.4 29.1 %collective-permute-start.35 = (f32[2,32,8,256]{3,2,1,0:T(8,128)S(1)}, f32[2,32,8,256]{3,2,1,0:T(8,128)S(1)}, u32[]{:S(2)}, u32[]{:S(2)}) collective-permute-start(f32[2,32,8,256]{3,2,1,0:T(8,128)S(1)} %constant_dynamic-update-slice_fusion.refs_5_.refs_6_), channel_id=1, source_target_pairs={{0,4},{1,5},{2,6},{3,7},{4,0},{5,1},{6,2},{7,3},{8,12},{9,13},{10,... | collective-permute-start | bytes 1572872 | tf_op jit(solution)/shard_map/ppermute | solution.py:258
  151.2 27.4 %collective-permute-start.39 = (f32[2,32,8,256]{3,2,1,0:T(8,128)S(1)}, f32[2,32,8,256]{3,2,1,0:T(8,128)S(1)}, u32[]{:S(2)}, u32[]{:S(2)}) collective-permute-start(f32[2,32,8,256]{3,2,1,0:T(8,128)S(1)} %constant_dynamic-update-slice_fusion.refs_5_.refs_6_), channel_id=1, source_target_pairs={{0,1},{1,0},{2,3},{3,2},{4,5},{5,4},{6,7},{7,6},{8,9},{9,8},{10,11... | collective-permute-start | bytes 1572872 | tf_op jit(solution)/shard_map/ppermute | solution.py:258
  151.2 27.4 %collective-permute-start.32 = (f32[2,32,8,256]{3,2,1,0:T(8,128)S(1)}, f32[2,32,8,256]{3,2,1,0:T(8,128)S(1)}, u32[]{:S(2)}, u32[]{:S(2)}) collective-permute-start(f32[2,32,8,256]{3,2,1,0:T(8,128)S(1)} %get-tuple-element.58.refs_4_.refs_5_), channel_id=1, source_target_pairs={{0,2},{1,3},{2,0},{3,1},{4,6},{5,7},{6,4},{7,5},{8,10},{9,11},{10,... | collective-permute-start | bytes 1572872 | tf_op jit(solution)/shard_map/ppermute | solution.py:258
  153.1 25.5 %collective-permute-start.34 = (f32[2,32,8,256]{3,2,1,0:T(8,128)S(1)}, f32[2,32,8,256]{3,2,1,0:T(8,128)S(1)}, u32[]{:S(2)}, u32[]{:S(2)}) collective-permute-start(f32[2,32,8,256]{3,2,1,0:T(8,128)S(1)} %get-tuple-element.58.refs_4_.refs_5_), channel_id=1, source_target_pairs={{0,4},{1,5},{2,6},{3,7},{4,0},{5,1},{6,2},{7,3},{8,12},{9,13},{10,... | collective-permute-start | bytes 1572872 | tf_op jit(solution)/shard_map/ppermute | solution.py:258
  179.3 14.4 %collective-permute-start.44 = (f32[2,32,8,256]{3,2,1,0:T(8,128)S(1)}, f32[2,32,8,256]{3,2,1,0:T(8,128)}, u32[]{:S(2)}, u32[]{:S(2)}) collective-permute-start(f32[2,32,8,256]{3,2,1,0:T(8,128)S(1)} %get-tuple-element.65.refs_8_.refs_9_), channel_id=1, source_target_pairs={{0,2},{1,3},{2,0},{3,1},{4,6},{5,7},{6,4},{7,5},{8,10},{9,11},{10,... | collective-permute-start | bytes 1572872 | tf_op jit(solution)/shard_map/ppermute | solution.py:258
  180.8 14.3 %collective-permute-start.45 = (f32[2,32,8,256]{3,2,1,0:T(8,128)S(1)}, f32[2,32,8,256]{3,2,1,0:T(8,128)}, u32[]{:S(2)}, u32[]{:S(2)}) collective-permute-start(f32[2,32,8,256]{3,2,1,0:T(8,128)S(1)} %get-tuple-element.64.refs_7_.refs_8_), channel_id=1, source_target_pairs={{0,4},{1,5},{2,6},{3,7},{4,0},{5,1},{6,2},{7,3},{8,12},{9,13},{10,... | collective-permute-start | bytes 1572872 | tf_op jit(solution)/shard_map/ppermute | solution.py:258
  (79 other events, 746.9 us)

commit v5 on v4

--- a/solution.py
+++ b/solution.py
@@ -150,13 +150,13 @@
     return scratch[...].T
 
 
-def upper_body(flag_ref, pos_ref, zt_ref, up_ref, low_ref, diag_ref, v_ref, vt_ref, *outs):
+def upper_body(flag_ref, pos_ref, zt_ref, up_ref, low_ref, diag_ref, low_diag_ref, v_ref, *outs):
     g_ref, gv_ref, a_ref, yp_ref, l_ref, scratch = outs
     z = in_order(pos_ref, [zt_ref], 0, scratch)
     g = -z * row_flags(z.shape[0], flag_ref[0], flag_ref[1])
     g_ref[...] = g
     on_first = flag_ref[4].astype(F32)
-    a = diag_ref[0] * on_first - dot3(local_lines(up_ref, 0), g)
+    a = diag_ref[...] * on_first - dot3(local_lines(up_ref, 0), g)
     a_ref[...] = a
     below = g * row_flags(z.shape[0], flag_ref[2], flag_ref[3])
     gv = dot3(below, v_ref[...])
@@ -164,10 +164,10 @@
     u = local_lines(low_ref, 0)
     yp = dot3(a, v_ref[...]) + dot3(u, below).T
     yp_ref[...] = -yp
-    l_ref[...] = dot3(vt_ref[...], yp) + dot3(u, gv) + diag_ref[1] * on_first
-
-
-def upper(j, flags, pos, zt, pieces, diag, v, vt):
+    l_ref[...] = dot3(v_ref[...].T, yp) + dot3(u, gv) + low_diag_ref[...] * on_first
+
+
+def upper(j, flags, pos, zt, pieces, diag, v):
     cols = zt.shape[2]
     square = jax.ShapeDtypeStruct((W, W), F32)
     tall = jax.ShapeDtypeStruct((cols, W), F32)
@@ -176,6 +176,9 @@
 
     def own(s):
         return pl.BlockSpec((PIECES, 1, 2, SUB, W), lambda i: (0, s, 0, 0, 0))
+
+    def block(s):
+        return pl.BlockSpec((W, W), lambda i: (s, 0))
 
     out_shape = (tall, tall, square, square, square)
     return pl.pallas_call(
@@ -183,13 +186,13 @@
         out_shape=out_shape,
         grid=(1,),
         in_specs=[pl.BlockSpec(memory_space=pltpu.SMEM)] * 2
-        + [whole(zt), own(j), own(UPPER_NODES_1 + j), whole(diag), whole(v), whole(vt)],
+        + [whole(zt), own(j), own(UPPER_NODES_1 + j), block(j), block(UPPER_NODES_1 + j), block(j)],
         out_specs=tuple(whole(o) for o in out_shape),
         scratch_shapes=[pltpu.VMEM((W, cols), F32)],
         compiler_params=params(24),
         cost_estimate=cost(24 * W * W * (cols + W), 4 * W * (6 * cols + 8 * W)),
         name="upper",
-    )(flags, pos, zt, pieces, pieces, diag, v, vt)
+    )(flags, pos, zt, pieces, pieces, diag, diag, v)
 
 
 def lower_body(parts, flag_ref, pos_ref, *refs):
@@ -316,9 +319,6 @@
 def one_group(sigma_anc, panels, diag_inv, scaled_parent_panel, struct_upper, struct_lower):
     me = lax.axis_index("blk")
     pos = piece_order(me)
-    v = scaled_parent_panel.reshape(LOWER_NODES_2, W, W)
-    vt = jnp.transpose(v, (0, 2, 1))
-    diag = diag_inv.reshape(UPPER_NODES_1 + LOWER_NODES_2, W, W)
     own_blocks = 2 * me + jnp.arange(2, dtype=jnp.int32)
     on_first = (me == 0).astype(jnp.int32)[None]
 
@@ -326,7 +326,7 @@
         return jnp.any(row[None, :] == own_blocks[:, None], axis=1).astype(jnp.int32)
 
     def finish_upper(j, zt):
-        return upper(j, upper_flags[j], pos, zt, pieces, upper_diag[j], v[j], vt[j])
+        return upper(j, upper_flags[j], pos, zt, pieces, diag_inv, scaled_parent_panel)
 
     def both_cores(lines):
         return lines + other_core(lines)
@@ -343,13 +343,11 @@
         jnp.concatenate([owns(struct_upper[j]), owns(struct_lower[j]), on_first])
         for j in range(UPPER_NODES_1)
     ]
-    upper_diag = [jnp.stack([diag[j], diag[UPPER_NODES_1 + j]]) for j in range(UPPER_NODES_1)]
     lower_flags = jnp.concatenate([owns(struct_lower[0]), owns(struct_lower[1])])
     own = picked(offsets(struct_upper, which).reshape(-1), spread)
     own_low = picked(offsets(struct_lower, UPPER_NODES_1 + which).reshape(-1), spread)
-    small = upper_flags + upper_diag + [v[0], v[1], vt[0], vt[1], lower_flags, pos, low_blocks]
+    small = upper_flags + [lower_flags, pos, low_blocks]
     (own,) = sync([own], small)
-    v, vt = small[4:6], small[6:8]
 
     lines, xs, ys = [own], [], []
     far_lines, far_xs, far_ys = [], [], []

time: 242 us -> 242 us (level)
  waiting for transfers between devices: 126 us -> 133 us
  local copies, waits for them, and re-layouts: 12.6 us -> 6.31 us
    all_to_all x1, waiting for transfers between devices: 42.9 us -> 47.7 us  [one_group(): spread = lax.all_to_all(pieces, 'blk', 0, 0, tiled=True).reshape(-1, SUB, W)]
    unnamed x95 -> x67, local copies, waits for them, and re-layouts: 6.98 us -> 4.62 us
  transfers between devices with their start and end apart: 56 -> 56, of which waited for: 27 -> 27; matrix products, arithmetic and copies ran while one was open for 3% -> 0% of each run, Pallas kernels for 14% -> 14%
where the time goes in v5:
time: 242 us; the launch traced here: 241 us
  waiting for transfers between devices  133 us (55%)
  Pallas kernels  53.4 us (22%)
  starting transfers between devices  44.8 us (19%)
  local copies, waits for them, and re-layouts  6.31 us (3%)
    ppermute x55, waiting for transfers between devices, move(): return lax.ppermute(x, 'blk', pairs)  84.8 us
    all_to_all x1, waiting for transfers between devices, one_group(): spread = lax.all_to_all(pieces, 'blk', 0, 0, tiled=True).reshape(-1, SUB, W)  47.7 us
    pallas_call x3, Pallas kernels, product(): pl.pallas_call(lambda *refs: product_body(accs, *refs), out_shape=jax.Sha...  39.6 us
    ppermute x55, starting transfers between devices, move(): return lax.ppermute(x, 'blk', pairs)  37.5 us
    all_to_all x1, starting transfers between devices, one_group(): spread = lax.all_to_all(pieces, 'blk', 0, 0, tiled=True).reshape(-1, SUB, W)  7.3 us
    pallas_call x2, Pallas kernels, upper(): pl.pallas_call(upper_body, out_shape=out_shape, grid=(1,), in_specs=[pl.B...  7.13 us
  transfers between devices with their start and end apart: 56, of which 27 were waited for; matrix products, arithmetic and copies ran while one was open for 0% of the time, Pallas kernels for 14%

profile of v5, /device:TPU:0, one launch (start us, length us, event | category | flops | bytes accessed | tf_op | source)
XLA Modules:
  0.0 240.8 jit_solution(16317983800531041585)
XLA Ops:
  4.1 7.3 %all-to-all-start = ((f32[32,4,2,8,256]{4,3,2,1,0:T(8,128)}), f32[32,4,2,8,256]{4,3,2,1,0:T(8,128)S(1)}, u32[]{:S(2)}, u32[]{:S(2)}) async-start(f32[32,4,2,8,256]{4,3,2,1,0:T(8,128)} %transposed_pieces.1.up_ref.low_ref.refs_3_), calls=%async_computation | async-start | bytes 4194304 | tf_op jit(solution)/shard_map/all_to_all | solution.py:336
  12.6 47.7 %all-to-all-done = f32[32,4,2,8,256]{4,3,2,1,0:T(8,128)S(1)} async-done(((f32[32,4,2,8,256]{4,3,2,1,0:T(8,128)}), f32[32,4,2,8,256]{4,3,2,1,0:T(8,128)S(1)}, u32[]{:S(2)}, u32[]{:S(2)}) %all-to-all-start) | async-done | bytes 2097184 | tf_op jit(solution)/shard_map/all_to_all | solution.py:336
  64.6 11.7 %collective-permute-done.refs_0_ = f32[1,64,8,256]{3,2,1,0:T(8,128)} collective-permute-done((f32[1,64,8,256]{3,2,1,0:T(8,128)S(1)}, f32[1,64,8,256]{3,2,1,0:T(8,128)}, u32[]{:S(2)}, u32[]{:S(2)}) %collective-permute-start) | collective-permute-done | bytes 524320 | tf_op jit(solution)/shard_map/ppermute | solution.py:261
  79.8 11.2 %collective-permute-done.4.refs_0_ = f32[1,64,8,256]{3,2,1,0:T(8,128)S(1)} collective-permute-done((f32[1,64,8,256]{3,2,1,0:T(8,128)}, f32[1,64,8,256]{3,2,1,0:T(8,128)S(1)}, u32[]{:S(2)}, u32[]{:S(2)}) %collective-permute-start.4) | collective-permute-done | bytes 524320 | tf_op jit(solution)/shard_map/ppermute | solution.py:261
  95.2 11.3 %collective-permute-done.10.refs_1_ = f32[1,64,8,256]{3,2,1,0:T(8,128)S(1)} collective-permute-done((f32[1,64,8,256]{3,2,1,0:T(8,128)S(1)}, f32[1,64,8,256]{3,2,1,0:T(8,128)S(1)}, u32[]{:S(2)}, u32[]{:S(2)}) %collective-permute-start.10) | collective-permute-done | bytes 524320 | tf_op jit(solution)/shard_map/ppermute | solution.py:261
  108.0 2.4 %collective-permute-done.9.refs_0_ = f32[1,64,8,256]{3,2,1,0:T(8,128)S(1)} collective-permute-done((f32[1,64,8,256]{3,2,1,0:T(8,128)S(1)}, f32[1,64,8,256]{3,2,1,0:T(8,128)S(1)}, u32[]{:S(2)}, u32[]{:S(2)}) %collective-permute-start.9) | collective-permute-done | bytes 524320 | tf_op jit(solution)/shard_map/ppermute | solution.py:261
  110.5 5.2 %collective-permute-done.19.refs_4_ = f32[1,32,8,256]{3,2,1,0:T(8,128)S(1)} collective-permute-done((f32[1,32,8,256]{3,2,1,0:T(8,128)S(1)}, f32[1,32,8,256]{3,2,1,0:T(8,128)S(1)}, u32[]{:S(2)}, u32[]{:S(2)}) %collective-permute-start.19) | collective-permute-done | bytes 262176 | tf_op jit(solution)/shard_map/ppermute | solution.py:261
  118.4 2.6 %collective-permute-done.18.refs_3_ = f32[1,64,8,256]{3,2,1,0:T(8,128)S(1)} collective-permute-done((f32[1,64,8,256]{3,2,1,0:T(8,128)S(1)}, f32[1,64,8,256]{3,2,1,0:T(8,128)S(1)}, u32[]{:S(2)}, u32[]{:S(2)}) %collective-permute-start.18) | collective-permute-done | bytes 524320 | tf_op jit(solution)/shard_map/ppermute | solution.py:261
  121.6 6.4 %collective-permute-done.15.refs_0_ = f32[1,64,8,256]{3,2,1,0:T(8,128)S(1)} collective-permute-done((f32[1,64,8,256]{3,2,1,0:T(8,128)S(1)}, f32[1,64,8,256]{3,2,1,0:T(8,128)S(1)}, u32[]{:S(2)}, u32[]{:S(2)}) %collective-permute-start.15) | collective-permute-done | bytes 524320 | tf_op jit(solution)/shard_map/ppermute | solution.py:261
  131.0 2.3 collective-permute-start.27
  135.4 8.4 %collective-permute-done.27.refs_3_ = f32[1,32,8,256]{3,2,1,0:T(8,128)S(1)} collective-permute-done((f32[1,32,8,256]{3,2,1,0:T(8,128)S(1)}, f32[1,32,8,256]{3,2,1,0:T(8,128)S(1)}, u32[]{:S(2)}, u32[]{:S(2)}) %collective-permute-start.27) | collective-permute-done | bytes 262176 | tf_op jit(solution)/shard_map/ppermute | solution.py:261
  149.7 1.9 collective-permute-start.32
  151.9 12.5 %product.4.refs_5_ = f32[1,256,512]{2,1,0:T(8,128)S(1)} custom-call(s32[32]{0:T(128)S(1)} %get-tuple-element.94.refs_0_, f32[16384,512]{1,0:T(8,128)} %refs_4_.5, f32[16384,512]{1,0:T(8,128)} %refs_4_.5, f32[16384,512]{1,0:T(8,128)} %refs_4_.5, f32[16384,512]{1,0:T(8,128)} %refs_4_.5, f32[1,64,8,256]{3,2,1,0:T(8,128)S(1)} %sync.8.refs_5_, ...), custom_call_target="tpu_custom_call" | custom-call | flops 6442450944 | bytes 25165824 | tf_op jit(solution)/shard_map/product/pallas_call | solution.py:119
  164.5 12.5 %product.3.refs_4_ = f32[1,256,512]{2,1,0:T(8,128)S(1)} custom-call(s32[32]{0:T(128)S(1)} %get-tuple-element.93.refs_0_, f32[16384,512]{1,0:T(8,128)} %refs_4_.5, f32[16384,512]{1,0:T(8,128)} %refs_4_.5, f32[16384,512]{1,0:T(8,128)} %refs_4_.5, f32[16384,512]{1,0:T(8,128)} %refs_4_.5, f32[1,64,8,256]{3,2,1,0:T(8,128)S(1)} %sync.8.refs_5_, ...), custom_call_target="tpu_custom_call" | custom-call | flops 6442450944 | bytes 25165824 | tf_op jit(solution)/shard_map/product/pallas_call | solution.py:119
  181.0 3.4 %upper.2 = (f32[512,256]{1,0:T(8,128)S(1)}, f32[512,256]{1,0:T(8,128)S(1)}, f32[256,256]{1,0:T(8,128)S(1)}, f32[256,256]{1,0:T(8,128)S(1)}, f32[256,256]{1,0:T(8,128)S(1)}) custom-call(s32[5]{0:T(128)S(1)} %get-tuple-element.97.refs_1_.flag_ref, s32[32]{0:T(128)S(1)} %stack.131.refs_4_.pos_ref.refs_1_, f32[1,256,512]{2,1,0:T(8,128)S(1)} %get-tuple-element.67.zt_ref, ...), custom_call_target="tpu_custom_call" | custom-call | flops 1207959552 | bytes 5242880 | tf_op jit(solution)/shard_map/upper/pallas_call | solution.py:184
  185.7 3.8 %upper.3 = (f32[512,256]{1,0:T(8,128)S(1)}, f32[512,256]{1,0:T(8,128)S(1)}, f32[256,256]{1,0:T(8,128)S(1)}, f32[256,256]{1,0:T(8,128)S(1)}, f32[256,256]{1,0:T(8,128)S(1)}) custom-call(s32[5]{0:T(128)S(1)} %get-tuple-element.98.refs_2_.flag_ref, s32[32]{0:T(128)S(1)} %stack.131.refs_4_.pos_ref.refs_1_, f32[1,256,512]{2,1,0:T(8,128)S(1)} %get-tuple-element.69.zt_ref, ...), custom_call_target="tpu_custom_call" | custom-call | flops 1207959552 | bytes 5242880 | tf_op jit(solution)/shard_map/upper/pallas_call | solution.py:184
  189.6 2.5 %collective-permute-done.44.refs_0_ = f32[2,32,8,256]{3,2,1,0:T(8,128)} collective-permute-done((f32[2,32,8,256]{3,2,1,0:T(8,128)S(1)}, f32[2,32,8,256]{3,2,1,0:T(8,128)}, u32[]{:S(2)}, u32[]{:S(2)}) %collective-permute-start.44) | collective-permute-done | bytes 524320 | tf_op jit(solution)/shard_map/ppermute | solution.py:261
  196.7 14.7 %product.5.refs_2_ = f32[2,256,512]{2,1,0:T(8,128)} custom-call(s32[32]{0:T(128)} %copy-done.30, f32[16384,512]{1,0:T(8,128)} %refs_4_.5, f32[16384,512]{1,0:T(8,128)} %refs_4_.5, f32[16384,512]{1,0:T(8,128)} %refs_4_.5, f32[16384,512]{1,0:T(8,128)} %refs_4_.5, f32[2,32,8,256]{3,2,1,0:T(8,128)} %copy-done.1, f32[2,32,8,256]{3,2,1,0:T(8,128)} %copy-done.9, ...), custom_call_target="tpu_custom_call" | custom-call | flops 6442450944 | bytes 25165824 | tf_op jit(solution)/shard_map/product/pallas_call | solution.py:119
  212.7 3.5 %lower.1 = (f32[512,1024]{1,0:T(8,128)}, f32[512,256]{1,0:T(8,128)S(1)}) custom-call(s32[4]{0:T(128)S(1)} %pad_add_fusion.refs_3_.refs_0_, s32[32]{0:T(128)S(1)} %stack.131.refs_4_.pos_ref.refs_1_, f32[2,256,512]{2,1,0:T(8,128)S(1)} %copy-done.8, f32[32,4,2,8,256]{4,3,2,1,0:T(8,128)} %transposed_pieces.1.up_ref.low_ref.refs_3_, f32[512,256]{1,0:T(8,128)S(1)} %copy-done.17, ...), custom_call_target="tpu_custom_call" | custom-call | flops 402653184 | bytes 7864320 | tf_op jit(solution)/shard_map/lower/pallas_call | solution.py:221
  216.5 2.3 collective-permute-done.48
  223.7 4.3 %collective-permute-done.49 = f32[4,48,256]{2,1,0:T(8,128)S(1)} collective-permute-done((f32[4,48,256]{2,1,0:T(8,128)S(1)}, f32[4,48,256]{2,1,0:T(8,128)S(1)}, u32[]{:S(2)}, u32[]{:S(2)}) %collective-permute-start.49) | collective-permute-done | bytes 196640 | tf_op jit(solution)/shard_map/ppermute | solution.py:261
  227.9 3.3 %collective-permute-done.50 = f32[4,48,256]{2,1,0:T(8,128)S(1)} collective-permute-done((f32[4,48,256]{2,1,0:T(8,128)S(1)}, f32[4,48,256]{2,1,0:T(8,128)S(1)}, u32[]{:S(2)}, u32[]{:S(2)}) %collective-permute-start.50) | collective-permute-done | bytes 196640 | tf_op jit(solution)/shard_map/ppermute | solution.py:261
  233.1 2.2 collective-permute-start.53
  236.5 2.2 collective-permute-done.52
  (203 shorter events, 53.7 us)
Async XLA Ops:
  4.1 56.2 %all-to-all-start = ((f32[32,4,2,8,256]{4,3,2,1,0:T(8,128)}), f32[32,4,2,8,256]{4,3,2,1,0:T(8,128)S(1)}, u32[]{:S(2)}, u32[]{:S(2)}) async-start(f32[32,4,2,8,256]{4,3,2,1,0:T(8,128)} %transposed_pieces.1.up_ref.low_ref.refs_3_), calls=%async_computation | async-start | bytes 4194304 | tf_op jit(solution)/shard_map/all_to_all | solution.py:336
  61.0 15.4 %collective-permute-start = (f32[1,64,8,256]{3,2,1,0:T(8,128)S(1)}, f32[1,64,8,256]{3,2,1,0:T(8,128)}, u32[]{:S(2)}, u32[]{:S(2)}) collective-permute-start(f32[1,64,8,256]{3,2,1,0:T(8,128)S(1)} %sync.8.refs_5_), channel_id=1, source_target_pairs={{0,8},{1,9},{2,10},{3,11},{4,12},{5,13},{6,14},{7,15},{8,16},{9,17... | collective-permute-start | bytes 1572872 | tf_op jit(solution)/shard_map/ppermute | solution.py:261
  61.0 15.4 %collective-permute-start.1 = (f32[1,64,8,256]{3,2,1,0:T(8,128)S(1)}, f32[1,64,8,256]{3,2,1,0:T(8,128)}, u32[]{:S(2)}, u32[]{:S(2)}) collective-permute-start(f32[1,64,8,256]{3,2,1,0:T(8,128)S(1)} %sync.8.refs_5_), channel_id=1, source_target_pairs={{0,2},{1,3},{2,0},{3,1},{4,6},{5,7},{6,4},{7,5},{8,10},{9,11},{10,... | collective-permute-start | bytes 1572872 | tf_op jit(solution)/shard_map/ppermute | solution.py:261
  62.5 13.9 %collective-permute-start.2 = (f32[1,64,8,256]{3,2,1,0:T(8,128)S(1)}, f32[1,64,8,256]{3,2,1,0:T(8,128)}, u32[]{:S(2)}, u32[]{:S(2)}) collective-permute-start(f32[1,64,8,256]{3,2,1,0:T(8,128)S(1)} %sync.8.refs_5_), channel_id=1, source_target_pairs={{0,4},{1,5},{2,6},{3,7},{4,0},{5,1},{6,2},{7,3},{8,12},{9,13},{10,... | collective-permute-start | bytes 1572872 | tf_op jit(solution)/shard_map/ppermute | solution.py:261
  76.4 14.6 %collective-permute-start.4 = (f32[1,64,8,256]{3,2,1,0:T(8,128)}, f32[1,64,8,256]{3,2,1,0:T(8,128)S(1)}, u32[]{:S(2)}, u32[]{:S(2)}) collective-permute-start(f32[1,64,8,256]{3,2,1,0:T(8,128)} %get-tuple-element.43.refs_6_), channel_id=1, source_target_pairs={{0,8},{1,9},{2,10},{3,11},{4,12},{5,13},{6,14},{7,15},{8,16},{9,17... | collective-permute-start | bytes 1572872 | tf_op jit(solution)/shard_map/ppermute | solution.py:261
  76.5 14.6 %collective-permute-start.5 = (f32[1,64,8,256]{3,2,1,0:T(8,128)}, f32[1,64,8,256]{3,2,1,0:T(8,128)S(1)}, u32[]{:S(2)}, u32[]{:S(2)}) collective-permute-start(f32[1,64,8,256]{3,2,1,0:T(8,128)} %get-tuple-element.43.refs_6_), channel_id=1, source_target_pairs={{0,2},{1,3},{2,0},{3,1},{4,6},{5,7},{6,4},{7,5},{8,10},{9,11},{10,... | collective-permute-start | bytes 1572872 | tf_op jit(solution)/shard_map/ppermute | solution.py:261
  78.2 13.4 %collective-permute-start.6 = (f32[1,64,8,256]{3,2,1,0:T(8,128)}, f32[1,64,8,256]{3,2,1,0:T(8,128)S(1)}, u32[]{:S(2)}, u32[]{:S(2)}) collective-permute-start(f32[1,64,8,256]{3,2,1,0:T(8,128)} %get-tuple-element.43.refs_6_), channel_id=1, source_target_pairs={{0,4},{1,5},{2,6},{3,7},{4,0},{5,1},{6,2},{7,3},{8,12},{9,13},{10,... | collective-permute-start | bytes 1572872 | tf_op jit(solution)/shard_map/ppermute | solution.py:261
  91.6 14.9 %collective-permute-start.10 = (f32[1,64,8,256]{3,2,1,0:T(8,128)S(1)}, f32[1,64,8,256]{3,2,1,0:T(8,128)S(1)}, u32[]{:S(2)}, u32[]{:S(2)}) collective-permute-start(f32[1,64,8,256]{3,2,1,0:T(8,128)S(1)} %get-tuple-element.45.refs_7_), channel_id=1, source_target_pairs={{0,2},{1,3},{2,0},{3,1},{4,6},{5,7},{6,4},{7,5},{8,10},{9,11},{10,... | collective-permute-start | bytes 1572872 | tf_op jit(solution)/shard_map/ppermute | solution.py:261
  92.5 14.4 %collective-permute-start.11 = (f32[1,64,8,256]{3,2,1,0:T(8,128)S(1)}, f32[1,64,8,256]{3,2,1,0:T(8,128)S(1)}, u32[]{:S(2)}, u32[]{:S(2)}) collective-permute-start(f32[1,64,8,256]{3,2,1,0:T(8,128)S(1)} %get-tuple-element.45.refs_7_), channel_id=1, source_target_pairs={{0,4},{1,5},{2,6},{3,7},{4,0},{5,1},{6,2},{7,3},{8,12},{9,13},{10,... | collective-permute-start | bytes 1572872 | tf_op jit(solution)/shard_map/ppermute | solution.py:261
  93.9 14.1 %collective-permute-start.12 = (f32[1,64,8,256]{3,2,1,0:T(8,128)S(1)}, f32[1,64,8,256]{3,2,1,0:T(8,128)S(1)}, u32[]{:S(2)}, u32[]{:S(2)}) collective-permute-start(f32[1,64,8,256]{3,2,1,0:T(8,128)S(1)} %get-tuple-element.45.refs_7_), channel_id=1, source_target_pairs={{0,1},{1,0},{2,3},{3,2},{4,5},{5,4},{6,7},{7,6},{8,9},{9,8},{10,11... | collective-permute-start | bytes 1572872 | tf_op jit(solution)/shard_map/ppermute | solution.py:261
  93.9 16.5 %collective-permute-start.9 = (f32[1,64,8,256]{3,2,1,0:T(8,128)S(1)}, f32[1,64,8,256]{3,2,1,0:T(8,128)S(1)}, u32[]{:S(2)}, u32[]{:S(2)}) collective-permute-start(f32[1,64,8,256]{3,2,1,0:T(8,128)S(1)} %get-tuple-element.45.refs_7_), channel_id=1, source_target_pairs={{0,8},{1,9},{2,10},{3,11},{4,12},{5,13},{6,14},{7,15},{8,16},{9,17... | collective-permute-start | bytes 1572872 | tf_op jit(solution)/shard_map/ppermute | solution.py:261
  94.5 22.3 %collective-permute-start.17 = (f32[1,64,8,256]{3,2,1,0:T(8,128)}, f32[1,64,8,256]{3,2,1,0:T(8,128)S(1)}, u32[]{:S(2)}, u32[]{:S(2)}) collective-permute-start(f32[1,64,8,256]{3,2,1,0:T(8,128)} %get-tuple-element.46.refs_13_), channel_id=1, source_target_pairs={{0,2},{1,3},{2,0},{3,1},{4,6},{5,7},{6,4},{7,5},{8,10},{9,11},{10,... | collective-permute-start | bytes 1572872 | tf_op jit(solution)/shard_map/ppermute | solution.py:261
  106.9 14.1 %collective-permute-start.18 = (f32[1,64,8,256]{3,2,1,0:T(8,128)S(1)}, f32[1,64,8,256]{3,2,1,0:T(8,128)S(1)}, u32[]{:S(2)}, u32[]{:S(2)}) collective-permute-start(f32[1,64,8,256]{3,2,1,0:T(8,128)S(1)} %get-tuple-element.49.refs_10_), channel_id=1, source_target_pairs={{0,4},{1,5},{2,6},{3,7},{4,0},{5,1},{6,2},{7,3},{8,12},{9,13},{10,... | collective-permute-start | bytes 1572872 | tf_op jit(solution)/shard_map/ppermute | solution.py:261
  108.0 13.0 %collective-permute-start.21 = (f32[1,64,8,256]{3,2,1,0:T(8,128)S(1)}, f32[1,64,8,256]{3,2,1,0:T(8,128)S(1)}, u32[]{:S(2)}, u32[]{:S(2)}) collective-permute-start(f32[1,64,8,256]{3,2,1,0:T(8,128)S(1)} %get-tuple-element.49.refs_10_), channel_id=1, source_target_pairs={{0,1},{1,0},{2,3},{3,2},{4,5},{5,4},{6,7},{7,6},{8,9},{9,8},{10,11... | collective-permute-start | bytes 1572872 | tf_op jit(solution)/shard_map/ppermute | solution.py:261
  116.8 14.3 %collective-permute-start.16 = (f32[1,64,8,256]{3,2,1,0:T(8,128)S(1)}, f32[1,64,8,256]{3,2,1,0:T(8,128)S(1)}, u32[]{:S(2)}, u32[]{:S(2)}) collective-permute-start(f32[1,64,8,256]{3,2,1,0:T(8,128)S(1)} %get-tuple-element.48.refs_8_), channel_id=1, source_target_pairs={{0,4},{1,5},{2,6},{3,7},{4,0},{5,1},{6,2},{7,3},{8,12},{9,13},{10,... | collective-permute-start | bytes 1572872 | tf_op jit(solution)/shard_map/ppermute | solution.py:261
  127.9 15.9 %collective-permute-start.14 = (f32[1,64,8,256]{3,2,1,0:T(8,128)S(1)}, f32[1,64,8,256]{3,2,1,0:T(8,128)S(1)}, u32[]{:S(2)}, u32[]{:S(2)}) collective-permute-start(f32[1,64,8,256]{3,2,1,0:T(8,128)S(1)} %get-tuple-element.47.refs_15_), channel_id=1, source_target_pairs={{0,2},{1,3},{2,0},{3,1},{4,6},{5,7},{6,4},{7,5},{8,10},{9,11},{10,... | collective-permute-start | bytes 1572872 | tf_op jit(solution)/shard_map/ppermute | solution.py:261
  131.0 12.8 %collective-permute-start.27 = (f32[1,32,8,256]{3,2,1,0:T(8,128)S(1)}, f32[1,32,8,256]{3,2,1,0:T(8,128)S(1)}, u32[]{:S(2)}, u32[]{:S(2)}) collective-permute-start(f32[1,32,8,256]{3,2,1,0:T(8,128)S(1)} %get-tuple-element.50), channel_id=1, source_target_pairs={{0,24},{1,25},{2,26},{3,27},{4,28},{5,29},{6,30},{7,31},{8,0},{9,1... | collective-permute-start | bytes 786440 | tf_op jit(solution)/shard_map/ppermute | solution.py:261
  147.8 16.6 %collective-permute-start.33 = (f32[2,32,8,256]{3,2,1,0:T(8,128)S(1)}, f32[2,32,8,256]{3,2,1,0:T(8,128)S(1)}, u32[]{:S(2)}, u32[]{:S(2)}) collective-permute-start(f32[2,32,8,256]{3,2,1,0:T(8,128)S(1)} %constant_dynamic-update-slice_fusion.refs_5_.refs_6_), channel_id=1, source_target_pairs={{0,2},{1,3},{2,0},{3,1},{4,6},{5,7},{6,4},{7,5},{8,10},{9,11},{10,... | collective-permute-start | bytes 1572872 | tf_op jit(solution)/shard_map/ppermute | solution.py:261
  147.9 29.1 %collective-permute-start.35 = (f32[2,32,8,256]{3,2,1,0:T(8,128)S(1)}, f32[2,32,8,256]{3,2,1,0:T(8,128)S(1)}, u32[]{:S(2)}, u32[]{:S(2)}) collective-permute-start(f32[2,32,8,256]{3,2,1,0:T(8,128)S(1)} %constant_dynamic-update-slice_fusion.refs_5_.refs_6_), channel_id=1, source_target_pairs={{0,4},{1,5},{2,6},{3,7},{4,0},{5,1},{6,2},{7,3},{8,12},{9,13},{10,... | collective-permute-start | bytes 1572872 | tf_op jit(solution)/shard_map/ppermute | solution.py:261
  149.7 27.4 %collective-permute-start.39 = (f32[2,32,8,256]{3,2,1,0:T(8,128)S(1)}, f32[2,32,8,256]{3,2,1,0:T(8,128)S(1)}, u32[]{:S(2)}, u32[]{:S(2)}) collective-permute-start(f32[2,32,8,256]{3,2,1,0:T(8,128)S(1)} %constant_dynamic-update-slice_fusion.refs_5_.refs_6_), channel_id=1, source_target_pairs={{0,1},{1,0},{2,3},{3,2},{4,5},{5,4},{6,7},{7,6},{8,9},{9,8},{10,11... | collective-permute-start | bytes 1572872 | tf_op jit(solution)/shard_map/ppermute | solution.py:261
  149.7 27.4 %collective-permute-start.32 = (f32[2,32,8,256]{3,2,1,0:T(8,128)S(1)}, f32[2,32,8,256]{3,2,1,0:T(8,128)S(1)}, u32[]{:S(2)}, u32[]{:S(2)}) collective-permute-start(f32[2,32,8,256]{3,2,1,0:T(8,128)S(1)} %get-tuple-element.58.refs_4_.refs_5_), channel_id=1, source_target_pairs={{0,2},{1,3},{2,0},{3,1},{4,6},{5,7},{6,4},{7,5},{8,10},{9,11},{10,... | collective-permute-start | bytes 1572872 | tf_op jit(solution)/shard_map/ppermute | solution.py:261
  151.6 25.4 %collective-permute-start.34 = (f32[2,32,8,256]{3,2,1,0:T(8,128)S(1)}, f32[2,32,8,256]{3,2,1,0:T(8,128)S(1)}, u32[]{:S(2)}, u32[]{:S(2)}) collective-permute-start(f32[2,32,8,256]{3,2,1,0:T(8,128)S(1)} %get-tuple-element.58.refs_4_.refs_5_), channel_id=1, source_target_pairs={{0,4},{1,5},{2,6},{3,7},{4,0},{5,1},{6,2},{7,3},{8,12},{9,13},{10,... | collective-permute-start | bytes 1572872 | tf_op jit(solution)/shard_map/ppermute | solution.py:261
  177.7 14.4 %collective-permute-start.44 = (f32[2,32,8,256]{3,2,1,0:T(8,128)S(1)}, f32[2,32,8,256]{3,2,1,0:T(8,128)}, u32[]{:S(2)}, u32[]{:S(2)}) collective-permute-start(f32[2,32,8,256]{3,2,1,0:T(8,128)S(1)} %get-tuple-element.65.refs_8_.refs_9_), channel_id=1, source_target_pairs={{0,2},{1,3},{2,0},{3,1},{4,6},{5,7},{6,4},{7,5},{8,10},{9,11},{10,... | collective-permute-start | bytes 1572872 | tf_op jit(solution)/shard_map/ppermute | solution.py:261
  179.2 14.3 %collective-permute-start.45 = (f32[2,32,8,256]{3,2,1,0:T(8,128)S(1)}, f32[2,32,8,256]{3,2,1,0:T(8,128)}, u32[]{:S(2)}, u32[]{:S(2)}) collective-permute-start(f32[2,32,8,256]{3,2,1,0:T(8,128)S(1)} %get-tuple-element.64.refs_7_.refs_8_), channel_id=1, source_target_pairs={{0,4},{1,5},{2,6},{3,7},{4,0},{5,1},{6,2},{7,3},{8,12},{9,13},{10,... | collective-permute-start | bytes 1572872 | tf_op jit(solution)/shard_map/ppermute | solution.py:261
  (65 other events, 675.8 us)

commit v6 on v5

--- a/solution.py
+++ b/solution.py
@@ -151,7 +151,7 @@
 
 
 def upper_body(flag_ref, pos_ref, zt_ref, up_ref, low_ref, diag_ref, low_diag_ref, v_ref, *outs):
-    g_ref, gv_ref, a_ref, yp_ref, l_ref, scratch = outs
+    g_ref, gv_ref, a_ref, yp_ref, l_ref, scratch = outs[-6:]
     z = in_order(pos_ref, [zt_ref], 0, scratch)
     g = -z * row_flags(z.shape[0], flag_ref[0], flag_ref[1])
     g_ref[...] = g
@@ -167,7 +167,7 @@
     l_ref[...] = dot3(v_ref[...].T, yp) + dot3(u, gv) + low_diag_ref[...] * on_first
 
 
-def upper(j, flags, pos, zt, pieces, diag, v):
+def upper(j, flags, pos, zt, pieces, diag, v, panel):
     cols = zt.shape[2]
     square = jax.ShapeDtypeStruct((W, W), F32)
     tall = jax.ShapeDtypeStruct((cols, W), F32)
@@ -180,37 +180,37 @@
     def block(s):
         return pl.BlockSpec((W, W), lambda i: (s, 0))
 
-    out_shape = (tall, tall, square, square, square)
+    out_shape = (jax.ShapeDtypeStruct((cols, 4 * W), F32), tall, square, square, square)
+    before = [] if panel is None else [panel]
     return pl.pallas_call(
         upper_body,
         out_shape=out_shape,
         grid=(1,),
         in_specs=[pl.BlockSpec(memory_space=pltpu.SMEM)] * 2
-        + [whole(zt), own(j), own(UPPER_NODES_1 + j), block(j), block(UPPER_NODES_1 + j), block(j)],
-        out_specs=tuple(whole(o) for o in out_shape),
+        + [whole(zt), own(j), own(UPPER_NODES_1 + j), block(j), block(UPPER_NODES_1 + j), block(j)]
+        + [pl.BlockSpec(memory_space=pl.ANY)] * len(before),
+        out_specs=(pl.BlockSpec((cols, W), lambda i: (0, j)), *(whole(o) for o in out_shape[1:])),
+        input_output_aliases={8: 0} if before else {},
         scratch_shapes=[pltpu.VMEM((W, cols), F32)],
         compiler_params=params(24),
         cost_estimate=cost(24 * W * W * (cols + W), 4 * W * (6 * cols + 8 * W)),
         name="upper",
-    )(flags, pos, zt, pieces, pieces, diag, diag, v)
+    )(flags, pos, zt, pieces, pieces, diag, diag, v, *before)
 
 
 def lower_body(parts, flag_ref, pos_ref, *refs):
     zt_refs = refs[:parts]
-    low_ref, g0, g1, gv0, gv1, l0, l1, panel_ref, late_ref, scratch = refs[parts:]
-    for j, g_ref in enumerate((g0, g1)):
-        panel_ref[:, j * W : (j + 1) * W] = g_ref[...]
+    low_ref, gv0, gv1, l0, l1, _, panel_ref, late_ref, scratch = refs[parts:]
     for c, (gv_ref, l_ref) in enumerate(((gv0, l0), (gv1, l1))):
         z = in_order(pos_ref, zt_refs, c, scratch)
         z = z * row_flags(z.shape[0], flag_ref[2 * c], flag_ref[2 * c + 1])
-        col = (UPPER_NODES_1 + c) * W
-        panel_ref[:, col : col + W] = -(gv_ref[...] + z)
+        panel_ref[:, c * W : (c + 1) * W] = -(gv_ref[...] + z)
         late_ref[c * W : (c + 1) * W, :] = l_ref[...] + dot3(local_lines(low_ref, c), z)
 
 
 def lower(flags, pos, zts, low, ups):
     cols = zts[0].shape[2]
-    operands = [ups[j][i] for i in (0, 1, 4) for j in range(UPPER_NODES_1)]
+    operands = [ups[j][i] for i in (1, 4) for j in range(UPPER_NODES_1)]
     def whole(x):
         return pl.BlockSpec(x.shape, lambda i: (0,) * x.ndim)
 
@@ -225,13 +225,15 @@
         in_specs=[pl.BlockSpec(memory_space=pltpu.SMEM)] * 2
         + [whole(z) for z in zts]
         + [pl.BlockSpec((PIECES, LOWER_NODES_2, 2, SUB, W), lambda i: (0, 1, 0, 0, 0))]
-        + [whole(o) for o in operands],
-        out_specs=tuple(whole(o) for o in out_shape),
+        + [whole(o) for o in operands]
+        + [pl.BlockSpec(memory_space=pl.ANY)],
+        out_specs=(pl.BlockSpec((cols, 2 * W), lambda i: (0, 1)), whole(out_shape[1])),
+        input_output_aliases={3 + len(zts) + len(operands): 0},
         scratch_shapes=[pltpu.VMEM((W, cols), F32)],
         compiler_params=params(32),
         cost_estimate=cost(12 * W * W * cols, 4 * W * (12 * cols + 6 * W)),
         name="lower",
-    )(flags, pos, *zts, low, *operands)
+    )(flags, pos, *zts, low, *operands, ups[1][0])
 
 
 def device_at(z, y, x, c):
@@ -325,8 +327,8 @@
     def owns(row):
         return jnp.any(row[None, :] == own_blocks[:, None], axis=1).astype(jnp.int32)
 
-    def finish_upper(j, zt):
-        return upper(j, upper_flags[j], pos, zt, pieces, diag_inv, scaled_parent_panel)
+    def finish_upper(j, zt, panel):
+        return upper(j, upper_flags[j], pos, zt, pieces, diag_inv, scaled_parent_panel, panel)
 
     def both_cores(lines):
         return lines + other_core(lines)
@@ -400,7 +402,8 @@
     *sides, zt0, zt1 = sync([*tx, *ty, zt0, zt1], far_s)
     tx, ty = sides[:2], sides[2:]
     corner = [move(ty[0], ALONG_X), move(tx[1], ALONG_Y)]
-    up0, up1 = finish_upper(0, zt0), finish_upper(1, zt1)
+    up0 = finish_upper(0, zt0, None)
+    up1 = finish_upper(1, zt1, up0[0])
     near = s + sides + far_s + other_core(sides)
     corner = list(sync(corner, [up0[2], up1[2], *near]))
     zt = product(low_blocks, sigma_anc, near + both_cores(corner), LOWER_NODES_2, mib=60)

time: 242 us -> 240 us (level)
  no operation moved by 1% of the time
where the time goes in v6:
time: 240 us; the launch traced here: 239 us
  waiting for transfers between devices  133 us (55%)
  Pallas kernels  52.4 us (22%)
  starting transfers between devices  44.8 us (19%)
  local copies, waits for them, and re-layouts  6.19 us (3%)
    ppermute x55, waiting for transfers between devices, move(): return lax.ppermute(x, 'blk', pairs)  85.7 us
    all_to_all x1, waiting for transfers between devices, one_group(): spread = lax.all_to_all(pieces, 'blk', 0, 0, tiled=True).reshape(-1, SUB, W)  47.7 us
    pallas_call x3, Pallas kernels, product(): pl.pallas_call(lambda *refs: product_body(accs, *refs), out_shape=jax.Sha...  39.6 us
    ppermute x55, starting transfers between devices, move(): return lax.ppermute(x, 'blk', pairs)  37.5 us
    all_to_all x1, starting transfers between devices, one_group(): spread = lax.all_to_all(pieces, 'blk', 0, 0, tiled=True).reshape(-1, SUB, W)  7.3 us
    pallas_call x2, Pallas kernels, upper(): pl.pallas_call(upper_body, out_shape=out_shape, grid=(1,), in_specs=[pl.B...  6.94 us
  transfers between devices with their start and end apart: 56, of which 27 were waited for; matrix products, arithmetic and copies ran while one was open for 0% of the time, Pallas kernels for 14%

profile of v6, /device:TPU:0, one launch (start us, length us, event | category | flops | bytes accessed | tf_op | source)
XLA Modules:
  0.0 239.4 jit_solution(9898089449140861697)
XLA Ops:
  4.1 7.3 %all-to-all-start = ((f32[32,4,2,8,256]{4,3,2,1,0:T(8,128)}), f32[32,4,2,8,256]{4,3,2,1,0:T(8,128)S(1)}, u32[]{:S(2)}, u32[]{:S(2)}) async-start(f32[32,4,2,8,256]{4,3,2,1,0:T(8,128)} %transposed_pieces.1.up_ref.low_ref.refs_3_), calls=%async_computation | async-start | bytes 4194304 | tf_op jit(solution)/shard_map/all_to_all | solution.py:338
  12.6 47.7 %all-to-all-done = f32[32,4,2,8,256]{4,3,2,1,0:T(8,128)S(1)} async-done(((f32[32,4,2,8,256]{4,3,2,1,0:T(8,128)}), f32[32,4,2,8,256]{4,3,2,1,0:T(8,128)S(1)}, u32[]{:S(2)}, u32[]{:S(2)}) %all-to-all-start) | async-done | bytes 2097184 | tf_op jit(solution)/shard_map/all_to_all | solution.py:338
  64.6 11.7 %collective-permute-done.refs_0_ = f32[1,64,8,256]{3,2,1,0:T(8,128)} collective-permute-done((f32[1,64,8,256]{3,2,1,0:T(8,128)S(1)}, f32[1,64,8,256]{3,2,1,0:T(8,128)}, u32[]{:S(2)}, u32[]{:S(2)}) %collective-permute-start) | collective-permute-done | bytes 524320 | tf_op jit(solution)/shard_map/ppermute | solution.py:263
  79.8 11.2 %collective-permute-done.4.refs_0_ = f32[1,64,8,256]{3,2,1,0:T(8,128)S(1)} collective-permute-done((f32[1,64,8,256]{3,2,1,0:T(8,128)}, f32[1,64,8,256]{3,2,1,0:T(8,128)S(1)}, u32[]{:S(2)}, u32[]{:S(2)}) %collective-permute-start.4) | collective-permute-done | bytes 524320 | tf_op jit(solution)/shard_map/ppermute | solution.py:263
  95.2 11.3 %collective-permute-done.10.refs_1_ = f32[1,64,8,256]{3,2,1,0:T(8,128)S(1)} collective-permute-done((f32[1,64,8,256]{3,2,1,0:T(8,128)S(1)}, f32[1,64,8,256]{3,2,1,0:T(8,128)S(1)}, u32[]{:S(2)}, u32[]{:S(2)}) %collective-permute-start.10) | collective-permute-done | bytes 524320 | tf_op jit(solution)/shard_map/ppermute | solution.py:263
  108.0 2.4 %collective-permute-done.9.refs_0_ = f32[1,64,8,256]{3,2,1,0:T(8,128)S(1)} collective-permute-done((f32[1,64,8,256]{3,2,1,0:T(8,128)S(1)}, f32[1,64,8,256]{3,2,1,0:T(8,128)S(1)}, u32[]{:S(2)}, u32[]{:S(2)}) %collective-permute-start.9) | collective-permute-done | bytes 524320 | tf_op jit(solution)/shard_map/ppermute | solution.py:263
  110.4 5.2 %collective-permute-done.19.refs_4_ = f32[1,32,8,256]{3,2,1,0:T(8,128)S(1)} collective-permute-done((f32[1,32,8,256]{3,2,1,0:T(8,128)S(1)}, f32[1,32,8,256]{3,2,1,0:T(8,128)S(1)}, u32[]{:S(2)}, u32[]{:S(2)}) %collective-permute-start.19) | collective-permute-done | bytes 262176 | tf_op jit(solution)/shard_map/ppermute | solution.py:263
  118.4 2.6 %collective-permute-done.18.refs_3_ = f32[1,64,8,256]{3,2,1,0:T(8,128)S(1)} collective-permute-done((f32[1,64,8,256]{3,2,1,0:T(8,128)S(1)}, f32[1,64,8,256]{3,2,1,0:T(8,128)S(1)}, u32[]{:S(2)}, u32[]{:S(2)}) %collective-permute-start.18) | collective-permute-done | bytes 524320 | tf_op jit(solution)/shard_map/ppermute | solution.py:263
  121.6 6.4 %collective-permute-done.15.refs_0_ = f32[1,64,8,256]{3,2,1,0:T(8,128)S(1)} collective-permute-done((f32[1,64,8,256]{3,2,1,0:T(8,128)S(1)}, f32[1,64,8,256]{3,2,1,0:T(8,128)S(1)}, u32[]{:S(2)}, u32[]{:S(2)}) %collective-permute-start.15) | collective-permute-done | bytes 524320 | tf_op jit(solution)/shard_map/ppermute | solution.py:263
  131.0 2.3 collective-permute-start.27
  135.4 8.4 %collective-permute-done.27.refs_3_ = f32[1,32,8,256]{3,2,1,0:T(8,128)S(1)} collective-permute-done((f32[1,32,8,256]{3,2,1,0:T(8,128)S(1)}, f32[1,32,8,256]{3,2,1,0:T(8,128)S(1)}, u32[]{:S(2)}, u32[]{:S(2)}) %collective-permute-start.27) | collective-permute-done | bytes 262176 | tf_op jit(solution)/shard_map/ppermute | solution.py:263
  149.7 1.9 collective-permute-start.32
  151.9 12.5 %product.4.refs_5_ = f32[1,256,512]{2,1,0:T(8,128)S(1)} custom-call(s32[32]{0:T(128)S(1)} %get-tuple-element.94.refs_0_, f32[16384,512]{1,0:T(8,128)} %refs_4_.5, f32[16384,512]{1,0:T(8,128)} %refs_4_.5, f32[16384,512]{1,0:T(8,128)} %refs_4_.5, f32[16384,512]{1,0:T(8,128)} %refs_4_.5, f32[1,64,8,256]{3,2,1,0:T(8,128)S(1)} %sync.8.refs_5_, ...), custom_call_target="tpu_custom_call" | custom-call | flops 6442450944 | bytes 25165824 | tf_op jit(solution)/shard_map/product/pallas_call | solution.py:119
  164.5 12.5 %product.3.refs_4_ = f32[1,256,512]{2,1,0:T(8,128)S(1)} custom-call(s32[32]{0:T(128)S(1)} %get-tuple-element.93.refs_0_, f32[16384,512]{1,0:T(8,128)} %refs_4_.5, f32[16384,512]{1,0:T(8,128)} %refs_4_.5, f32[16384,512]{1,0:T(8,128)} %refs_4_.5, f32[16384,512]{1,0:T(8,128)} %refs_4_.5, f32[1,64,8,256]{3,2,1,0:T(8,128)S(1)} %sync.8.refs_5_, ...), custom_call_target="tpu_custom_call" | custom-call | flops 6442450944 | bytes 25165824 | tf_op jit(solution)/shard_map/product/pallas_call | solution.py:119
  180.9 3.4 %upper.2 = (f32[512,1024]{1,0:T(8,128)}, f32[512,256]{1,0:T(8,128)S(1)}, f32[256,256]{1,0:T(8,128)S(1)}, f32[256,256]{1,0:T(8,128)S(1)}, f32[256,256]{1,0:T(8,128)S(1)}) custom-call(s32[5]{0:T(128)S(1)} %get-tuple-element.97.refs_1_.flag_ref, s32[32]{0:T(128)S(1)} %stack.131.refs_4_.pos_ref.refs_1_, f32[1,256,512]{2,1,0:T(8,128)S(1)} %get-tuple-element.67.zt_ref, ...), custom_call_target="tpu_custom_call" | custom-call | flops 1207959552 | bytes 5242880 | tf_op jit(solution)/shard_map/upper/pallas_call | solution.py:185
  185.0 3.6 %upper.3 = (f32[512,1024]{1,0:T(8,128)}, f32[512,256]{1,0:T(8,128)S(1)}, f32[256,256]{1,0:T(8,128)S(1)}, f32[256,256]{1,0:T(8,128)S(1)}, f32[256,256]{1,0:T(8,128)S(1)}) custom-call(s32[5]{0:T(128)S(1)} %get-tuple-element.98.refs_2_.flag_ref, s32[32]{0:T(128)S(1)} %stack.131.refs_4_.pos_ref.refs_1_, ...), custom_call_target="tpu_custom_call", output_to_operand_aliasing={{0}: (8, {})} | custom-call | flops 1207959552 | bytes 5242880 | tf_op jit(solution)/shard_map/upper/pallas_call | solution.py:185
  188.7 3.4 %collective-permute-done.44.refs_0_ = f32[2,32,8,256]{3,2,1,0:T(8,128)} collective-permute-done((f32[2,32,8,256]{3,2,1,0:T(8,128)S(1)}, f32[2,32,8,256]{3,2,1,0:T(8,128)}, u32[]{:S(2)}, u32[]{:S(2)}) %collective-permute-start.44) | collective-permute-done | bytes 524320 | tf_op jit(solution)/shard_map/ppermute | solution.py:263
  197.5 14.6 %product.5.refs_2_ = f32[2,256,512]{2,1,0:T(8,128)} custom-call(s32[32]{0:T(128)} %copy-done.26, f32[16384,512]{1,0:T(8,128)} %refs_4_.5, f32[16384,512]{1,0:T(8,128)} %refs_4_.5, f32[16384,512]{1,0:T(8,128)} %refs_4_.5, f32[16384,512]{1,0:T(8,128)} %refs_4_.5, f32[2,32,8,256]{3,2,1,0:T(8,128)} %copy-done.1, f32[2,32,8,256]{3,2,1,0:T(8,128)} %copy-done.9, ...), custom_call_target="tpu_custom_call" | custom-call | flops 6442450944 | bytes 25165824 | tf_op jit(solution)/shard_map/product/pallas_call | solution.py:119
  213.4 2.7 %lower.1 = (f32[512,1024]{1,0:T(8,128)}, f32[512,256]{1,0:T(8,128)S(1)}) custom-call(s32[4]{0:T(128)S(1)} %pad_add_fusion.refs_3_.refs_0_, s32[32]{0:T(128)S(1)} %stack.131.refs_4_.pos_ref.refs_1_, f32[2,256,512]{2,1,0:T(8,128)S(1)} %copy-done.8, f32[32,4,2,8,256]{4,3,2,1,0:T(8,128)} %transposed_pieces.1.up_ref.low_ref.refs_3_, ...), custom_call_target="tpu_custom_call", output_to_operand_aliasing={{0}: (8, {})} | custom-call | flops 402653184 | bytes 7864320 | tf_op jit(solution)/shard_map/lower/pallas_call | solution.py:221
  216.5 2.1 collective-permute-done.48
  222.3 4.3 %collective-permute-done.49 = f32[4,48,256]{2,1,0:T(8,128)S(1)} collective-permute-done((f32[4,48,256]{2,1,0:T(8,128)S(1)}, f32[4,48,256]{2,1,0:T(8,128)S(1)}, u32[]{:S(2)}, u32[]{:S(2)}) %collective-permute-start.49) | collective-permute-done | bytes 196640 | tf_op jit(solution)/shard_map/ppermute | solution.py:263
  226.6 3.3 %collective-permute-done.50 = f32[4,48,256]{2,1,0:T(8,128)S(1)} collective-permute-done((f32[4,48,256]{2,1,0:T(8,128)S(1)}, f32[4,48,256]{2,1,0:T(8,128)S(1)}, u32[]{:S(2)}, u32[]{:S(2)}) %collective-permute-start.50) | collective-permute-done | bytes 196640 | tf_op jit(solution)/shard_map/ppermute | solution.py:263
  231.7 2.2 collective-permute-start.53
  235.1 2.2 collective-permute-done.52
  (199 shorter events, 52.6 us)
Async XLA Ops:
  4.1 56.2 %all-to-all-start = ((f32[32,4,2,8,256]{4,3,2,1,0:T(8,128)}), f32[32,4,2,8,256]{4,3,2,1,0:T(8,128)S(1)}, u32[]{:S(2)}, u32[]{:S(2)}) async-start(f32[32,4,2,8,256]{4,3,2,1,0:T(8,128)} %transposed_pieces.1.up_ref.low_ref.refs_3_), calls=%async_computation | async-start | bytes 4194304 | tf_op jit(solution)/shard_map/all_to_all | solution.py:338
  60.9 15.4 %collective-permute-start = (f32[1,64,8,256]{3,2,1,0:T(8,128)S(1)}, f32[1,64,8,256]{3,2,1,0:T(8,128)}, u32[]{:S(2)}, u32[]{:S(2)}) collective-permute-start(f32[1,64,8,256]{3,2,1,0:T(8,128)S(1)} %sync.8.refs_5_), channel_id=1, source_target_pairs={{0,8},{1,9},{2,10},{3,11},{4,12},{5,13},{6,14},{7,15},{8,16},{9,17... | collective-permute-start | bytes 1572872 | tf_op jit(solution)/shard_map/ppermute | solution.py:263
  61.0 15.4 %collective-permute-start.1 = (f32[1,64,8,256]{3,2,1,0:T(8,128)S(1)}, f32[1,64,8,256]{3,2,1,0:T(8,128)}, u32[]{:S(2)}, u32[]{:S(2)}) collective-permute-start(f32[1,64,8,256]{3,2,1,0:T(8,128)S(1)} %sync.8.refs_5_), channel_id=1, source_target_pairs={{0,2},{1,3},{2,0},{3,1},{4,6},{5,7},{6,4},{7,5},{8,10},{9,11},{10,... | collective-permute-start | bytes 1572872 | tf_op jit(solution)/shard_map/ppermute | solution.py:263
  62.5 13.9 %collective-permute-start.2 = (f32[1,64,8,256]{3,2,1,0:T(8,128)S(1)}, f32[1,64,8,256]{3,2,1,0:T(8,128)}, u32[]{:S(2)}, u32[]{:S(2)}) collective-permute-start(f32[1,64,8,256]{3,2,1,0:T(8,128)S(1)} %sync.8.refs_5_), channel_id=1, source_target_pairs={{0,4},{1,5},{2,6},{3,7},{4,0},{5,1},{6,2},{7,3},{8,12},{9,13},{10,... | collective-permute-start | bytes 1572872 | tf_op jit(solution)/shard_map/ppermute | solution.py:263
  76.4 14.6 %collective-permute-start.4 = (f32[1,64,8,256]{3,2,1,0:T(8,128)}, f32[1,64,8,256]{3,2,1,0:T(8,128)S(1)}, u32[]{:S(2)}, u32[]{:S(2)}) collective-permute-start(f32[1,64,8,256]{3,2,1,0:T(8,128)} %get-tuple-element.43.refs_6_), channel_id=1, source_target_pairs={{0,8},{1,9},{2,10},{3,11},{4,12},{5,13},{6,14},{7,15},{8,16},{9,17... | collective-permute-start | bytes 1572872 | tf_op jit(solution)/shard_map/ppermute | solution.py:263
  76.5 14.6 %collective-permute-start.5 = (f32[1,64,8,256]{3,2,1,0:T(8,128)}, f32[1,64,8,256]{3,2,1,0:T(8,128)S(1)}, u32[]{:S(2)}, u32[]{:S(2)}) collective-permute-start(f32[1,64,8,256]{3,2,1,0:T(8,128)} %get-tuple-element.43.refs_6_), channel_id=1, source_target_pairs={{0,2},{1,3},{2,0},{3,1},{4,6},{5,7},{6,4},{7,5},{8,10},{9,11},{10,... | collective-permute-start | bytes 1572872 | tf_op jit(solution)/shard_map/ppermute | solution.py:263
  78.2 13.4 %collective-permute-start.6 = (f32[1,64,8,256]{3,2,1,0:T(8,128)}, f32[1,64,8,256]{3,2,1,0:T(8,128)S(1)}, u32[]{:S(2)}, u32[]{:S(2)}) collective-permute-start(f32[1,64,8,256]{3,2,1,0:T(8,128)} %get-tuple-element.43.refs_6_), channel_id=1, source_target_pairs={{0,4},{1,5},{2,6},{3,7},{4,0},{5,1},{6,2},{7,3},{8,12},{9,13},{10,... | collective-permute-start | bytes 1572872 | tf_op jit(solution)/shard_map/ppermute | solution.py:263
  91.6 14.9 %collective-permute-start.10 = (f32[1,64,8,256]{3,2,1,0:T(8,128)S(1)}, f32[1,64,8,256]{3,2,1,0:T(8,128)S(1)}, u32[]{:S(2)}, u32[]{:S(2)}) collective-permute-start(f32[1,64,8,256]{3,2,1,0:T(8,128)S(1)} %get-tuple-element.45.refs_7_), channel_id=1, source_target_pairs={{0,2},{1,3},{2,0},{3,1},{4,6},{5,7},{6,4},{7,5},{8,10},{9,11},{10,... | collective-permute-start | bytes 1572872 | tf_op jit(solution)/shard_map/ppermute | solution.py:263
  92.5 14.4 %collective-permute-start.11 = (f32[1,64,8,256]{3,2,1,0:T(8,128)S(1)}, f32[1,64,8,256]{3,2,1,0:T(8,128)S(1)}, u32[]{:S(2)}, u32[]{:S(2)}) collective-permute-start(f32[1,64,8,256]{3,2,1,0:T(8,128)S(1)} %get-tuple-element.45.refs_7_), channel_id=1, source_target_pairs={{0,4},{1,5},{2,6},{3,7},{4,0},{5,1},{6,2},{7,3},{8,12},{9,13},{10,... | collective-permute-start | bytes 1572872 | tf_op jit(solution)/shard_map/ppermute | solution.py:263
  93.9 14.1 %collective-permute-start.12 = (f32[1,64,8,256]{3,2,1,0:T(8,128)S(1)}, f32[1,64,8,256]{3,2,1,0:T(8,128)S(1)}, u32[]{:S(2)}, u32[]{:S(2)}) collective-permute-start(f32[1,64,8,256]{3,2,1,0:T(8,128)S(1)} %get-tuple-element.45.refs_7_), channel_id=1, source_target_pairs={{0,1},{1,0},{2,3},{3,2},{4,5},{5,4},{6,7},{7,6},{8,9},{9,8},{10,11... | collective-permute-start | bytes 1572872 | tf_op jit(solution)/shard_map/ppermute | solution.py:263
  93.9 16.5 %collective-permute-start.9 = (f32[1,64,8,256]{3,2,1,0:T(8,128)S(1)}, f32[1,64,8,256]{3,2,1,0:T(8,128)S(1)}, u32[]{:S(2)}, u32[]{:S(2)}) collective-permute-start(f32[1,64,8,256]{3,2,1,0:T(8,128)S(1)} %get-tuple-element.45.refs_7_), channel_id=1, source_target_pairs={{0,8},{1,9},{2,10},{3,11},{4,12},{5,13},{6,14},{7,15},{8,16},{9,17... | collective-permute-start | bytes 1572872 | tf_op jit(solution)/shard_map/ppermute | solution.py:263
  94.5 22.3 %collective-permute-start.17 = (f32[1,64,8,256]{3,2,1,0:T(8,128)}, f32[1,64,8,256]{3,2,1,0:T(8,128)S(1)}, u32[]{:S(2)}, u32[]{:S(2)}) collective-permute-start(f32[1,64,8,256]{3,2,1,0:T(8,128)} %get-tuple-element.46.refs_13_), channel_id=1, source_target_pairs={{0,2},{1,3},{2,0},{3,1},{4,6},{5,7},{6,4},{7,5},{8,10},{9,11},{10,... | collective-permute-start | bytes 1572872 | tf_op jit(solution)/shard_map/ppermute | solution.py:263
  106.9 14.1 %collective-permute-start.18 = (f32[1,64,8,256]{3,2,1,0:T(8,128)S(1)}, f32[1,64,8,256]{3,2,1,0:T(8,128)S(1)}, u32[]{:S(2)}, u32[]{:S(2)}) collective-permute-start(f32[1,64,8,256]{3,2,1,0:T(8,128)S(1)} %get-tuple-element.49.refs_10_), channel_id=1, source_target_pairs={{0,4},{1,5},{2,6},{3,7},{4,0},{5,1},{6,2},{7,3},{8,12},{9,13},{10,... | collective-permute-start | bytes 1572872 | tf_op jit(solution)/shard_map/ppermute | solution.py:263
  108.0 13.0 %collective-permute-start.21 = (f32[1,64,8,256]{3,2,1,0:T(8,128)S(1)}, f32[1,64,8,256]{3,2,1,0:T(8,128)S(1)}, u32[]{:S(2)}, u32[]{:S(2)}) collective-permute-start(f32[1,64,8,256]{3,2,1,0:T(8,128)S(1)} %get-tuple-element.49.refs_10_), channel_id=1, source_target_pairs={{0,1},{1,0},{2,3},{3,2},{4,5},{5,4},{6,7},{7,6},{8,9},{9,8},{10,11... | collective-permute-start | bytes 1572872 | tf_op jit(solution)/shard_map/ppermute | solution.py:263
  116.8 14.3 %collective-permute-start.16 = (f32[1,64,8,256]{3,2,1,0:T(8,128)S(1)}, f32[1,64,8,256]{3,2,1,0:T(8,128)S(1)}, u32[]{:S(2)}, u32[]{:S(2)}) collective-permute-start(f32[1,64,8,256]{3,2,1,0:T(8,128)S(1)} %get-tuple-element.48.refs_8_), channel_id=1, source_target_pairs={{0,4},{1,5},{2,6},{3,7},{4,0},{5,1},{6,2},{7,3},{8,12},{9,13},{10,... | collective-permute-start | bytes 1572872 | tf_op jit(solution)/shard_map/ppermute | solution.py:263
  127.9 15.9 %collective-permute-start.14 = (f32[1,64,8,256]{3,2,1,0:T(8,128)S(1)}, f32[1,64,8,256]{3,2,1,0:T(8,128)S(1)}, u32[]{:S(2)}, u32[]{:S(2)}) collective-permute-start(f32[1,64,8,256]{3,2,1,0:T(8,128)S(1)} %get-tuple-element.47.refs_15_), channel_id=1, source_target_pairs={{0,2},{1,3},{2,0},{3,1},{4,6},{5,7},{6,4},{7,5},{8,10},{9,11},{10,... | collective-permute-start | bytes 1572872 | tf_op jit(solution)/shard_map/ppermute | solution.py:263
  131.0 12.8 %collective-permute-start.27 = (f32[1,32,8,256]{3,2,1,0:T(8,128)S(1)}, f32[1,32,8,256]{3,2,1,0:T(8,128)S(1)}, u32[]{:S(2)}, u32[]{:S(2)}) collective-permute-start(f32[1,32,8,256]{3,2,1,0:T(8,128)S(1)} %get-tuple-element.50), channel_id=1, source_target_pairs={{0,24},{1,25},{2,26},{3,27},{4,28},{5,29},{6,30},{7,31},{8,0},{9,1... | collective-permute-start | bytes 786440 | tf_op jit(solution)/shard_map/ppermute | solution.py:263
  147.8 16.6 %collective-permute-start.33 = (f32[2,32,8,256]{3,2,1,0:T(8,128)S(1)}, f32[2,32,8,256]{3,2,1,0:T(8,128)S(1)}, u32[]{:S(2)}, u32[]{:S(2)}) collective-permute-start(f32[2,32,8,256]{3,2,1,0:T(8,128)S(1)} %constant_dynamic-update-slice_fusion.refs_5_.refs_6_), channel_id=1, source_target_pairs={{0,2},{1,3},{2,0},{3,1},{4,6},{5,7},{6,4},{7,5},{8,10},{9,11},{10,... | collective-permute-start | bytes 1572872 | tf_op jit(solution)/shard_map/ppermute | solution.py:263
  147.9 29.1 %collective-permute-start.35 = (f32[2,32,8,256]{3,2,1,0:T(8,128)S(1)}, f32[2,32,8,256]{3,2,1,0:T(8,128)S(1)}, u32[]{:S(2)}, u32[]{:S(2)}) collective-permute-start(f32[2,32,8,256]{3,2,1,0:T(8,128)S(1)} %constant_dynamic-update-slice_fusion.refs_5_.refs_6_), channel_id=1, source_target_pairs={{0,4},{1,5},{2,6},{3,7},{4,0},{5,1},{6,2},{7,3},{8,12},{9,13},{10,... | collective-permute-start | bytes 1572872 | tf_op jit(solution)/shard_map/ppermute | solution.py:263
  149.7 27.4 %collective-permute-start.39 = (f32[2,32,8,256]{3,2,1,0:T(8,128)S(1)}, f32[2,32,8,256]{3,2,1,0:T(8,128)S(1)}, u32[]{:S(2)}, u32[]{:S(2)}) collective-permute-start(f32[2,32,8,256]{3,2,1,0:T(8,128)S(1)} %constant_dynamic-update-slice_fusion.refs_5_.refs_6_), channel_id=1, source_target_pairs={{0,1},{1,0},{2,3},{3,2},{4,5},{5,4},{6,7},{7,6},{8,9},{9,8},{10,11... | collective-permute-start | bytes 1572872 | tf_op jit(solution)/shard_map/ppermute | solution.py:263
  149.7 27.4 %collective-permute-start.32 = (f32[2,32,8,256]{3,2,1,0:T(8,128)S(1)}, f32[2,32,8,256]{3,2,1,0:T(8,128)S(1)}, u32[]{:S(2)}, u32[]{:S(2)}) collective-permute-start(f32[2,32,8,256]{3,2,1,0:T(8,128)S(1)} %get-tuple-element.58.refs_4_.refs_5_), channel_id=1, source_target_pairs={{0,2},{1,3},{2,0},{3,1},{4,6},{5,7},{6,4},{7,5},{8,10},{9,11},{10,... | collective-permute-start | bytes 1572872 | tf_op jit(solution)/shard_map/ppermute | solution.py:263
  151.6 25.4 %collective-permute-start.34 = (f32[2,32,8,256]{3,2,1,0:T(8,128)S(1)}, f32[2,32,8,256]{3,2,1,0:T(8,128)S(1)}, u32[]{:S(2)}, u32[]{:S(2)}) collective-permute-start(f32[2,32,8,256]{3,2,1,0:T(8,128)S(1)} %get-tuple-element.58.refs_4_.refs_5_), channel_id=1, source_target_pairs={{0,4},{1,5},{2,6},{3,7},{4,0},{5,1},{6,2},{7,3},{8,12},{9,13},{10,... | collective-permute-start | bytes 1572872 | tf_op jit(solution)/shard_map/ppermute | solution.py:263
  177.7 14.4 %collective-permute-start.44 = (f32[2,32,8,256]{3,2,1,0:T(8,128)S(1)}, f32[2,32,8,256]{3,2,1,0:T(8,128)}, u32[]{:S(2)}, u32[]{:S(2)}) collective-permute-start(f32[2,32,8,256]{3,2,1,0:T(8,128)S(1)} %get-tuple-element.65.refs_8_.refs_9_), channel_id=1, source_target_pairs={{0,2},{1,3},{2,0},{3,1},{4,6},{5,7},{6,4},{7,5},{8,10},{9,11},{10,... | collective-permute-start | bytes 1572872 | tf_op jit(solution)/shard_map/ppermute | solution.py:263
  179.2 14.3 %collective-permute-start.45 = (f32[2,32,8,256]{3,2,1,0:T(8,128)S(1)}, f32[2,32,8,256]{3,2,1,0:T(8,128)}, u32[]{:S(2)}, u32[]{:S(2)}) collective-permute-start(f32[2,32,8,256]{3,2,1,0:T(8,128)S(1)} %get-tuple-element.64.refs_7_.refs_8_), channel_id=1, source_target_pairs={{0,4},{1,5},{2,6},{3,7},{4,0},{5,1},{6,2},{7,3},{8,12},{9,13},{10,... | collective-permute-start | bytes 1572872 | tf_op jit(solution)/shard_map/ppermute | solution.py:263
  (63 other events, 647.2 us)
